TPU v7x, 256 devices: a whole 4x4x8 slice. The times are simulated.
256 devices in a mesh: seq: 16 (over x_hi, z), dp: 4 (over x_lo, core), tensor: 4 (over y).
Axes of the slice: x: 4 (x_hi: 2, x_lo: 2; x = x_hi * 2 + x_lo), y: 4, z: 8, core: 2. Of those that a mesh axis runs over, the one named last changes fastest.
Arguments:
- layer_input: bfloat16 [4, 8192, 512], P('dp', 'seq'), may hold values from -6 to 6
- grad_output: bfloat16 [4, 8192, 512], P('dp', 'seq'), may hold values from -6 to 6
- weight_in: bfloat16 [512, 2048], P(None, 'tensor'), may hold values from -0.25 to 0.25
- weight_out: bfloat16 [512, 512], P('tensor'), may hold values from -0.25 to 0.25
- time_table: float32 [4, 128], P('tensor'), may hold values from -1 to 1
- user_lengths: int32 [4, 3], P('dp'), may hold values from 1 to 32, 64 in all within a row
- time_buckets: int32 [4, 8192], P('dp', 'seq'), may hold values from 0 to 127
Outputs:
- grad_input: bfloat16 [4, 8192, 512], P('dp', 'seq', 'tensor')
- grad_weight_in: float32 [512, 2048], P(None, 'tensor')
- grad_weight_out: float32 [512, 512], P('tensor')
Inputs may be any that keep to these rules, and one draw needn't show every extreme that they name: user_lengths[w, 0] and user_lengths[w, 1] are the two users' lengths in blocks of 128 rows, user_lengths[w, 2] the padding at the window's end; each row sums to 64.
All inputs are finite; a program needn't handle non-finite values.
Results may differ from a plain program's by a relative error of at most 0.015.
Values may be sent and summed in bfloat16 or wider, within the bound.
No kernel may reach another device: no remote copies, remote signals or barrier semaphores. Data moves between devices by JAX's collectives and lax.ppermute only.
A program may use at most 64 MiB of HBM per device.

v0:
```python
import math

import jax
import jax.numpy as jnp
from jax import lax
from jax.sharding import PartitionSpec as P

PAD_ROWS = 128


EPSILON = 0.05


def silu_slope(values):
    sigmoid = jax.nn.sigmoid(values)
    return sigmoid * (1.0 + values * (1.0 - sigmoid))


def time_position(rows, per_device, devices):
    half = per_device // 2
    device = rows // per_device
    offset = rows % per_device
    early = device * half + offset
    late = (2 * devices - 1 - device) * half + offset - half
    return jnp.where(offset < half, early, late)


def row_meta(rows, bounds):
    first_end, second_end = bounds
    user_ids = (rows >= first_end).astype(jnp.int32) + (rows >= second_end).astype(jnp.int32)
    zero_int = jnp.zeros_like(rows)
    user_first = jnp.where(
        rows < first_end,
        zero_int,
        jnp.where(rows < second_end, zero_int + first_end, zero_int + second_end),
    )
    return (user_ids, user_first)


def bucket_hot(times, buckets):
    return (times[:, None] == jnp.arange(buckets, dtype=jnp.int32)[None, :]).astype(jnp.float32)


def square_table(table_row):
    buckets = table_row.shape[0]
    index = jnp.arange(buckets, dtype=jnp.int32)
    gaps = jnp.abs(index[:, None] - index[None, :])
    picks = (gaps[:, :, None] == index[None, None, :]).astype(jnp.float32)
    return jnp.sum(picks * table_row[None, None, :], axis=-1)


def pair_tile(query_blk, key_blk, query_lifted, key_times, query_rows, key_rows, bounds, factor):
    query_users, query_first = row_meta(query_rows, bounds)
    key_users, unused_first = row_meta(key_rows, bounds)
    scores = (
        jnp.einsum("qd,kd->qk", query_blk, key_blk, preferred_element_type=jnp.float32) * factor
    )
    key_hot = bucket_hot(key_times, query_lifted.shape[1])
    scores = scores + lax.dot_general(
        query_lifted,
        key_hot,
        (((1,), (1,)), ((), ())),
        precision=lax.Precision.HIGHEST,
        preferred_element_type=jnp.float32,
    )
    allowed = (
        (key_rows[None, :] <= query_rows[:, None])
        & (key_users[None, :] == query_users[:, None])
        & (query_rows < bounds[1])[:, None]
    )
    counts = jnp.maximum(query_rows - query_first + 1, 1).astype(jnp.float32)
    return (scores, allowed, counts)


def tile_grads(
    query_blk,
    key_blk,
    query_lifted,
    key_times,
    query_rows,
    key_rows,
    value_blk,
    grad_blk,
    bounds,
    factor,
):
    scores, allowed, counts = pair_tile(
        query_blk, key_blk, query_lifted, key_times, query_rows, key_rows, bounds, factor
    )
    attend = (jnp.where(allowed, jax.nn.silu(scores), 0.0) / counts[:, None]).astype(jnp.bfloat16)
    raw = jnp.einsum("qd,kd->qk", grad_blk, value_blk, preferred_element_type=jnp.float32)
    slope = (jnp.where(allowed, raw * silu_slope(scores), 0.0) / counts[:, None]).astype(
        jnp.bfloat16
    )
    return (attend, slope)


def over_blocks(total_rows, block_fn, carry):
    block = math.gcd(total_rows, 512)
    return lax.fori_loop(
        0,
        total_rows // block,
        lambda position, running: block_fn(position * block, block, running),
        carry,
    )


def body(layer_input, grad_output, weight_in, weight_out, time_table, user_lengths, time_buckets):
    inputs_local = layer_input[0]
    upstream = grad_output[0]
    table_row = time_table[0]
    my_times = time_buckets[0]
    buckets = table_row.shape[0]
    bias_square = square_table(table_row)
    rows_local = inputs_local.shape[0]
    cycle_size = lax.axis_size("seq")
    head_width = weight_out.shape[0]
    factor = 1.0 / math.sqrt(head_width)
    first_end = PAD_ROWS * user_lengths[0, 0]
    bounds = (first_end, first_end + PAD_ROWS * user_lengths[0, 1])
    row_base = lax.axis_index("seq") * rows_local
    my_rows = time_position(
        row_base + jnp.arange(rows_local, dtype=jnp.int32), rows_local, cycle_size
    )
    my_lifted = jnp.dot(
        bucket_hot(my_times, buckets),
        bias_square,
        precision=lax.Precision.HIGHEST,
        preferred_element_type=jnp.float32,
    )
    projected = jnp.dot(inputs_local, weight_in, preferred_element_type=jnp.float32)
    activated = jax.nn.silu(projected).astype(jnp.bfloat16)
    gate_part = activated[:, :head_width]
    value_part = activated[:, head_width : 2 * head_width]
    query_part = activated[:, 2 * head_width : 3 * head_width]
    key_part = activated[:, 3 * head_width :]
    zeros_local = jnp.zeros((rows_local, head_width), jnp.float32)

    def stored_positions(begin, block):
        return time_position(begin + jnp.arange(block, dtype=jnp.int32), rows_local, cycle_size)

    key_piece = lax.all_gather(key_part, "seq", axis=0, tiled=True)
    value_piece = lax.all_gather(value_part, "seq", axis=0, tiled=True)
    time_piece = lax.all_gather(my_times, "seq", axis=0, tiled=True)

    def forward_one_block(offset, block, running):
        key_rows = stored_positions(offset, block)
        key_blk = lax.dynamic_slice_in_dim(key_piece, offset, block, 0)
        value_blk = lax.dynamic_slice_in_dim(value_piece, offset, block, 0)
        time_blk = lax.dynamic_slice_in_dim(time_piece, offset, block, 0)
        scores, allowed, counts = pair_tile(
            query_part, key_blk, my_lifted, time_blk, my_rows, key_rows, bounds, factor
        )
        attend = (jnp.where(allowed, jax.nn.silu(scores), 0.0) / counts[:, None]).astype(
            jnp.bfloat16
        )
        return running + jnp.dot(attend, value_blk, preferred_element_type=jnp.float32)

    attended = over_blocks(key_piece.shape[0], forward_one_block, zeros_local)
    spread = jnp.sqrt(jnp.mean(attended * attended, axis=-1, keepdims=True) + EPSILON)
    normed = attended / spread
    gate_float = gate_part.astype(jnp.float32)
    gated = (normed * gate_float).astype(jnp.bfloat16)
    grad_gated = lax.dot_general(
        upstream, weight_out, (((1,), (1,)), ((), ())), preferred_element_type=jnp.float32
    )
    grad_gate = grad_gated * normed
    grad_normed = grad_gated * gate_float
    grad_attended = (
        (grad_normed - normed * jnp.mean(grad_normed * normed, axis=-1, keepdims=True)) / spread
    ).astype(jnp.bfloat16)
    total_rows = cycle_size * rows_local
    query_key_piece = lax.all_gather(key_part, "seq", axis=0, tiled=True)
    query_value_piece = lax.all_gather(value_part, "seq", axis=0, tiled=True)
    query_time_piece = lax.all_gather(my_times, "seq", axis=0, tiled=True)

    def query_one_block(offset, block, running):
        key_rows = stored_positions(offset, block)
        key_blk = lax.dynamic_slice_in_dim(query_key_piece, offset, block, 0)
        value_blk = lax.dynamic_slice_in_dim(query_value_piece, offset, block, 0)
        time_blk = lax.dynamic_slice_in_dim(query_time_piece, offset, block, 0)
        unused_attend, slope = tile_grads(
            query_part,
            key_blk,
            my_lifted,
            time_blk,
            my_rows,
            key_rows,
            value_blk,
            grad_attended,
            bounds,
            factor,
        )
        return running + jnp.dot(slope, key_blk, preferred_element_type=jnp.float32)

    grad_query = over_blocks(query_key_piece.shape[0], query_one_block, zeros_local)
    query_piece = lax.all_gather(query_part, "seq", axis=0, tiled=True)
    grad_piece = lax.all_gather(grad_attended, "seq", axis=0, tiled=True)
    key_time_piece = lax.all_gather(my_times, "seq", axis=0, tiled=True)

    def key_one_block(offset, block, running):
        query_rows = stored_positions(offset, block)
        query_blk = lax.dynamic_slice_in_dim(query_piece, offset, block, 0)
        grad_blk = lax.dynamic_slice_in_dim(grad_piece, offset, block, 0)
        time_blk = lax.dynamic_slice_in_dim(key_time_piece, offset, block, 0)
        grad_key_now, grad_value_now = running
        query_lifted = jnp.dot(
            bucket_hot(time_blk, buckets),
            bias_square,
            precision=lax.Precision.HIGHEST,
            preferred_element_type=jnp.float32,
        )
        attend, slope = tile_grads(
            query_blk,
            key_part,
            query_lifted,
            my_times,
            query_rows,
            my_rows,
            value_part,
            grad_blk,
            bounds,
            factor,
        )
        grad_key_now = grad_key_now + jnp.einsum(
            "qk,qd->kd", slope, query_blk, preferred_element_type=jnp.float32
        )
        grad_value_now = grad_value_now + jnp.einsum(
            "qk,qd->kd", attend, grad_blk, preferred_element_type=jnp.float32
        )
        return (grad_key_now, grad_value_now)

    grad_key, grad_value = over_blocks(
        query_piece.shape[0], key_one_block, (zeros_local, zeros_local)
    )
    grad_query = grad_query * factor
    grad_key = grad_key * factor
    grad_activated = jnp.concatenate([grad_gate, grad_value, grad_query, grad_key], 1)
    grad_projected = (grad_activated * silu_slope(projected)).astype(jnp.bfloat16)
    input_terms = lax.dot_general(
        grad_projected, weight_in, (((1,), (1,)), ((), ())), preferred_element_type=jnp.float32
    )
    grad_local = lax.psum_scatter(
        input_terms.astype(jnp.bfloat16), "tensor", scatter_dimension=1, tiled=True
    )
    win_terms = lax.dot_general(
        inputs_local, grad_projected, (((0,), (0,)), ((), ())), preferred_element_type=jnp.float32
    )
    wout_terms = lax.dot_general(
        gated, upstream, (((0,), (0,)), ((), ())), preferred_element_type=jnp.float32
    )
    win_total, wout_total = lax.psum((win_terms, wout_terms), ("seq", "dp"))
    normalizer = 1.0 / math.sqrt(lax.axis_size("dp") * total_rows)
    return (grad_local[None], win_total * normalizer, wout_total * normalizer)


def solution(mesh):
    placed = (
        P("dp", "seq", None),
        P("dp", "seq", None),
        P(None, "tensor"),
        P("tensor", None),
        P("tensor", None),
        P("dp", None),
        P("dp", "seq"),
    )
    return jax.shard_map(
        body,
        mesh=mesh,
        in_specs=placed,
        out_specs=(P("dp", "seq", "tensor"), P(None, "tensor"), P("tensor", None)),
        check_vma=False,
    )
```

profile of v0, /device:TPU:1, one launch (start us, length us, event | category | flops | bytes accessed | tf_op | source)
XLA Modules:
  0.0 690.3 jit_solution(13198691548719057488)
XLA Ops:
  17.9 37.6 %all-gather = s32[1,8192]{1,0:T(1,128)S(1)} all-gather(s32[1,512]{1,0:T(1,128)S(1)} %copy-done.12), channel_id=2, replica_groups=mesh['seq'=16,'dp'=4,'tensor'=4] {'seq'}, dimensions={1}, use_global_device_ids=true | all-gather | bytes 34816 | tf_op jit(solution)/shard_map/all_gather | solution.py:144
  55.5 5.1 select_reduce_fusion
  61.0 36.5 %all-gather.6.cloned.1.call-done = bf16[8192,128]{0,1:T(8,128)(2,1)} async-done(((bf16[512,128]{0,1:T(8,128)(2,1)}), bf16[8192,128]{0,1:T(8,128)(2,1)}) %all-gather.6.cloned.1.call-update) | async-done | bytes 2097168 | tf_op jit(solution)/shard_map/all_gather | solution.py:142
  97.5 4.1 copy.42
  101.5 80.7 %all-gather.8.cloned.1.call-done = bf16[8192,128]{0,1:T(8,128)(2,1)} async-done(((bf16[512,128]{0,1:T(8,128)(2,1)}), bf16[8192,128]{0,1:T(8,128)(2,1)}) %all-gather.8.cloned.1.call-update) | async-done | bytes 2097168 | tf_op jit(solution)/shard_map/all_gather | solution.py:143
  182.2 4.1 copy.44
  186.3 58.0 %while.50 = (s32[]{:T(128)}, f32[512,128]{1,0:T(8,128)}, s32[]{:T(128)}, s32[]{:T(128)}, bf16[8192,128]{1,0:T(8,128)(2,1)}, /*index=5*/bf16[512,128]{1,0:T(8,128...) while((s32[]{:T(128)}, f32[512,128]{1,0:T(8,128)}, ...), condition=%wide.region_2.3_spmd.clone, body=%wide.region_1.2_spmd.clone.sunk | while | flops 540556800 | bytes 3306216 | solution.py:100
  187.1 2.7 convolution_add_fusion.4
  190.6 2.8 convolution_add_fusion.4
  194.2 2.8 convolution_add_fusion.4
  197.9 2.8 convolution_add_fusion.4
  201.5 2.8 convolution_add_fusion.4
  205.1 2.8 convolution_add_fusion.4
  208.8 2.8 convolution_add_fusion.4
  212.4 2.8 convolution_add_fusion.4
  216.0 2.8 convolution_add_fusion.4
  219.7 2.8 convolution_add_fusion.4
  223.3 2.8 convolution_add_fusion.4
  226.9 2.8 convolution_add_fusion.4
  230.6 2.8 convolution_add_fusion.4
  234.2 2.8 convolution_add_fusion.4
  237.8 2.8 convolution_add_fusion.4
  241.5 2.8 convolution_add_fusion.4
  250.6 78.1 %while.52 = (s32[]{:T(128)}, f32[512,128]{1,0:T(8,128)}, s32[]{:T(128)}, s32[]{:T(128)}, bf16[8192,128]{1,0:T(8,128)(2,1)}, /*index=5*/bf16[512,128]{1,0:T(8,128...) while((s32[]{:T(128)}, f32[512,128]{1,0:T(8,128)}, ...), condition=%wide.region_8.9_spmd.clone, body=%wide.region_7.8_spmd.clone.sunk | while | flops 608714240 | bytes 6189840 | solution.py:100
  252.7 2.7 fusion.200
  257.5 2.9 fusion.200
  262.3 2.9 fusion.200
  267.2 2.9 fusion.200
  272.1 2.9 fusion.200
  277.0 2.9 fusion.200
  281.9 2.9 fusion.200
  286.8 2.9 fusion.200
  291.7 2.9 fusion.200
  296.6 2.9 fusion.200
  301.4 2.9 fusion.200
  306.3 2.9 fusion.200
  311.2 2.9 fusion.200
  316.1 2.9 fusion.200
  321.0 2.9 fusion.200
  325.9 2.9 fusion.200
  330.5 2.1 fusion.122
  332.6 18.4 %all-gather.10.cloned.1.call-done = bf16[8192,128]{0,1:T(8,128)(2,1)} async-done(((bf16[512,128]{0,1:T(8,128)(2,1)}), bf16[8192,128]{0,1:T(8,128)(2,1)}) %all-gather.10.cloned.1.call-update) | async-done | bytes 2097168 | tf_op jit(solution)/shard_map/all_gather | solution.py:198
  351.0 115.0 %while.51 = (s32[]{:T(128)}, f32[512,128]{1,0:T(8,128)}, f32[512,128]{1,0:T(8,128)}, s32[]{:T(128)}, s32[]{:T(128)}, /*index=5*/bf16[8192,128]{0,1:T(8,128)(2,1)...) while((s32[]{:T(128)}, f32[512,128]{1,0:T(8,128)}, ...), condition=%wide.region_6.7_spmd.clone, body=%wide.region_5.6_spmd.clone.sunk | while | flops 779580928 | bytes 11904381 | solution.py:100
  355.3 2.1 fusion.191
  369.7 2.1 fusion.191
  384.1 2.1 fusion.191
  472.7 183.7 %all-reduce.3.cloned.1.call-done = (f32[512,512]{0,1:T(8,128)}, f32[128,512]{1,0:T(8,128)}) async-done(((f32[512,512]{0,1:T(8,128)}, f32[128,512]{1,0:T(8,128)}), (f32[512,512]{0,1:T(8,128)}, f32[128,512]{1,0:T(8,128)})) %all-reduce.3.cloned.1.call-update) | async-done | bytes 1310736 | tf_op jit(solution)/shard_map/psum | solution.py:252
  659.8 21.9 %reduce-scatter.4.cloned.1.call-done = bf16[128,512]{1,0:T(8,128)(2,1)} async-done(((bf16[512,512]{1,0:T(8,128)(2,1)}), bf16[128,512]{1,0:T(8,128)(2,1)}) %reduce-scatter.4.cloned.1.call-update) | async-done | bytes 131088
  (589 shorter events, 180.4 us)
Async XLA Ops:
  7.2 9.0 %copy-start.13 = (s32[1,3]{1,0:T(1,128)S(1)}, s32[1,3]{1,0:T(1,128)}, u32[]{:S(2)}) copy-start(s32[1,3]{1,0:T(1,128)} %param.18) | copy-start | bytes 40
  7.2 10.7 %copy-start.12 = (s32[1,512]{1,0:T(1,128)S(1)}, s32[1,512]{1,0:T(1,128)}, u32[]{:S(2)}) copy-start(s32[1,512]{1,0:T(1,128)} %param.19) | copy-start | bytes 6148
  7.2 90.3 %all-gather.6.cloned.1.call-start = ((), (), s32[]{:S(2)}) async-start(), calls=%async_computation.1 | async-start | bytes 2228224 | tf_op jit(solution)/shard_map/all_gather | solution.py:142
  9.9 45.6 %copy-start.14 = (f32[1,128]{1,0:T(1,128)S(1)}, f32[1,128]{1,0:T(1,128)}, u32[]{:S(2)}) copy-start(f32[1,128]{1,0:T(1,128)} %param.17) | copy-start | bytes 1540
  11.4 170.7 %all-gather.8.cloned.1.call-start = ((), (), s32[]{:S(2)}) async-start(), calls=%async_computation.2 | async-start | bytes 2228224 | tf_op jit(solution)/shard_map/all_gather | solution.py:143
  12.2 320.4 %all-gather.12.cloned.1.call-start = ((), (), s32[]{:S(2)}) async-start(), calls=%async_computation.4 | async-start | bytes 2228224 | tf_op jit(solution)/shard_map/all_gather | solution.py:197
  12.9 338.1 %all-gather.10.cloned.1.call-start = ((), (), s32[]{:S(2)}) async-start(), calls=%async_computation.3 | async-start | bytes 2228224 | tf_op jit(solution)/shard_map/all_gather | solution.py:198
  245.4 5.2 copy-start.3
  250.6 405.8 %all-reduce.3.cloned.1.call-start = ((), (), s32[]{:S(2)}) async-start(), calls=%async_computation.6 | async-start | bytes 2621440 | tf_op jit(solution)/shard_map/psum | solution.py:252
  250.7 2.0 copy-start.11
  265.2 2.0 copy-start.11
  279.9 2.0 copy-start.11
  318.9 2.0 copy-start.11
  351.0 2.5 copy-start.8
  355.3 2.2 copy-start.9
  358.2 2.4 copy-start.8
  362.5 2.2 copy-start.9
  365.4 2.5 copy-start.8
  369.7 2.2 copy-start.9
  372.6 2.4 copy-start.8
  376.9 2.2 copy-start.9
  379.7 2.5 copy-start.8
  384.1 2.2 copy-start.9
  386.9 2.4 copy-start.8
  391.3 2.2 copy-start.9
  394.1 2.5 copy-start.8
  398.4 2.2 copy-start.9
  401.3 2.4 copy-start.8
  405.6 2.2 copy-start.9
  408.5 2.5 copy-start.8
  412.8 2.2 copy-start.9
  415.7 2.4 copy-start.8
  420.0 2.2 copy-start.9
  422.9 2.5 copy-start.8
  427.2 2.2 copy-start.9
  430.1 2.4 copy-start.8
  434.4 2.2 copy-start.9
  437.2 2.5 copy-start.8
  441.6 2.2 copy-start.9
  444.4 2.4 copy-start.8
  448.8 2.2 copy-start.9
  451.6 2.5 copy-start.8
  455.9 2.2 copy-start.9
  458.8 2.4 copy-start.8
  463.1 2.2 copy-start.9
  466.0 3.2 copy-start.2
  471.1 210.7 %reduce-scatter.4.cloned.1.call-start = ((), (), s32[]{:S(2)}) async-start(), calls=%async_computation.5 | async-start | bytes 655360
  656.4 2.7 copy-start.10
  (48 other events, 69.6 us)
Sparse Core Ops, SparseCore 0:
  11.6 85.8 all-gather.5
  100.5 81.6 all-gather.7
  184.7 81.7 all-gather.11
  269.3 81.6 all-gather.9
  471.2 185.1 all-reduce.2
  658.9 22.7 reduce-scatter.3
where the time goes:
time: 694 us; the launch traced here: 690 us
  waiting for transfers between devices  343 us (49%)
  matrix products  237 us (34%)
  local copies, waits for them, and re-layouts  39.1 us (6%)
  blocking collectives  37.6 us (5%)
  between operations  15.5 us (2%)
  other arithmetic  15.4 us (2%)
    psum x1, waiting for transfers between devices, body(): win_total, wout_total = lax.psum((win_terms, wout_terms), ('seq', 'dp'))  184 us
    all_gather x1, waiting for transfers between devices, body(): value_piece = lax.all_gather(value_part, 'seq', axis=0, tiled=True)  80.7 us
    dot_general x16, matrix products, query_one_block(): return running + jnp.dot(slope, key_blk, preferred_element_type=jnp.float32)  45.6 us
    dot_general x16, matrix products, forward_one_block(): jnp.dot(attend, value_blk, preferred_element_type=jnp.float32)  45.2 us
    dot_general x32, matrix products, pair_tile(): jnp.einsum('qd,kd->qk', query_blk, key_blk, preferred_element_type=jnp.fl...  39 us
    all_gather x1, blocking collectives, body(): time_piece = lax.all_gather(my_times, 'seq', axis=0, tiled=True)  37.6 us
    all_gather x1, waiting for transfers between devices, body(): key_piece = lax.all_gather(key_part, 'seq', axis=0, tiled=True)  36.5 us
    dot_general x16, matrix products, key_one_block(): jnp.einsum('qk,qd->kd', slope, query_blk, preferred_element_type=jnp.floa...  34 us
  transfers between devices with their start and end apart: 6, of which 5 were waited for; matrix products, arithmetic and copies ran while one was open for 24% of the time, Pallas kernels for 0%

commit v1 on v0

v1 whole, which is shorter than its diff:
```python
import functools
import math

import jax
import jax.numpy as jnp
from jax import lax
from jax.experimental import pallas as pl
from jax.experimental.pallas import tpu as pltpu
from jax.sharding import Mesh
from jax.sharding import PartitionSpec as P

PAD_ROWS = 128
EPSILON = 0.05
ROWS = 512
HALF = 256
DH = 128
NB = 128
WIDTH = 512
GROUP = 4
BIG = 1 << 24
BF = jnp.bfloat16
F32 = jnp.float32
FACTOR = 1.0 / math.sqrt(DH)
PIECE = 80
STEP = 2
LIST = 128

TRANSPOSED = ("z2", "z1", "xl", "core")
SWAP = [
    (8 * a + 4 * b + 2 * c + d, 8 * d + 4 * c + 2 * b + a)
    for a in (0, 1)
    for b in (0, 1)
    for c in (0, 1)
    for d in (0, 1)
]
FLIP = [(0, 1), (1, 0)]


def flip_x(rel):
    return [(i, i ^ rel) for i in range(4)]


def dot(a, b, dims=((1,), (0,))):
    return lax.dot_general(a, b, (dims, ((), ())), preferred_element_type=F32)


NT = ((1,), (1,))
TN = ((0,), (0,))


def call(kernel, outs, args, scratch=(), flops=0, unread=0, passed=0):
    specs = [pl.BlockSpec(memory_space=pltpu.VMEM)] * (len(args) - unread - passed)
    specs += [pl.BlockSpec(memory_space=pl.ANY)] * (unread + passed)
    for n, a in enumerate(args):
        if a.ndim == 1:
            specs[n] = pl.BlockSpec(memory_space=pltpu.SMEM)
    before = len(outs)
    outs = list(outs) + [(a.shape, a.dtype) for a in args[len(args) - passed :]]
    out_specs = [pl.BlockSpec(memory_space=pltpu.VMEM)] * before
    out_specs += [pl.BlockSpec(memory_space=pl.ANY)] * passed
    for n, (shape, _) in enumerate(outs):
        if len(shape) == 1:
            out_specs[n] = pl.BlockSpec(memory_space=pltpu.SMEM)
    moved = sum(a.size * a.dtype.itemsize for a in args)
    moved += sum(math.prod(s) * jnp.dtype(t).itemsize for s, t in outs)
    return pl.pallas_call(
        kernel,
        out_shape=[jax.ShapeDtypeStruct(s, t) for s, t in outs],
        in_specs=specs,
        out_specs=out_specs,
        input_output_aliases={len(args) - passed + n: before + n for n in range(passed)},
        scratch_shapes=list(scratch),
        compiler_params=pltpu.CompilerParams(vmem_limit_bytes=40 * 1024 * 1024),
        cost_estimate=pl.CostEstimate(flops=flops, bytes_accessed=moved, transcendentals=0),
    )(*args)


def prepare_kernel(x_ref, times_ref, lengths_ref, out_ref):
    out_ref[0:ROWS, :] = x_ref[...]
    row = lax.broadcasted_iota(jnp.int32, (16, WIDTH), 0)
    lengths = jnp.concatenate([lengths_ref[...]] * (WIDTH // DH), 1).astype(F32)
    times = times_ref[...].astype(F32)
    out_ref[ROWS:, :] = jnp.where(row == 0, times, jnp.where(row == 1, lengths, 0.0)).astype(BF)


def gated_kernel(upstream_ref, wout_ref, out_ref):
    out_ref[...] = dot(upstream_ref[...], wout_ref[...], NT).astype(BF)


def project_kernel(xa_ref, w_ref, table_ref, _, kv_ref, q_ref, gate_ref, slope_ref, __):
    projected = dot(xa_ref[0:ROWS, :], w_ref[...])
    sig = 0.5 + 0.5 * jnp.tanh(0.5 * projected)
    act = projected * sig
    slope_ref[...] = sig * (1.0 + projected * (1.0 - sig))
    gate_ref[...] = act[:, 0:DH].astype(BF)
    kv_ref[0:ROWS, DH : 2 * DH] = act[:, DH : 2 * DH].astype(BF)
    q_ref[:, 0:DH] = (act[:, 2 * DH : 3 * DH] * (0.5 * FACTOR)).astype(BF)
    kv_ref[0:ROWS, 0:DH] = act[:, 3 * DH : 4 * DH].astype(BF)
    times = xa_ref[ROWS : ROWS + 16, :].astype(F32)[0:1, :]
    row = lax.broadcasted_iota(jnp.int32, (16, HALF), 0)
    extra = jnp.where(row == 0, times[:, 0:HALF], jnp.where(row == 1, times[:, HALF:], 0.0))
    kv_ref[ROWS : ROWS + 16, :] = extra.astype(BF)
    table = jnp.broadcast_to(table_ref[...] * 0.5, (NB, NB))
    rolled = pltpu.roll(table, 0, 1, stride=1, stride_axis=0)
    first = lax.broadcasted_iota(jnp.int32, (NB, NB), 0)
    second = lax.broadcasted_iota(jnp.int32, (NB, NB), 1)
    square = jnp.where(second >= first, rolled, rolled.T).astype(BF)
    bucket = lax.broadcasted_iota(jnp.int32, (NB, ROWS), 0).astype(F32)
    hot = (bucket == times).astype(F32).astype(BF)
    q_ref[:, DH : 2 * DH] = dot(square, hot).T.astype(BF)


def first_of(rows, first_end, second_end):
    return jnp.where(rows < first_end, 0, jnp.where(rows < second_end, first_end, BIG))


def key_row_of(meta_ref, slot):
    x, core, z = (meta_ref[n] for n in range(2, 5))
    owner = x ^ (slot // 2)
    index = 8 * (owner // 2) + 2 * (owner % 2) + 4 * core + z
    return jnp.where(slot % 2 == 0, index, 31 - index) * HALF


def query_row_of(meta_ref, j):
    x, core, z = (meta_ref[n] for n in range(2, 5))
    rel = j % GROUP
    index = 8 * (x // 2) + 2 * (x % 2) + 4 * (core ^ (rel // 2)) + (z ^ (rel % 2))
    return jnp.where(j < GROUP, index, 31 - index) * HALF


def list_pairs(meta_ref, list_ref):
    first_end, second_end = meta_ref[0], meta_ref[1]

    def queries(j, count):
        row = query_row_of(meta_ref, j)
        lowest = first_of(row, first_end, second_end)

        def keys(slot, count):
            key_row = key_row_of(meta_ref, slot)
            valid = (key_row <= row) & (key_row + HALF > lowest)
            list_ref[count] = j * 8 + slot
            return count + valid.astype(jnp.int32)

        return lax.fori_loop(0, 2 * GROUP, keys, count, unroll=True)

    count = lax.fori_loop(0, 2 * GROUP, queries, jnp.int32(0))
    for more in range(STEP):
        list_ref[count + more] = -1
    list_ref[LIST - 1] = count


def sweep(meta_ref, list_ref, one, key_axis):
    def step(i, carry):
        done = []
        for n in range(STEP):
            item = list_ref[i * STEP + n]
            live = item >= 0
            item = jnp.maximum(item, 0)
            j, slot = item // 8, item % 8
            rows = jnp.where(live, query_row_of(meta_ref, j), -HALF)
            mask = mask_of(rows, key_row_of(meta_ref, slot), meta_ref[0], meta_ref[1], key_axis)
            done.append(one(j, slot, mask))
        for finish in done:
            finish()
        return carry

    lax.fori_loop(0, (list_ref[LIST - 1] + STEP - 1) // STEP, step, 0)


def mask_of(query_row, key_row, first_end, second_end, key_axis):
    shape_q = (HALF, 1) if key_axis == 1 else (1, HALF)
    rows_q = query_row + lax.broadcasted_iota(jnp.int32, shape_q, 1 - key_axis)
    rows_k = key_row + lax.broadcasted_iota(jnp.int32, (HALF, HALF), key_axis)
    return (rows_k <= rows_q) & (rows_k >= first_of(rows_q, first_end, second_end))


def forward_kernel(
    meta_ref, kv0, kv1, kv2, kv3, q0, q1, q2, q3, _,
    keep_ref, send_ref, k_ref, v_ref, q_ref, list_ref, acc,
):
    bucket = lax.broadcasted_iota(jnp.int32, (NB, HALF), 0).astype(F32)
    for rel, kv in enumerate((kv0, kv1, kv2, kv3)):
        tail = kv[ROWS : ROWS + 16, :].astype(F32)
        for half in (0, 1):
            rows = slice(half * HALF, (half + 1) * HALF)
            hot = (bucket == tail[half : half + 1, :]).astype(F32)
            k_ref[rel * 2 + half, :, 0:DH] = kv[rows, 0:DH]
            k_ref[rel * 2 + half, :, DH : 2 * DH] = hot.T.astype(BF)
            v_ref[rel * 2 + half] = kv[rows, DH : 2 * DH]
    for rel, q in enumerate((q0, q1, q2, q3)):
        for half in (0, 1):
            q_ref[half * GROUP + rel] = q[half * HALF : (half + 1) * HALF, :]
    acc[...] = jnp.zeros_like(acc)

    list_pairs(meta_ref, list_ref)

    def one(j, slot, mask):
        scores = dot(q_ref[j], k_ref[slot], NT)
        attend = jnp.where(mask, scores + scores * jnp.tanh(scores), 0.0)
        result = dot(attend.astype(BF), v_ref[slot])

        def finish():
            acc[j] += result

        return finish

    sweep(meta_ref, list_ref, one, 1)
    for rel in (0, 1):
        for half in (0, 1):
            rows = slice(rel * ROWS + half * HALF, rel * ROWS + (half + 1) * HALF)
            keep_ref[rows, :] = acc[half * GROUP + rel]
            send_ref[rows, :] = acc[half * GROUP + rel + 2].astype(BF)


def middle_kernel(
    meta_ref, keep, got_core, got_z, grad_gated_ref, gate, slope, grad_ref, gate_ref, gated_ref
):
    first_end, second_end, x, core, z = (meta_ref[n] for n in range(5))
    block = 8 * (x // 2) + 2 * (x % 2) + 4 * core + z
    offset = lax.broadcasted_iota(jnp.int32, (ROWS, 1), 0)
    rows = jnp.where(offset < HALF, block * HALF + offset, (31 - block) * HALF + offset - HALF)
    first = jnp.where(rows < first_end, 0, jnp.where(rows < second_end, first_end, second_end))
    inverse = 1.0 / jnp.maximum(rows - first + 1, 1).astype(F32)
    total = keep[0:ROWS, :] + got_core[0:ROWS, :].astype(F32) + got_z[...].astype(F32)
    attended = total * inverse
    spread = 1.0 / jnp.sqrt(jnp.mean(attended * attended, axis=-1, keepdims=True) + EPSILON)
    normed = attended * spread
    gate_float = gate[...].astype(F32)
    gated_ref[...] = (normed * gate_float).astype(BF)
    grad_gated = grad_gated_ref[...].astype(F32)
    gate_ref[...] = (grad_gated * normed * slope[:, 0:DH]).astype(BF)
    grad_normed = grad_gated * gate_float
    inner = jnp.mean(grad_normed * normed, axis=-1, keepdims=True)
    grad_ref[...] = ((grad_normed - normed * inner) * (spread * inverse * 0.5)).astype(BF)


def backward_kernel(
    meta_ref, list_ref, k_ref, v_ref, q_ref, g0, g1, g2, g3,
    own_ref, s1_ref, s2_ref, s3_ref, keep_ref, send_ref,
    grad, kt, acc_k, acc_v, acc_q,
):
    for rel, g in enumerate((g0, g1, g2, g3)):
        for half in (0, 1):
            grad[half * GROUP + rel] = g[half * HALF : (half + 1) * HALF, :]
    for slot in range(2 * GROUP):
        kt[slot] = k_ref[slot, :, 0:DH].astype(F32).T.astype(BF)
    acc_k[...] = jnp.zeros_like(acc_k)
    acc_v[...] = jnp.zeros_like(acc_v)
    acc_q[...] = jnp.zeros_like(acc_q)

    def one(j, slot, mask):
        scores = dot(k_ref[slot], q_ref[j], NT)
        raw = dot(v_ref[slot], grad[j], NT)
        tanh = jnp.tanh(scores)
        more = 1.0 + tanh
        attend = scores * more
        slope = jnp.where(mask, raw * (more + attend * (1.0 - tanh)), 0.0).astype(BF)
        attend = jnp.where(mask, attend, 0.0).astype(BF)
        grad_q = dot(kt[slot], slope)
        grad_k = dot(slope, q_ref[j, :, 0:DH])
        grad_v = dot(attend, grad[j])

        def finish():
            acc_q[j] += grad_q
            acc_k[slot] += grad_k
            acc_v[slot] += grad_v

        return finish

    sweep(meta_ref, list_ref, one, 0)
    for rel, out in enumerate((own_ref, s1_ref, s2_ref, s3_ref)):
        for half in (0, 1):
            rows = slice(half * HALF, (half + 1) * HALF)
            out[rows, 0:DH] = (acc_k[rel * 2 + half] * 2.0).astype(out.dtype)
            out[rows, DH : 2 * DH] = (acc_v[rel * 2 + half] * 2.0).astype(out.dtype)
    for rel in (0, 1):
        for half in (0, 1):
            rows = slice(rel * ROWS + half * HALF, rel * ROWS + (half + 1) * HALF)
            keep_ref[rows, :] = acc_q[half * GROUP + rel].T * FACTOR
            send_ref[rows, :] = (acc_q[half * GROUP + rel + 2].T * FACTOR).astype(BF)


def tail_kernel(
    meta_ref, own, r1, r2, r3, keep, got_core, got_z, grad_gate, slope, w, xa, wout_terms,
    t0_ref, t1_ref, t2_ref, t3_ref, stay_ref, away_ref,
    grad, full,
):
    core, y = meta_ref[3], meta_ref[5]
    kv = own[...] + r1[...].astype(F32) + r2[...].astype(F32) + r3[...].astype(F32)
    query = keep[0:ROWS, :] + got_core[0:ROWS, :].astype(F32) + got_z[...].astype(F32)
    grad[:, 0:DH] = grad_gate[...]
    grad[:, DH : 2 * DH] = (kv[:, DH:] * slope[:, DH : 2 * DH]).astype(BF)
    grad[:, 2 * DH : 3 * DH] = (query * slope[:, 2 * DH : 3 * DH]).astype(BF)
    grad[:, 3 * DH :] = (kv[:, 0:DH] * slope[:, 3 * DH :]).astype(BF)
    for rel, out in enumerate((t0_ref, t1_ref, t2_ref, t3_ref)):
        rows = w[pl.ds(pl.multiple_of((y ^ rel) * DH, DH), DH), :]
        out[...] = dot(grad[...], rows, NT).astype(out.dtype)
    full[0:WIDTH, :] = dot(xa[0:ROWS, :], grad[...], TN)
    full[WIDTH:, :] = wout_terms[...]
    size = full.shape[0] // 2
    stay_ref[...] = full[pl.ds(pl.multiple_of(core * size, 64), size), :]
    away_ref[...] = full[pl.ds(pl.multiple_of((1 - core) * size, 64), size), :].astype(BF)


def gather_kernel(p0, p1, p2, p3, t0, t1, t2, t3, total_ref, grad_ref):
    total = p0[...] + p1[...].astype(F32) + p2[...].astype(F32) + p3[...].astype(F32)
    total_ref[...] = total.astype(BF)
    grad = t0[...] + t1[...].astype(F32) + t2[...].astype(F32) + t3[...].astype(F32)
    grad_ref[...] = grad.astype(BF)


def add_kernel(a_ref, b_ref, _, out_ref):
    out_ref[...] = (a_ref[...].astype(F32) + b_ref[...].astype(F32)).astype(BF)


def split_kernel(meta_ref, stay, got, p0_ref, p1_ref, p2_ref, p3_ref, total):
    x = meta_ref[2]
    total[...] = stay[...] + got[...].astype(F32)
    for rel, out in enumerate((p0_ref, p1_ref, p2_ref, p3_ref)):
        rows = pl.ds(pl.multiple_of((x ^ rel) * PIECE, 16), PIECE)
        out[...] = total[rows, :].astype(out.dtype)


def join_kernel(meta_ref, p0, p1, p2, p3, out_ref):
    x = meta_ref[2]
    for rel, piece in enumerate((p0, p1, p2, p3)):
        out_ref[pl.ds(pl.multiple_of((x ^ rel) * PIECE, 16), PIECE), :] = piece[...]


def final_kernel(scale, meta_ref, mine, other, win_ref, wout_ref, full):
    core = meta_ref[3]
    size = full.shape[0] // 2
    full[pl.ds(pl.multiple_of(core * size, 64), size), :] = mine[...].astype(F32) * scale
    full[pl.ds(pl.multiple_of((1 - core) * size, 64), size), :] = other[...].astype(F32) * scale
    win_ref[...] = full[0:WIDTH, :]
    wout_ref[...] = full[WIDTH:, :]


def body(layer_input, grad_output, weight_in, weight_out, time_table, user_lengths, time_buckets):
    lengths = jnp.pad(user_lengths, ((0, 0), (0, DH - 3)))
    (xa,) = call(
        prepare_kernel,
        [((ROWS + 16, WIDTH), BF)],
        (layer_input[0], time_buckets, lengths),
    )
    xa = lax.ppermute(xa, TRANSPOSED, SWAP)

    core = lax.axis_index("core")
    x = 2 * lax.axis_index("xh") + lax.axis_index("xl")
    z = lax.axis_index("z0")
    lengths = PAD_ROWS * xa[ROWS + 1, 0:2].astype(jnp.int32)
    places = jnp.stack([x, core, z, lax.axis_index("y"), 0 * x, 0 * x])
    meta = jnp.concatenate(
        [lengths[0:1], lengths[0:1] + lengths[1:2], places.astype(jnp.int32)]
    )

    (grad_gated,) = call(
        gated_kernel, [((ROWS, DH), BF)], (grad_output[0], weight_out)
    )
    kv, q, gate, slope, grad_gated = call(
        project_kernel,
        [((ROWS + 16, 2 * DH), BF), ((ROWS, 2 * DH), BF), ((ROWS, DH), BF), ((ROWS, WIDTH), F32)],
        (xa, weight_in, time_table, grad_gated),
        passed=1,
        flops=2 * ROWS * WIDTH * WIDTH,
    )
    kvs = [kv] + [lax.ppermute(kv, ("xh", "xl"), flip_x(rel)) for rel in (1, 3, 2)]
    kvs = [kvs[0], kvs[1], kvs[3], kvs[2]]
    grad_gated = lax.ppermute(grad_gated, TRANSPOSED, SWAP)
    q_z = lax.ppermute(q, "z0", FLIP)
    qs = [q, q_z, lax.ppermute(q, "core", FLIP), lax.ppermute(q_z, "core", FLIP)]

    blocks = 2 * GROUP
    keep, send, k_all, v_all, q_all, pairs = call(
        forward_kernel,
        [
            ((2 * ROWS, DH), F32),
            ((2 * ROWS, DH), BF),
            ((blocks, HALF, 2 * DH), BF),
            ((blocks, HALF, DH), BF),
            ((blocks, HALF, 2 * DH), BF),
            ((LIST,), jnp.int32),
        ],
        (meta, *kvs, *qs, grad_gated),
        unread=1,
        scratch=[pltpu.VMEM((blocks, HALF, DH), F32)],
        flops=20 * 6 * HALF * HALF * DH,
    )
    got_core = lax.ppermute(send, "core", FLIP)
    part = (keep[ROWS:] + got_core[ROWS:].astype(F32)).astype(BF)
    got_z = lax.ppermute(part, "z0", FLIP)

    grad, grad_gate, gated = call(
        middle_kernel,
        [((ROWS, DH), BF)] * 3,
        (meta, keep, got_core, got_z, grad_gated, gate, slope),
        flops=2 * ROWS * WIDTH * DH,
    )
    grad_z = lax.ppermute(grad, "z0", FLIP)
    grads = [grad, grad_z, lax.ppermute(grad, "core", FLIP), lax.ppermute(grad_z, "core", FLIP)]
    gated = lax.ppermute(gated, TRANSPOSED, SWAP)
    wout_terms = dot(gated, grad_output[0], TN)

    own, s1, s2, s3, keep, send = call(
        backward_kernel,
        [((ROWS, 2 * DH), F32)]
        + [((ROWS, 2 * DH), BF)] * 3
        + [((2 * ROWS, DH), F32), ((2 * ROWS, DH), BF)],
        (meta, pairs, k_all, v_all, q_all, *grads),
        scratch=[
            pltpu.VMEM((blocks, HALF, DH), BF),
            pltpu.VMEM((blocks, DH, HALF), BF),
            pltpu.VMEM((blocks, HALF, DH), F32),
            pltpu.VMEM((blocks, HALF, DH), F32),
            pltpu.VMEM((blocks, DH, HALF), F32),
        ],
        flops=20 * 12 * HALF * HALF * DH,
    )
    r1 = lax.ppermute(s1, ("xh", "xl"), flip_x(1))
    r3 = lax.ppermute(s3, ("xh", "xl"), flip_x(3))
    r2 = lax.ppermute(s2, ("xh", "xl"), flip_x(2))
    got_core = lax.ppermute(send, "core", FLIP)
    part = (keep[ROWS:] + got_core[ROWS:].astype(F32)).astype(BF)
    got_z = lax.ppermute(part, "z0", FLIP)

    t0, t1, t2, t3, stay, away = call(
        tail_kernel,
        [((ROWS, DH), F32)] + [((ROWS, DH), BF)] * 3 + [((320, WIDTH), F32), ((320, WIDTH), BF)],
        (meta, own, r1, r2, r3, keep, got_core, got_z, grad_gate, slope, weight_in, xa, wout_terms),
        scratch=[pltpu.VMEM((ROWS, WIDTH), BF), pltpu.VMEM((WIDTH + DH, WIDTH), F32)],
        flops=4 * ROWS * WIDTH * WIDTH,
    )
    got = lax.ppermute(away, "core", FLIP)
    flip_y = [[(i, i ^ rel) for i in range(4)] for rel in range(4)]
    u1, u3, u2 = (lax.ppermute(t, "y", flip_y[rel]) for t, rel in ((t1, 1), (t3, 3), (t2, 2)))

    p0, p1, p2, p3 = call(
        split_kernel,
        [((PIECE, WIDTH), F32)] + [((PIECE, WIDTH), BF)] * 3,
        (meta, stay, got),
        scratch=[pltpu.VMEM((GROUP * PIECE, WIDTH), F32)],
    )
    g1, g3, g2 = (
        lax.ppermute(p, ("xh", "xl"), flip_x(rel)) for p, rel in ((p1, 1), (p3, 3), (p2, 2))
    )
    total, grad_local = call(
        gather_kernel,
        [((PIECE, WIDTH), BF), ((ROWS, DH), BF)],
        (p0, g1, g2, g3, t0, u1, u2, u3),
    )
    grad_local = lax.ppermute(grad_local, TRANSPOSED, SWAP)
    other = lax.ppermute(total, "z0", FLIP)
    total = (total.astype(F32) + other.astype(F32)).astype(BF)
    other = lax.ppermute(total, "z1", FLIP)
    total = (total.astype(F32) + other.astype(F32)).astype(BF)
    other = lax.ppermute(total, "z2", FLIP)
    (total,) = call(add_kernel, [((PIECE, WIDTH), BF)], (total, other, grad_local), unread=1)
    h1, h3, h2 = (lax.ppermute(total, ("xh", "xl"), flip_x(rel)) for rel in (1, 3, 2))
    (mine_half,) = call(join_kernel, [((320, WIDTH), BF)], (meta, total, h1, h2, h3))
    other_half = lax.ppermute(mine_half, "core", FLIP)
    normalizer = 1.0 / math.sqrt(4 * 16 * ROWS)
    win, wout = call(
        functools.partial(final_kernel, normalizer),
        [((WIDTH, WIDTH), F32), ((DH, WIDTH), F32)],
        (meta, mine_half, other_half),
        scratch=[pltpu.VMEM((WIDTH + DH, WIDTH), F32)],
    )
    return (grad_local[None], win, wout)


def solution(mesh):
    names = ("xh", "z2", "z1", "z0", "xl", "core", "y")
    fine = Mesh(mesh.devices.reshape(2, 2, 2, 2, 2, 2, 4), names)
    dp, seq = ("xl", "core"), ("xh", "z2", "z1", "z0")
    placed = (
        P(dp, seq, None),
        P(dp, seq, None),
        P(None, "y"),
        P("y", None),
        P("y", None),
        P(dp, None),
        P(dp, seq),
    )
    return jax.shard_map(
        body,
        mesh=fine,
        in_specs=placed,
        out_specs=(P(dp, seq, "y"), P(None, "y"), P("y", None)),
        check_vma=False,
    )
```

time: 694 us -> 159 us (0.23)
  waiting for transfers between devices: 343 us -> 50 us
  matrix products: 237 us -> 0.25 us
  starting transfers between devices: 0.24 us -> 79.7 us
  blocking collectives: 37.6 us -> 0 us
  local copies, waits for them, and re-layouts: 39.1 us -> 3.71 us
  Pallas kernels: 0 us -> 21.8 us
  other arithmetic: 15.4 us -> 0.12 us
  between operations: 15.5 us -> 2.17 us
    dot_general x166 -> x1, matrix products: 237 us -> 0.25 us  [dot(): return lax.dot_general(a, b, (dims, ((), ())), preferred_element_type=F32)]
    psum x1 -> x0, waiting for transfers between devices: 184 us -> none  [body(): win_total, wout_total = lax.psum((win_terms, wout_terms), ('seq', 'dp'))]
    all_gather x4 -> x0, waiting for transfers between devices: 136 us -> none  [the longest x1 80.7 us: body(): value_piece = lax.all_gather(value_part, 'seq', axis=0, tiled=True)]
    ppermute x0 -> x34, starting transfers between devices: none -> 79.7 us  [the longest x3 16.4 us: body(): lax.ppermute(kv, ('xh', 'xl'), flip_x(rel))]
    ppermute x0 -> x34, waiting for transfers between devices: none -> 50 us  [the longest x1 10.2 us: body(): xa = lax.ppermute(xa, TRANSPOSED, SWAP)]
    all_gather x1 -> x0, blocking collectives: 37.6 us -> none  [body(): time_piece = lax.all_gather(my_times, 'seq', axis=0, tiled=True)]
    unnamed x7 -> x0, waiting for transfers between devices: 23.4 us -> none
    pallas_call x0 -> x12, Pallas kernels: none -> 21.8 us  [call(): pl.pallas_call(kernel, out_shape=[jax.ShapeDtypeStruct(s, t) for s, t in...]
  transfers between devices with their start and end apart: 6 -> 34, of which waited for: 5 -> 18; matrix products, arithmetic and copies ran while one was open for 24% -> 1% of each run, Pallas kernels for 0% -> 1%
where the time goes in v1:
time: 159 us; the launch traced here: 158 us
  starting transfers between devices  79.7 us (50%)
  waiting for transfers between devices  50 us (31%)
  Pallas kernels  21.8 us (14%)
  local copies, waits for them, and re-layouts  3.71 us (2%)
  between operations  2.17 us (1%)
    pallas_call x12, Pallas kernels, call(): pl.pallas_call(kernel, out_shape=[jax.ShapeDtypeStruct(s, t) for s, t in...  21.8 us
    ppermute x3, starting transfers between devices, body(): lax.ppermute(kv, ('xh', 'xl'), flip_x(rel))  16.4 us
    ppermute x1, starting transfers between devices, body(): xa = lax.ppermute(xa, TRANSPOSED, SWAP)  10.3 us
    ppermute x1, waiting for transfers between devices, body(): xa = lax.ppermute(xa, TRANSPOSED, SWAP)  10.2 us
    ppermute x1, waiting for transfers between devices, body(): grad_local = lax.ppermute(grad_local, TRANSPOSED, SWAP)  7.24 us
    ppermute x1, waiting for transfers between devices, body(): r2 = lax.ppermute(s2, ('xh', 'xl'), flip_x(2))  5.62 us
    ppermute x1, starting transfers between devices, body(): r1 = lax.ppermute(s1, ('xh', 'xl'), flip_x(1))  5.06 us
    ppermute x1, starting transfers between devices, body(): grad_gated = lax.ppermute(grad_gated, TRANSPOSED, SWAP)  5.01 us
  transfers between devices with their start and end apart: 34, of which 18 were waited for; matrix products, arithmetic and copies ran while one was open for 1% of the time, Pallas kernels for 1%

profile of v1, /device:TPU:1, one launch (start us, length us, event | category | flops | bytes accessed | tf_op | source)
XLA Modules:
  0.0 157.7 jit_solution(4678793906368896699)
XLA Ops:
  1.3 1.0 copy-done.2
  2.4 10.3 %collective-permute-start = (bf16[528,512]{1,0:T(8,128)(2,1)S(1)}, bf16[528,512]{1,0:T(8,128)(2,1)S(1)}, u32[]{:S(2)}, u32[]{:S(2)}) collective-permute-start(bf16[528,512]{1,0:T(8,128)(2,1)S(1)} %shard_map.94), channel_id=1, source_target_pairs={{0,0},{4,64},{8,32},{12,96},{32,8},{36,72},{40,40},{44,104},{64,4}... | collective-permute-start | bytes 1622024 | tf_op jit(solution)/shard_map/ppermute | solution.py:346
  13.1 10.2 %collective-permute-done.xa_ref.xa = bf16[528,512]{1,0:T(8,128)(2,1)S(1)} collective-permute-done((bf16[528,512]{1,0:T(8,128)(2,1)S(1)}, bf16[528,512]{1,0:T(8,128)(2,1)S(1)}, u32[]{:S(2)}, u32[]{:S(2)}) %collective-permute-start) | collective-permute-done | bytes 540704 | tf_op jit(solution)/shard_map/ppermute | solution.py:346
  23.3 1.4 shard_map.96
  24.7 0.7 collective-permute-start.4
  25.4 5.0 %collective-permute-start.7 = (bf16[512,128]{1,0:T(8,128)(2,1)S(1)}, bf16[512,128]{1,0:T(8,128)(2,1)S(1)}, u32[]{:S(2)}, u32[]{:S(2)}) collective-permute-start(bf16[512,128]{1,0:T(8,128)(2,1)S(1)} %get-tuple-element.39), channel_id=1, source_target_pairs={{0,0},{4,64},{8,32},{12,96},{32,8},{36,72},{40,40},{44,104},{64,4}... | collective-permute-start | bytes 393224 | tf_op jit(solution)/shard_map/ppermute | solution.py:369
  30.5 11.1 %collective-permute-start.3 = (bf16[528,256]{1,0:T(8,128)(2,1)S(1)}, bf16[528,256]{1,0:T(8,128)(2,1)}, u32[]{:S(2)}, u32[]{:S(2)}) collective-permute-start(bf16[528,256]{1,0:T(8,128)(2,1)S(1)} %get-tuple-element.37.kv0), channel_id=1, source_target_pairs={{0,136},{8,128},{128,8},{136,0},{1,137},{9,129},{129,9},{137,1},{2... | collective-permute-start | bytes 811016 | tf_op jit(solution)/shard_map/ppermute | solution.py:367
  41.9 5.0 %collective-permute-start.1 = (bf16[528,256]{1,0:T(8,128)(2,1)S(1)}, bf16[528,256]{1,0:T(8,128)(2,1)}, u32[]{:S(2)}, u32[]{:S(2)}) collective-permute-start(bf16[528,256]{1,0:T(8,128)(2,1)S(1)} %get-tuple-element.37.kv0), channel_id=1, source_target_pairs={{0,8},{8,0},{128,136},{136,128},{1,9},{9,1},{129,137},{137,129},{2... | collective-permute-start | bytes 811016 | tf_op jit(solution)/shard_map/ppermute | solution.py:367
  48.8 0.7 concatenate.3.meta_ref
  49.5 4.2 %collective-permute-done.3.kv3 = bf16[528,256]{1,0:T(8,128)(2,1)} collective-permute-done((bf16[528,256]{1,0:T(8,128)(2,1)S(1)}, bf16[528,256]{1,0:T(8,128)(2,1)}, u32[]{:S(2)}, u32[]{:S(2)}) %collective-permute-start.3) | collective-permute-done | bytes 270368 | tf_op jit(solution)/shard_map/ppermute | solution.py:367
  53.7 0.8 collective-permute-done.1.kv1
  54.6 7.1 %shard_map.97 = (f32[1024,128]{1,0:T(8,128)S(1)}, bf16[1024,128]{1,0:T(8,128)(2,1)S(1)}, bf16[8,256,256]{2,1,0:T(8,128)(2,1)S(1)}, bf16[8,256,128]{2,1,0:T(8,128...) custom-call(s32[8]{0:T(128)S(1)} %concatenate.3.meta_ref, bf16[528,256]{1,0:T(8,128)(2,1)S(1)} %get-tuple-element.37.kv0, ...), custom_call_target="tpu_custom_call" | custom-call | flops 1006632960 | bytes 5669408 | tf_op jit(solution)/shard_map/pallas_call | solution.py:66
  61.7 1.4 collective-permute-start.8
  63.1 1.2 collective-permute-done.8.got_core
  64.3 1.7 %collective-permute-start.9 = (bf16[512,128]{1,0:T(8,128)(2,1)S(1)}, bf16[512,128]{1,0:T(8,128)(2,1)S(1)}, u32[]{:S(2)}, u32[]{:S(2)}) collective-permute-start(bf16[512,128]{1,0:T(8,128)(2,1)S(1)} %add_convert_fusion.1), channel_id=1, source_target_pairs={{0,16},{16,0},{1,17},{17,1},{2,18},{18,2},{3,19},{19,3},{4,20},{20... | collective-permute-start | bytes 393224 | tf_op jit(solution)/shard_map/ppermute | solution.py:391
  65.9 3.4 %collective-permute-done.9.got_z = bf16[512,128]{1,0:T(8,128)(2,1)S(1)} collective-permute-done((bf16[512,128]{1,0:T(8,128)(2,1)S(1)}, bf16[512,128]{1,0:T(8,128)(2,1)S(1)}, u32[]{:S(2)}, u32[]{:S(2)}) %collective-permute-start.9) | collective-permute-done | bytes 131104 | tf_op jit(solution)/shard_map/ppermute | solution.py:391
  69.3 0.9 shard_map.98
  70.3 1.4 collective-permute-start.10
  71.7 1.5 collective-permute-start.11
  73.2 1.0 collective-permute-done.10.g1
  74.2 2.2 %collective-permute-start.12 = (bf16[512,128]{1,0:T(8,128)(2,1)S(1)}, bf16[512,128]{1,0:T(8,128)(2,1)S(1)}, u32[]{:S(2)}, u32[]{:S(2)}) collective-permute-start(bf16[512,128]{1,0:T(8,128)(2,1)S(1)} %collective-permute-done.10.g1), channel_id=1, source_target_pairs={{0,4},{4,0},{1,5},{5,1},{2,6},{6,2},{3,7},{7,3},{8,12},{12,8},{9,1... | collective-permute-start | bytes 393224 | tf_op jit(solution)/shard_map/ppermute | solution.py:400
  76.4 1.0 collective-permute-done.12.g3
  77.4 7.1 %shard_map.99 = (f32[512,256]{1,0:T(8,128)S(1)}, bf16[512,256]{1,0:T(8,128)(2,1)S(1)}, bf16[512,256]{1,0:T(8,128)(2,1)S(1)}, bf16[512,256]{1,0:T(8,128)(2,1)S(1)...) custom-call(s32[8]{0:T(128)S(1)} %concatenate.3.meta_ref, s32[128]{0:T(128)S(1)} %get-tuple-element.40.list_ref, ...), custom_call_target="tpu_custom_call" | custom-call | flops 2013265920 | bytes 5243424 | tf_op jit(solution)/shard_map/pallas_call | solution.py:66
  85.0 1.9 %collective-permute-start.18 = (bf16[512,128]{1,0:T(8,128)(2,1)S(1)}, bf16[512,128]{1,0:T(8,128)(2,1)S(1)}, u32[]{:S(2)}, u32[]{:S(2)}) collective-permute-start(bf16[512,128]{1,0:T(8,128)(2,1)S(1)} %get-tuple-element.56), channel_id=1, source_target_pairs={{0,0},{4,64},{8,32},{12,96},{32,8},{36,72},{40,40},{44,104},{64,4}... | collective-permute-start | bytes 393224 | tf_op jit(solution)/shard_map/ppermute | solution.py:401
  86.9 5.1 %collective-permute-start.13 = (bf16[512,256]{1,0:T(8,128)(2,1)S(1)}, bf16[512,256]{1,0:T(8,128)(2,1)S(1)}, u32[]{:S(2)}, u32[]{:S(2)}) collective-permute-start(bf16[512,256]{1,0:T(8,128)(2,1)S(1)} %get-tuple-element.50), channel_id=1, source_target_pairs={{0,8},{8,0},{128,136},{136,128},{1,9},{9,1},{129,137},{137,129},{2... | collective-permute-start | bytes 786440 | tf_op jit(solution)/shard_map/ppermute | solution.py:419
  92.5 1.9 %collective-permute-start.15 = (bf16[512,256]{1,0:T(8,128)(2,1)S(1)}, bf16[512,256]{1,0:T(8,128)(2,1)S(1)}, u32[]{:S(2)}, u32[]{:S(2)}) collective-permute-start(bf16[512,256]{1,0:T(8,128)(2,1)S(1)} %get-tuple-element.52), channel_id=1, source_target_pairs={{0,136},{8,128},{128,8},{136,0},{1,137},{9,129},{129,9},{137,1},{2... | collective-permute-start | bytes 786440 | tf_op jit(solution)/shard_map/ppermute | solution.py:420
  94.5 1.7 %collective-permute-start.17 = (bf16[512,128]{1,0:T(8,128)(2,1)S(1)}, bf16[512,128]{1,0:T(8,128)(2,1)S(1)}, u32[]{:S(2)}, u32[]{:S(2)}) collective-permute-start(bf16[512,128]{1,0:T(8,128)(2,1)S(1)} %add_convert_fusion), channel_id=1, source_target_pairs={{0,16},{16,0},{1,17},{17,1},{2,18},{18,2},{3,19},{19,3},{4,20},{20... | collective-permute-start | bytes 393224 | tf_op jit(solution)/shard_map/ppermute | solution.py:424
  96.4 3.9 %collective-permute-done.13.r1 = bf16[512,256]{1,0:T(8,128)(2,1)S(1)} collective-permute-done((bf16[512,256]{1,0:T(8,128)(2,1)S(1)}, bf16[512,256]{1,0:T(8,128)(2,1)S(1)}, u32[]{:S(2)}, u32[]{:S(2)}) %collective-permute-start.13) | collective-permute-done | bytes 262176 | tf_op jit(solution)/shard_map/ppermute | solution.py:419
  100.3 5.6 %collective-permute-done.14.r2 = bf16[512,256]{1,0:T(8,128)(2,1)S(1)} collective-permute-done((bf16[512,256]{1,0:T(8,128)(2,1)S(1)}, bf16[512,256]{1,0:T(8,128)(2,1)S(1)}, u32[]{:S(2)}, u32[]{:S(2)}) %collective-permute-start.14) | collective-permute-done | bytes 262176 | tf_op jit(solution)/shard_map/ppermute | solution.py:421
  105.9 1.7 %shard_map.100 = (f32[512,128]{1,0:T(8,128)S(1)}, bf16[512,128]{1,0:T(8,128)(2,1)S(1)}, bf16[512,128]{1,0:T(8,128)(2,1)S(1)}, bf16[512,128]{1,0:T(8,128)(2,1)S(1...) custom-call(s32[8]{0:T(128)S(1)} %concatenate.3.meta_ref, f32[512,256]{1,0:T(8,128)S(1)} %get-tuple-element.49.own, ...), custom_call_target="tpu_custom_call" | custom-call | flops 536870912 | bytes 6373408 | tf_op jit(solution)/shard_map/pallas_call | solution.py:66
  107.6 3.4 %collective-permute-start.19 = (bf16[320,512]{1,0:T(8,128)(2,1)S(1)}, bf16[320,512]{1,0:T(8,128)(2,1)S(1)}, u32[]{:S(2)}, u32[]{:S(2)}) collective-permute-start(bf16[320,512]{1,0:T(8,128)(2,1)S(1)} %get-tuple-element.58), channel_id=1, source_target_pairs={{0,4},{4,0},{1,5},{5,1},{2,6},{6,2},{3,7},{7,3},{8,12},{12,8},{9,1... | collective-permute-start | bytes 983048 | tf_op jit(solution)/shard_map/ppermute | solution.py:433
  111.0 1.3 collective-permute-start.23
  112.3 2.6 %collective-permute-start.24 = (bf16[512,128]{1,0:T(8,128)(2,1)S(1)}, bf16[512,128]{1,0:T(8,128)(2,1)S(1)}, u32[]{:S(2)}, u32[]{:S(2)}) collective-permute-start(bf16[512,128]{1,0:T(8,128)(2,1)S(1)} %get-tuple-element.65), channel_id=1, source_target_pairs={{0,2},{1,3},{2,0},{3,1},{4,6},{5,7},{6,4},{7,5},{8,10},{9,11},{10,... | collective-permute-start | bytes 393224 | tf_op jit(solution)/shard_map/ppermute | solution.py:435
  115.7 1.9 %collective-permute-start.21 = (bf16[80,512]{1,0:T(8,128)(2,1)S(1)}, bf16[80,512]{1,0:T(8,128)(2,1)S(1)}, u32[]{:S(2)}, u32[]{:S(2)}) collective-permute-start(bf16[80,512]{1,0:T(8,128)(2,1)S(1)} %get-tuple-element.61), channel_id=1, source_target_pairs={{0,128},{8,136},{128,0},{136,8},{1,129},{9,137},{129,1},{137,9},{2... | collective-permute-start | bytes 245768 | tf_op jit(solution)/shard_map/ppermute | solution.py:444
  117.6 1.9 %collective-permute-start.22 = (bf16[80,512]{1,0:T(8,128)(2,1)S(1)}, bf16[80,512]{1,0:T(8,128)(2,1)S(1)}, u32[]{:S(2)}, u32[]{:S(2)}) collective-permute-start(bf16[80,512]{1,0:T(8,128)(2,1)S(1)} %get-tuple-element.62), channel_id=1, source_target_pairs={{0,136},{8,128},{128,8},{136,0},{1,137},{9,129},{129,9},{137,1},{2... | collective-permute-start | bytes 245768 | tf_op jit(solution)/shard_map/ppermute | solution.py:444
  119.6 1.8 %collective-permute-done.24.t2 = bf16[512,128]{1,0:T(8,128)(2,1)S(1)} collective-permute-done((bf16[512,128]{1,0:T(8,128)(2,1)S(1)}, bf16[512,128]{1,0:T(8,128)(2,1)S(1)}, u32[]{:S(2)}, u32[]{:S(2)}) %collective-permute-start.24) | collective-permute-done | bytes 131104 | tf_op jit(solution)/shard_map/ppermute | solution.py:435
  121.4 2.5 %collective-permute-done.25.t3 = bf16[512,128]{1,0:T(8,128)(2,1)S(1)} collective-permute-done((bf16[512,128]{1,0:T(8,128)(2,1)S(1)}, bf16[512,128]{1,0:T(8,128)(2,1)S(1)}, u32[]{:S(2)}, u32[]{:S(2)}) %collective-permute-start.25) | collective-permute-done | bytes 131104 | tf_op jit(solution)/shard_map/ppermute | solution.py:435
  124.0 1.9 %collective-permute-start.27 = (bf16[80,512]{1,0:T(8,128)(2,1)S(1)}, bf16[80,512]{1,0:T(8,128)(2,1)S(1)}, u32[]{:S(2)}, u32[]{:S(2)}) collective-permute-start(bf16[80,512]{1,0:T(8,128)(2,1)S(1)} %get-tuple-element.68), channel_id=1, source_target_pairs={{0,16},{16,0},{1,17},{17,1},{2,18},{18,2},{3,19},{19,3},{4,20},{20... | collective-permute-start | bytes 245768 | tf_op jit(solution)/shard_map/ppermute | solution.py:452
  125.9 1.8 %collective-permute-done.27 = bf16[80,512]{1,0:T(8,128)(2,1)S(1)} collective-permute-done((bf16[80,512]{1,0:T(8,128)(2,1)S(1)}, bf16[80,512]{1,0:T(8,128)(2,1)S(1)}, u32[]{:S(2)}, u32[]{:S(2)}) %collective-permute-start.27) | collective-permute-done | bytes 81952 | tf_op jit(solution)/shard_map/ppermute | solution.py:452
  127.8 1.1 collective-permute-start.28
  128.8 4.8 %collective-permute-start.26 = (bf16[512,128]{1,0:T(8,128)(2,1)S(1)}, bf16[512,128]{1,0:T(8,128)(2,1)S(1)}, u32[]{:S(2)}, u32[]{:S(2)}) collective-permute-start(bf16[512,128]{1,0:T(8,128)(2,1)S(1)} %get-tuple-element.67), channel_id=1, source_target_pairs={{0,0},{4,64},{8,32},{12,96},{32,8},{36,72},{40,40},{44,104},{64,4}... | collective-permute-start | bytes 393224 | tf_op jit(solution)/shard_map/ppermute | solution.py:451
  133.8 7.2 %collective-permute-done.26._ = bf16[512,128]{1,0:T(8,128)(2,1)S(1)} collective-permute-done((bf16[512,128]{1,0:T(8,128)(2,1)S(1)}, bf16[512,128]{1,0:T(8,128)(2,1)S(1)}, u32[]{:S(2)}, u32[]{:S(2)}) %collective-permute-start.26) | collective-permute-done | bytes 131104 | tf_op jit(solution)/shard_map/ppermute | solution.py:451
  141.9 4.0 %collective-permute-start.31 = (bf16[80,512]{1,0:T(8,128)(2,1)S(1)}, bf16[80,512]{1,0:T(8,128)(2,1)S(1)}, u32[]{:S(2)}, u32[]{:S(2)}) collective-permute-start(bf16[80,512]{1,0:T(8,128)(2,1)S(1)} %shard_map.103.p0), channel_id=1, source_target_pairs={{0,128},{8,136},{128,0},{136,8},{1,129},{9,137},{129,1},{137,9},{2... | collective-permute-start | bytes 245768 | tf_op jit(solution)/shard_map/ppermute | solution.py:458
  146.1 1.7 %collective-permute-done.31.p2 = bf16[80,512]{1,0:T(8,128)(2,1)S(1)} collective-permute-done((bf16[80,512]{1,0:T(8,128)(2,1)S(1)}, bf16[80,512]{1,0:T(8,128)(2,1)S(1)}, u32[]{:S(2)}, u32[]{:S(2)}) %collective-permute-start.31) | collective-permute-done | bytes 81952 | tf_op jit(solution)/shard_map/ppermute | solution.py:458
  147.8 1.8 %collective-permute-done.30.p1 = bf16[80,512]{1,0:T(8,128)(2,1)S(1)} collective-permute-done((bf16[80,512]{1,0:T(8,128)(2,1)S(1)}, bf16[80,512]{1,0:T(8,128)(2,1)S(1)}, u32[]{:S(2)}, u32[]{:S(2)}) %collective-permute-start.30) | collective-permute-done | bytes 81952 | tf_op jit(solution)/shard_map/ppermute | solution.py:458
  150.1 3.9 %collective-permute-start.33 = (bf16[320,512]{1,0:T(8,128)(2,1)S(1)}, bf16[320,512]{1,0:T(8,128)(2,1)S(1)}, u32[]{:S(2)}, u32[]{:S(2)}) collective-permute-start(bf16[320,512]{1,0:T(8,128)(2,1)S(1)} %shard_map.104.mine), channel_id=1, source_target_pairs={{0,4},{4,0},{1,5},{5,1},{2,6},{6,2},{3,7},{7,3},{8,12},{12,8},{9,1... | collective-permute-start | bytes 983048 | tf_op jit(solution)/shard_map/ppermute | solution.py:460
  154.0 1.3 collective-permute-done.33.other
  155.3 1.8 %shard_map.105 = (f32[512,512]{1,0:T(8,128)}, f32[128,512]{1,0:T(8,128)}) custom-call(s32[8]{0:T(128)S(1)} %concatenate.3.meta_ref, bf16[320,512]{1,0:T(8,128)(2,1)S(1)} %shard_map.104.mine, bf16[320,512]{1,0:T(8,128)(2,1)S(1)} %collective-permute-done.33.other), custom_call_target="tpu_custom_call" | custom-call | bytes 1966112 | tf_op jit(solution)/shard_map/pallas_call | solution.py:66
  (55 shorter events, 6.6 us)
Async XLA Ops:
  0.6 0.7 copy-start.4
  1.3 1.0 copy-start.2
  2.4 10.4 %copy-start = (bf16[1,512,512]{2,1,0:T(8,128)(2,1)S(1)}, bf16[1,512,512]{2,1,0:T(8,128)(2,1)}, u32[]{:S(2)}) copy-start(bf16[1,512,512]{2,1,0:T(8,128)(2,1)} %param.8) | copy-start | bytes 1572868
  2.4 10.4 %copy-start.3 = (bf16[128,512]{1,0:T(8,128)(2,1)S(1)}, bf16[128,512]{1,0:T(8,128)(2,1)}, u32[]{:S(2)}) copy-start(bf16[128,512]{1,0:T(8,128)(2,1)} %wout_ref.1) | copy-start | bytes 393220
  2.4 20.9 %copy-start.1 = (bf16[512,512]{1,0:T(8,128)(2,1)S(1)}, bf16[512,512]{1,0:T(8,128)(2,1)}, u32[]{:S(2)}) copy-start(bf16[512,512]{1,0:T(8,128)(2,1)} %w.1) | copy-start | bytes 1572868
  2.4 20.9 %collective-permute-start = (bf16[528,512]{1,0:T(8,128)(2,1)S(1)}, bf16[528,512]{1,0:T(8,128)(2,1)S(1)}, u32[]{:S(2)}, u32[]{:S(2)}) collective-permute-start(bf16[528,512]{1,0:T(8,128)(2,1)S(1)} %shard_map.94), channel_id=1, source_target_pairs={{0,0},{4,64},{8,32},{12,96},{32,8},{36,72},{40,40},{44,104},{64,4}... | collective-permute-start | bytes 1622024 | tf_op jit(solution)/shard_map/ppermute | solution.py:346
  12.8 10.5 %copy-start.5 = (f32[1,128]{1,0:T(1,128)S(1)}, f32[1,128]{1,0:T(1,128)}, u32[]{:S(2)}) copy-start(f32[1,128]{1,0:T(1,128)} %table_ref.1) | copy-start | bytes 1540
  24.7 22.2 %collective-permute-start.4 = (bf16[512,256]{1,0:T(8,128)(2,1)}, bf16[512,256]{1,0:T(8,128)(2,1)}, u32[]{:S(2)}, u32[]{:S(2)}) collective-permute-start(bf16[512,256]{1,0:T(8,128)(2,1)} %get-tuple-element.38.q0), channel_id=1, source_target_pairs={{0,16},{16,0},{1,17},{17,1},{2,18},{18,2},{3,19},{19,3},{4,20},{20... | collective-permute-start | bytes 786440 | tf_op jit(solution)/shard_map/ppermute | solution.py:370
  25.4 16.4 %collective-permute-start.7 = (bf16[512,128]{1,0:T(8,128)(2,1)S(1)}, bf16[512,128]{1,0:T(8,128)(2,1)S(1)}, u32[]{:S(2)}, u32[]{:S(2)}) collective-permute-start(bf16[512,128]{1,0:T(8,128)(2,1)S(1)} %get-tuple-element.39), channel_id=1, source_target_pairs={{0,0},{4,64},{8,32},{12,96},{32,8},{36,72},{40,40},{44,104},{64,4}... | collective-permute-start | bytes 393224 | tf_op jit(solution)/shard_map/ppermute | solution.py:369
  30.4 19.1 %collective-permute-start.5 = (bf16[512,256]{1,0:T(8,128)(2,1)}, bf16[512,256]{1,0:T(8,128)(2,1)}, u32[]{:S(2)}, u32[]{:S(2)}) collective-permute-start(bf16[512,256]{1,0:T(8,128)(2,1)} %get-tuple-element.38.q0), channel_id=1, source_target_pairs={{0,4},{4,0},{1,5},{5,1},{2,6},{6,2},{3,7},{7,3},{8,12},{12,8},{9,1... | collective-permute-start | bytes 786440 | tf_op jit(solution)/shard_map/ppermute | solution.py:371
  30.5 23.2 %collective-permute-start.3 = (bf16[528,256]{1,0:T(8,128)(2,1)S(1)}, bf16[528,256]{1,0:T(8,128)(2,1)}, u32[]{:S(2)}, u32[]{:S(2)}) collective-permute-start(bf16[528,256]{1,0:T(8,128)(2,1)S(1)} %get-tuple-element.37.kv0), channel_id=1, source_target_pairs={{0,136},{8,128},{128,8},{136,0},{1,137},{9,129},{129,9},{137,1},{2... | collective-permute-start | bytes 811016 | tf_op jit(solution)/shard_map/ppermute | solution.py:367
  41.6 12.1 %collective-permute-start.2 = (bf16[528,256]{1,0:T(8,128)(2,1)S(1)}, bf16[528,256]{1,0:T(8,128)(2,1)}, u32[]{:S(2)}, u32[]{:S(2)}) collective-permute-start(bf16[528,256]{1,0:T(8,128)(2,1)S(1)} %get-tuple-element.37.kv0), channel_id=1, source_target_pairs={{0,128},{8,136},{128,0},{136,8},{1,129},{9,137},{129,1},{137,9},{2... | collective-permute-start | bytes 811016 | tf_op jit(solution)/shard_map/ppermute | solution.py:367
  41.9 12.7 %collective-permute-start.1 = (bf16[528,256]{1,0:T(8,128)(2,1)S(1)}, bf16[528,256]{1,0:T(8,128)(2,1)}, u32[]{:S(2)}, u32[]{:S(2)}) collective-permute-start(bf16[528,256]{1,0:T(8,128)(2,1)S(1)} %get-tuple-element.37.kv0), channel_id=1, source_target_pairs={{0,8},{8,0},{128,136},{136,128},{1,9},{9,1},{129,137},{137,129},{2... | collective-permute-start | bytes 811016 | tf_op jit(solution)/shard_map/ppermute | solution.py:367
  46.9 7.7 %collective-permute-start.6 = (bf16[512,256]{1,0:T(8,128)(2,1)}, bf16[512,256]{1,0:T(8,128)(2,1)}, u32[]{:S(2)}, u32[]{:S(2)}) collective-permute-start(bf16[512,256]{1,0:T(8,128)(2,1)} %collective-permute-done.4.q1), channel_id=1, source_target_pairs={{0,4},{4,0},{1,5},{5,1},{2,6},{6,2},{3,7},{7,3},{8,12},{12,8},{9,1... | collective-permute-start | bytes 786440 | tf_op jit(solution)/shard_map/ppermute | solution.py:371
  61.7 2.5 %collective-permute-start.8 = (bf16[1024,128]{1,0:T(8,128)(2,1)S(1)}, bf16[1024,128]{1,0:T(8,128)(2,1)S(1)}, u32[]{:S(2)}, u32[]{:S(2)}) collective-permute-start(bf16[1024,128]{1,0:T(8,128)(2,1)S(1)} %get-tuple-element.45), channel_id=1, source_target_pairs={{0,4},{4,0},{1,5},{5,1},{2,6},{6,2},{3,7},{7,3},{8,12},{12,8},{9,1... | collective-permute-start | bytes 786440 | tf_op jit(solution)/shard_map/ppermute | solution.py:389
  64.3 5.1 %collective-permute-start.9 = (bf16[512,128]{1,0:T(8,128)(2,1)S(1)}, bf16[512,128]{1,0:T(8,128)(2,1)S(1)}, u32[]{:S(2)}, u32[]{:S(2)}) collective-permute-start(bf16[512,128]{1,0:T(8,128)(2,1)S(1)} %add_convert_fusion.1), channel_id=1, source_target_pairs={{0,16},{16,0},{1,17},{17,1},{2,18},{18,2},{3,19},{19,3},{4,20},{20... | collective-permute-start | bytes 393224 | tf_op jit(solution)/shard_map/ppermute | solution.py:391
  70.3 3.9 %collective-permute-start.10 = (bf16[512,128]{1,0:T(8,128)(2,1)S(1)}, bf16[512,128]{1,0:T(8,128)(2,1)S(1)}, u32[]{:S(2)}, u32[]{:S(2)}) collective-permute-start(bf16[512,128]{1,0:T(8,128)(2,1)S(1)} %get-tuple-element.48.g0), channel_id=1, source_target_pairs={{0,16},{16,0},{1,17},{17,1},{2,18},{18,2},{3,19},{19,3},{4,20},{20... | collective-permute-start | bytes 393224 | tf_op jit(solution)/shard_map/ppermute | solution.py:399
  71.7 4.7 %collective-permute-start.11 = (bf16[512,128]{1,0:T(8,128)(2,1)S(1)}, bf16[512,128]{1,0:T(8,128)(2,1)S(1)}, u32[]{:S(2)}, u32[]{:S(2)}) collective-permute-start(bf16[512,128]{1,0:T(8,128)(2,1)S(1)} %get-tuple-element.48.g0), channel_id=1, source_target_pairs={{0,4},{4,0},{1,5},{5,1},{2,6},{6,2},{3,7},{7,3},{8,12},{12,8},{9,1... | collective-permute-start | bytes 393224 | tf_op jit(solution)/shard_map/ppermute | solution.py:400
  74.2 3.2 %collective-permute-start.12 = (bf16[512,128]{1,0:T(8,128)(2,1)S(1)}, bf16[512,128]{1,0:T(8,128)(2,1)S(1)}, u32[]{:S(2)}, u32[]{:S(2)}) collective-permute-start(bf16[512,128]{1,0:T(8,128)(2,1)S(1)} %collective-permute-done.10.g1), channel_id=1, source_target_pairs={{0,4},{4,0},{1,5},{5,1},{2,6},{6,2},{3,7},{7,3},{8,12},{12,8},{9,1... | collective-permute-start | bytes 393224 | tf_op jit(solution)/shard_map/ppermute | solution.py:400
  84.5 9.9 %collective-permute-start.16 = (bf16[1024,128]{1,0:T(8,128)(2,1)S(1)}, bf16[1024,128]{1,0:T(8,128)(2,1)S(1)}, u32[]{:S(2)}, u32[]{:S(2)}) collective-permute-start(bf16[1024,128]{1,0:T(8,128)(2,1)S(1)} %get-tuple-element.54), channel_id=1, source_target_pairs={{0,4},{4,0},{1,5},{5,1},{2,6},{6,2},{3,7},{7,3},{8,12},{12,8},{9,1... | collective-permute-start | bytes 786440 | tf_op jit(solution)/shard_map/ppermute | solution.py:422
  85.0 11.2 %collective-permute-start.18 = (bf16[512,128]{1,0:T(8,128)(2,1)S(1)}, bf16[512,128]{1,0:T(8,128)(2,1)S(1)}, u32[]{:S(2)}, u32[]{:S(2)}) collective-permute-start(bf16[512,128]{1,0:T(8,128)(2,1)S(1)} %get-tuple-element.56), channel_id=1, source_target_pairs={{0,0},{4,64},{8,32},{12,96},{32,8},{36,72},{40,40},{44,104},{64,4}... | collective-permute-start | bytes 393224 | tf_op jit(solution)/shard_map/ppermute | solution.py:401
  86.9 13.4 %collective-permute-start.13 = (bf16[512,256]{1,0:T(8,128)(2,1)S(1)}, bf16[512,256]{1,0:T(8,128)(2,1)S(1)}, u32[]{:S(2)}, u32[]{:S(2)}) collective-permute-start(bf16[512,256]{1,0:T(8,128)(2,1)S(1)} %get-tuple-element.50), channel_id=1, source_target_pairs={{0,8},{8,0},{128,136},{136,128},{1,9},{9,1},{129,137},{137,129},{2... | collective-permute-start | bytes 786440 | tf_op jit(solution)/shard_map/ppermute | solution.py:419
  91.9 14.0 %collective-permute-start.14 = (bf16[512,256]{1,0:T(8,128)(2,1)S(1)}, bf16[512,256]{1,0:T(8,128)(2,1)S(1)}, u32[]{:S(2)}, u32[]{:S(2)}) collective-permute-start(bf16[512,256]{1,0:T(8,128)(2,1)S(1)} %get-tuple-element.51), channel_id=1, source_target_pairs={{0,128},{8,136},{128,0},{136,8},{1,129},{9,137},{129,1},{137,9},{2... | collective-permute-start | bytes 786440 | tf_op jit(solution)/shard_map/ppermute | solution.py:421
  92.5 13.4 %collective-permute-start.15 = (bf16[512,256]{1,0:T(8,128)(2,1)S(1)}, bf16[512,256]{1,0:T(8,128)(2,1)S(1)}, u32[]{:S(2)}, u32[]{:S(2)}) collective-permute-start(bf16[512,256]{1,0:T(8,128)(2,1)S(1)} %get-tuple-element.52), channel_id=1, source_target_pairs={{0,136},{8,128},{128,8},{136,0},{1,137},{9,129},{129,9},{137,1},{2... | collective-permute-start | bytes 786440 | tf_op jit(solution)/shard_map/ppermute | solution.py:420
  94.5 11.5 %collective-permute-start.17 = (bf16[512,128]{1,0:T(8,128)(2,1)S(1)}, bf16[512,128]{1,0:T(8,128)(2,1)S(1)}, u32[]{:S(2)}, u32[]{:S(2)}) collective-permute-start(bf16[512,128]{1,0:T(8,128)(2,1)S(1)} %add_convert_fusion), channel_id=1, source_target_pairs={{0,16},{16,0},{1,17},{17,1},{2,18},{18,2},{3,19},{19,3},{4,20},{20... | collective-permute-start | bytes 393224 | tf_op jit(solution)/shard_map/ppermute | solution.py:424
  107.6 7.3 %collective-permute-start.19 = (bf16[320,512]{1,0:T(8,128)(2,1)S(1)}, bf16[320,512]{1,0:T(8,128)(2,1)S(1)}, u32[]{:S(2)}, u32[]{:S(2)}) collective-permute-start(bf16[320,512]{1,0:T(8,128)(2,1)S(1)} %get-tuple-element.58), channel_id=1, source_target_pairs={{0,4},{4,0},{1,5},{5,1},{2,6},{6,2},{3,7},{7,3},{8,12},{12,8},{9,1... | collective-permute-start | bytes 983048 | tf_op jit(solution)/shard_map/ppermute | solution.py:433
  111.0 6.6 %collective-permute-start.23 = (bf16[512,128]{1,0:T(8,128)(2,1)S(1)}, bf16[512,128]{1,0:T(8,128)(2,1)S(1)}, u32[]{:S(2)}, u32[]{:S(2)}) collective-permute-start(bf16[512,128]{1,0:T(8,128)(2,1)S(1)} %get-tuple-element.64), channel_id=1, source_target_pairs={{0,1},{1,0},{2,3},{3,2},{4,5},{5,4},{6,7},{7,6},{8,9},{9,8},{10,11... | collective-permute-start | bytes 393224 | tf_op jit(solution)/shard_map/ppermute | solution.py:435
  112.3 9.0 %collective-permute-start.24 = (bf16[512,128]{1,0:T(8,128)(2,1)S(1)}, bf16[512,128]{1,0:T(8,128)(2,1)S(1)}, u32[]{:S(2)}, u32[]{:S(2)}) collective-permute-start(bf16[512,128]{1,0:T(8,128)(2,1)S(1)} %get-tuple-element.65), channel_id=1, source_target_pairs={{0,2},{1,3},{2,0},{3,1},{4,6},{5,7},{6,4},{7,5},{8,10},{9,11},{10,... | collective-permute-start | bytes 393224 | tf_op jit(solution)/shard_map/ppermute | solution.py:435
  115.0 9.0 %collective-permute-start.25 = (bf16[512,128]{1,0:T(8,128)(2,1)S(1)}, bf16[512,128]{1,0:T(8,128)(2,1)S(1)}, u32[]{:S(2)}, u32[]{:S(2)}) collective-permute-start(bf16[512,128]{1,0:T(8,128)(2,1)S(1)} %get-tuple-element.66), channel_id=1, source_target_pairs={{0,3},{1,2},{2,1},{3,0},{4,7},{5,6},{6,5},{7,4},{8,11},{9,10},{10,... | collective-permute-start | bytes 393224 | tf_op jit(solution)/shard_map/ppermute | solution.py:435
  115.6 8.3 %collective-permute-start.20 = (bf16[80,512]{1,0:T(8,128)(2,1)S(1)}, bf16[80,512]{1,0:T(8,128)(2,1)S(1)}, u32[]{:S(2)}, u32[]{:S(2)}) collective-permute-start(bf16[80,512]{1,0:T(8,128)(2,1)S(1)} %get-tuple-element.60), channel_id=1, source_target_pairs={{0,8},{8,0},{128,136},{136,128},{1,9},{9,1},{129,137},{137,129},{2... | collective-permute-start | bytes 245768 | tf_op jit(solution)/shard_map/ppermute | solution.py:444
  115.7 8.2 %collective-permute-start.21 = (bf16[80,512]{1,0:T(8,128)(2,1)S(1)}, bf16[80,512]{1,0:T(8,128)(2,1)S(1)}, u32[]{:S(2)}, u32[]{:S(2)}) collective-permute-start(bf16[80,512]{1,0:T(8,128)(2,1)S(1)} %get-tuple-element.61), channel_id=1, source_target_pairs={{0,128},{8,136},{128,0},{136,8},{1,129},{9,137},{129,1},{137,9},{2... | collective-permute-start | bytes 245768 | tf_op jit(solution)/shard_map/ppermute | solution.py:444
  117.6 6.3 %collective-permute-start.22 = (bf16[80,512]{1,0:T(8,128)(2,1)S(1)}, bf16[80,512]{1,0:T(8,128)(2,1)S(1)}, u32[]{:S(2)}, u32[]{:S(2)}) collective-permute-start(bf16[80,512]{1,0:T(8,128)(2,1)S(1)} %get-tuple-element.62), channel_id=1, source_target_pairs={{0,136},{8,128},{128,8},{136,0},{1,137},{9,129},{129,9},{137,1},{2... | collective-permute-start | bytes 245768 | tf_op jit(solution)/shard_map/ppermute | solution.py:444
  124.0 3.7 %collective-permute-start.27 = (bf16[80,512]{1,0:T(8,128)(2,1)S(1)}, bf16[80,512]{1,0:T(8,128)(2,1)S(1)}, u32[]{:S(2)}, u32[]{:S(2)}) collective-permute-start(bf16[80,512]{1,0:T(8,128)(2,1)S(1)} %get-tuple-element.68), channel_id=1, source_target_pairs={{0,16},{16,0},{1,17},{17,1},{2,18},{18,2},{3,19},{19,3},{4,20},{20... | collective-permute-start | bytes 245768 | tf_op jit(solution)/shard_map/ppermute | solution.py:452
  127.8 5.9 %collective-permute-start.28 = (bf16[80,512]{1,0:T(8,128)(2,1)S(1)}, bf16[80,512]{1,0:T(8,128)(2,1)S(1)}, u32[]{:S(2)}, u32[]{:S(2)}) collective-permute-start(bf16[80,512]{1,0:T(8,128)(2,1)S(1)} %add_convert_fusion.3), channel_id=1, source_target_pairs={{0,32},{32,0},{1,33},{33,1},{2,34},{34,2},{3,35},{35,3},{4,36},{36... | collective-permute-start | bytes 245768 | tf_op jit(solution)/shard_map/ppermute | solution.py:454
  128.8 12.2 %collective-permute-start.26 = (bf16[512,128]{1,0:T(8,128)(2,1)S(1)}, bf16[512,128]{1,0:T(8,128)(2,1)S(1)}, u32[]{:S(2)}, u32[]{:S(2)}) collective-permute-start(bf16[512,128]{1,0:T(8,128)(2,1)S(1)} %get-tuple-element.67), channel_id=1, source_target_pairs={{0,0},{4,64},{8,32},{12,96},{32,8},{36,72},{40,40},{44,104},{64,4}... | collective-permute-start | bytes 393224 | tf_op jit(solution)/shard_map/ppermute | solution.py:451
  133.7 7.8 %collective-permute-start.29 = (bf16[80,512]{1,0:T(8,128)(2,1)S(1)}, bf16[80,512]{1,0:T(8,128)(2,1)S(1)}, u32[]{:S(2)}, u32[]{:S(2)}) collective-permute-start(bf16[80,512]{1,0:T(8,128)(2,1)S(1)} %add_convert_fusion.2.a_ref), channel_id=1, source_target_pairs={{0,64},{64,0},{1,65},{65,1},{2,66},{66,2},{3,67},{67,3},{4,68},{68... | collective-permute-start | bytes 245768 | tf_op jit(solution)/shard_map/ppermute | solution.py:456
  141.5 4.6 %collective-permute-start.32 = (bf16[80,512]{1,0:T(8,128)(2,1)S(1)}, bf16[80,512]{1,0:T(8,128)(2,1)S(1)}, u32[]{:S(2)}, u32[]{:S(2)}) collective-permute-start(bf16[80,512]{1,0:T(8,128)(2,1)S(1)} %shard_map.103.p0), channel_id=1, source_target_pairs={{0,136},{8,128},{128,8},{136,0},{1,137},{9,129},{129,9},{137,1},{2... | collective-permute-start | bytes 245768 | tf_op jit(solution)/shard_map/ppermute | solution.py:458
  141.9 5.8 %collective-permute-start.31 = (bf16[80,512]{1,0:T(8,128)(2,1)S(1)}, bf16[80,512]{1,0:T(8,128)(2,1)S(1)}, u32[]{:S(2)}, u32[]{:S(2)}) collective-permute-start(bf16[80,512]{1,0:T(8,128)(2,1)S(1)} %shard_map.103.p0), channel_id=1, source_target_pairs={{0,128},{8,136},{128,0},{136,8},{1,129},{9,137},{129,1},{137,9},{2... | collective-permute-start | bytes 245768 | tf_op jit(solution)/shard_map/ppermute | solution.py:458
  146.0 3.6 %collective-permute-start.30 = (bf16[80,512]{1,0:T(8,128)(2,1)S(1)}, bf16[80,512]{1,0:T(8,128)(2,1)S(1)}, u32[]{:S(2)}, u32[]{:S(2)}) collective-permute-start(bf16[80,512]{1,0:T(8,128)(2,1)S(1)} %shard_map.103.p0), channel_id=1, source_target_pairs={{0,8},{8,0},{128,136},{136,128},{1,9},{9,1},{129,137},{137,129},{2... | collective-permute-start | bytes 245768 | tf_op jit(solution)/shard_map/ppermute | solution.py:458
  150.1 5.2 %collective-permute-start.33 = (bf16[320,512]{1,0:T(8,128)(2,1)S(1)}, bf16[320,512]{1,0:T(8,128)(2,1)S(1)}, u32[]{:S(2)}, u32[]{:S(2)}) collective-permute-start(bf16[320,512]{1,0:T(8,128)(2,1)S(1)} %shard_map.104.mine), channel_id=1, source_target_pairs={{0,4},{4,0},{1,5},{5,1},{2,6},{6,2},{3,7},{7,3},{8,12},{12,8},{9,1... | collective-permute-start | bytes 983048 | tf_op jit(solution)/shard_map/ppermute | solution.py:460

commit v2 on v1

--- a/solution.py
+++ b/solution.py
@@ -22,17 +22,18 @@
 F32 = jnp.float32
 FACTOR = 1.0 / math.sqrt(DH)
 PIECE = 80
-STEP = 2
 LIST = 128
 
-TRANSPOSED = ("z2", "z1", "xl", "core")
-SWAP = [
-    (8 * a + 4 * b + 2 * c + d, 8 * d + 4 * c + 2 * b + a)
+MOVED = ("z2", "z1", "z0", "xl", "core")
+AWAY = [
+    (16 * a + 8 * b + 4 * c + 2 * d + e, 16 * e + 8 * d + 4 * c + 2 * (b ^ c) + (a ^ b))
     for a in (0, 1)
     for b in (0, 1)
     for c in (0, 1)
     for d in (0, 1)
+    for e in (0, 1)
 ]
+HOME = [(b, a) for a, b in AWAY]
 FLIP = [(0, 1), (1, 0)]
 
 
@@ -40,6 +41,11 @@
     return [(i, i ^ rel) for i in range(4)]
 
 
+def row_index(x, core, z):
+    middle = (x % 2) ^ z
+    return 8 * (x // 2) + 4 * (core ^ middle) + 2 * middle + z
+
+
 def dot(a, b, dims=((1,), (0,))):
     return lax.dot_general(a, b, (dims, ((), ())), preferred_element_type=F32)
 
@@ -48,9 +54,10 @@
 TN = ((0,), (0,))
 
 
-def call(kernel, outs, args, scratch=(), flops=0, unread=0, passed=0):
+def call(kernel, outs, args, scratch=(), flops=0, unread=0, passed=0, held=0, limit=40):
     specs = [pl.BlockSpec(memory_space=pltpu.VMEM)] * (len(args) - unread - passed)
     specs += [pl.BlockSpec(memory_space=pl.ANY)] * (unread + passed)
+    specs[:held] = [pl.BlockSpec(memory_space=pltpu.HBM)] * held
     for n, a in enumerate(args):
         if a.ndim == 1:
             specs[n] = pl.BlockSpec(memory_space=pltpu.SMEM)
@@ -70,25 +77,44 @@
         out_specs=out_specs,
         input_output_aliases={len(args) - passed + n: before + n for n in range(passed)},
         scratch_shapes=list(scratch),
-        compiler_params=pltpu.CompilerParams(vmem_limit_bytes=40 * 1024 * 1024),
+        compiler_params=pltpu.CompilerParams(vmem_limit_bytes=limit * 1024 * 1024),
         cost_estimate=pl.CostEstimate(flops=flops, bytes_accessed=moved, transcendentals=0),
     )(*args)
 
 
-def prepare_kernel(x_ref, times_ref, lengths_ref, out_ref):
-    out_ref[0:ROWS, :] = x_ref[...]
+def prepare_kernel(
+    x_hbm, times_hbm, lengths_hbm, upstream_hbm, out_ref, times_ref, lengths_ref, sems
+):
+    quarter = pl.ds(pl.multiple_of(lax.axis_index("y") * DH, DH), DH)
+    pairs = (
+        (times_hbm, times_ref),
+        (lengths_hbm, lengths_ref),
+        (x_hbm.at[quarter, :], out_ref.at[0:DH, :]),
+        (upstream_hbm.at[quarter, :], out_ref.at[DH + 16 :, :]),
+    )
+    copies = [pltpu.make_async_copy(a, b, sems.at[n]) for n, (a, b) in enumerate(pairs)]
+    for copy in copies:
+        copy.start()
+    for copy in copies[:2]:
+        copy.wait()
     row = lax.broadcasted_iota(jnp.int32, (16, WIDTH), 0)
-    lengths = jnp.concatenate([lengths_ref[...]] * (WIDTH // DH), 1).astype(F32)
+    column = lax.broadcasted_iota(jnp.int32, (16, WIDTH), 1)
+    lengths = lengths_ref[...].astype(F32)
+    lengths = jnp.where(column == 0, lengths[:, 0:1], lengths[:, 1:2])
     times = times_ref[...].astype(F32)
-    out_ref[ROWS:, :] = jnp.where(row == 0, times, jnp.where(row == 1, lengths, 0.0)).astype(BF)
-
-
-def gated_kernel(upstream_ref, wout_ref, out_ref):
-    out_ref[...] = dot(upstream_ref[...], wout_ref[...], NT).astype(BF)
-
-
-def project_kernel(xa_ref, w_ref, table_ref, _, kv_ref, q_ref, gate_ref, slope_ref, __):
-    projected = dot(xa_ref[0:ROWS, :], w_ref[...])
+    extra = jnp.where(row == 0, times, jnp.where(row == 1, lengths, 0.0))
+    out_ref[DH : DH + 16, :] = extra.astype(BF)
+    for copy in copies[2:]:
+        copy.wait()
+
+
+def project_kernel(
+    _, xa_ref, x1, x2, x3, w_ref, table_ref, kv_ref, q_ref, gate_ref, slope_ref, x_ref
+):
+    y = lax.axis_index("y")
+    for rel, piece in enumerate((xa_ref, x1, x2, x3)):
+        x_ref[pl.ds(pl.multiple_of((y ^ rel) * DH, DH), DH), :] = piece[0:DH, :]
+    projected = dot(x_ref[...], w_ref[...])
     sig = 0.5 + 0.5 * jnp.tanh(0.5 * projected)
     act = projected * sig
     slope_ref[...] = sig * (1.0 + projected * (1.0 - sig))
@@ -96,7 +122,7 @@
     kv_ref[0:ROWS, DH : 2 * DH] = act[:, DH : 2 * DH].astype(BF)
     q_ref[:, 0:DH] = (act[:, 2 * DH : 3 * DH] * (0.5 * FACTOR)).astype(BF)
     kv_ref[0:ROWS, 0:DH] = act[:, 3 * DH : 4 * DH].astype(BF)
-    times = xa_ref[ROWS : ROWS + 16, :].astype(F32)[0:1, :]
+    times = xa_ref[DH : DH + 16, :].astype(F32)[0:1, :]
     row = lax.broadcasted_iota(jnp.int32, (16, HALF), 0)
     extra = jnp.where(row == 0, times[:, 0:HALF], jnp.where(row == 1, times[:, HALF:], 0.0))
     kv_ref[ROWS : ROWS + 16, :] = extra.astype(BF)
@@ -117,18 +143,18 @@
 def key_row_of(meta_ref, slot):
     x, core, z = (meta_ref[n] for n in range(2, 5))
     owner = x ^ (slot // 2)
-    index = 8 * (owner // 2) + 2 * (owner % 2) + 4 * core + z
+    index = row_index(owner, core, z)
     return jnp.where(slot % 2 == 0, index, 31 - index) * HALF
 
 
 def query_row_of(meta_ref, j):
     x, core, z = (meta_ref[n] for n in range(2, 5))
     rel = j % GROUP
-    index = 8 * (x // 2) + 2 * (x % 2) + 4 * (core ^ (rel // 2)) + (z ^ (rel % 2))
+    index = row_index(x, core ^ (rel // 2), z ^ (rel % 2))
     return jnp.where(j < GROUP, index, 31 - index) * HALF
 
 
-def list_pairs(meta_ref, list_ref):
+def list_kernel(meta_ref, list_ref):
     first_end, second_end = meta_ref[0], meta_ref[1]
 
     def queries(j, count):
@@ -144,27 +170,32 @@
         return lax.fori_loop(0, 2 * GROUP, keys, count, unroll=True)
 
     count = lax.fori_loop(0, 2 * GROUP, queries, jnp.int32(0))
-    for more in range(STEP):
-        list_ref[count + more] = -1
     list_ref[LIST - 1] = count
 
 
-def sweep(meta_ref, list_ref, one, key_axis):
-    def step(i, carry):
+def sweep(meta_ref, list_ref, one, key_axis, size):
+    def several(first, number):
         done = []
-        for n in range(STEP):
-            item = list_ref[i * STEP + n]
-            live = item >= 0
-            item = jnp.maximum(item, 0)
+        for n in range(number):
+            item = list_ref[first + n]
             j, slot = item // 8, item % 8
-            rows = jnp.where(live, query_row_of(meta_ref, j), -HALF)
-            mask = mask_of(rows, key_row_of(meta_ref, slot), meta_ref[0], meta_ref[1], key_axis)
+            rows, key_rows = query_row_of(meta_ref, j), key_row_of(meta_ref, slot)
+            mask = mask_of(rows, key_rows, meta_ref[0], meta_ref[1], key_axis)
             done.append(one(j, slot, mask))
         for finish in done:
             finish()
+
+    def step(i, carry):
+        several(i * size, size)
         return carry
 
-    lax.fori_loop(0, (list_ref[LIST - 1] + STEP - 1) // STEP, step, 0)
+    def rest(i, carry):
+        several(i, 1)
+        return carry
+
+    count = list_ref[LIST - 1]
+    lax.fori_loop(0, count // size, step, 0)
+    lax.fori_loop(count // size * size, count, rest, 0)
 
 
 def mask_of(query_row, key_row, first_end, second_end, key_axis):
@@ -175,8 +206,8 @@
 
 
 def forward_kernel(
-    meta_ref, kv0, kv1, kv2, kv3, q0, q1, q2, q3, _,
-    keep_ref, send_ref, k_ref, v_ref, q_ref, list_ref, acc,
+    meta_ref, kv0, kv1, kv2, kv3, q0, q1, q2, q3, list_ref,
+    keep_ref, send_ref, k_ref, v_ref, q_ref, acc,
 ):
     bucket = lax.broadcasted_iota(jnp.int32, (NB, HALF), 0).astype(F32)
     for rel, kv in enumerate((kv0, kv1, kv2, kv3)):
@@ -192,8 +223,6 @@
             q_ref[half * GROUP + rel] = q[half * HALF : (half + 1) * HALF, :]
     acc[...] = jnp.zeros_like(acc)
 
-    list_pairs(meta_ref, list_ref)
-
     def one(j, slot, mask):
         scores = dot(q_ref[j], k_ref[slot], NT)
         attend = jnp.where(mask, scores + scores * jnp.tanh(scores), 0.0)
@@ -204,7 +233,7 @@
 
         return finish
 
-    sweep(meta_ref, list_ref, one, 1)
+    sweep(meta_ref, list_ref, one, 1, 4)
     for rel in (0, 1):
         for half in (0, 1):
             rows = slice(rel * ROWS + half * HALF, rel * ROWS + (half + 1) * HALF)
@@ -213,10 +242,16 @@
 
 
 def middle_kernel(
-    meta_ref, keep, got_core, got_z, grad_gated_ref, gate, slope, grad_ref, gate_ref, gated_ref
+    meta_ref, keep, got_core, got_z, up0, up1, up2, up3, wout, gate, slope,
+    grad_ref, gate_ref, gated_ref,
+    grad_gated_ref, gated,
 ):
+    y = meta_ref[5]
+    for rel, up in enumerate((up0, up1, up2, up3)):
+        rows = pl.ds(pl.multiple_of((y ^ rel) * DH, DH), DH)
+        grad_gated_ref[rows, :] = dot(up[DH + 16 :, :], wout[...], NT)
     first_end, second_end, x, core, z = (meta_ref[n] for n in range(5))
-    block = 8 * (x // 2) + 2 * (x % 2) + 4 * core + z
+    block = row_index(x, core, z)
     offset = lax.broadcasted_iota(jnp.int32, (ROWS, 1), 0)
     rows = jnp.where(offset < HALF, block * HALF + offset, (31 - block) * HALF + offset - HALF)
     first = jnp.where(rows < first_end, 0, jnp.where(rows < second_end, first_end, second_end))
@@ -226,8 +261,11 @@
     spread = 1.0 / jnp.sqrt(jnp.mean(attended * attended, axis=-1, keepdims=True) + EPSILON)
     normed = attended * spread
     gate_float = gate[...].astype(F32)
-    gated_ref[...] = (normed * gate_float).astype(BF)
-    grad_gated = grad_gated_ref[...].astype(F32)
+    gated[...] = (normed * gate_float).astype(BF)
+    for rel in range(GROUP):
+        rows = pl.ds(pl.multiple_of((y ^ rel) * DH, DH), DH)
+        gated_ref[rel * DH : (rel + 1) * DH, :] = gated[rows, :]
+    grad_gated = grad_gated_ref[...]
     gate_ref[...] = (grad_gated * normed * slope[:, 0:DH]).astype(BF)
     grad_normed = grad_gated * gate_float
     inner = jnp.mean(grad_normed * normed, axis=-1, keepdims=True)
@@ -267,7 +305,7 @@
 
         return finish
 
-    sweep(meta_ref, list_ref, one, 0)
+    sweep(meta_ref, list_ref, one, 0, 4)
     for rel, out in enumerate((own_ref, s1_ref, s2_ref, s3_ref)):
         for half in (0, 1):
             rows = slice(half * HALF, (half + 1) * HALF)
@@ -280,8 +318,15 @@
             send_ref[rows, :] = (acc_q[half * GROUP + rel + 2].T * FACTOR).astype(BF)
 
 
+def wout_kernel(gated, up0, up1, up2, up3, out_ref):
+    total = dot(gated[0:DH, :], up0[DH + 16 :, :], TN)
+    for rel, up in ((1, up1), (2, up2), (3, up3)):
+        total = total + dot(gated[rel * DH : (rel + 1) * DH, :], up[DH + 16 :, :], TN)
+    out_ref[...] = total
+
+
 def tail_kernel(
-    meta_ref, own, r1, r2, r3, keep, got_core, got_z, grad_gate, slope, w, xa, wout_terms,
+    meta_ref, own, r1, r2, r3, keep, got_core, got_z, grad_gate, slope, w, x_all, wout_terms,
     t0_ref, t1_ref, t2_ref, t3_ref, stay_ref, away_ref,
     grad, full,
 ):
@@ -295,22 +340,22 @@
     for rel, out in enumerate((t0_ref, t1_ref, t2_ref, t3_ref)):
         rows = w[pl.ds(pl.multiple_of((y ^ rel) * DH, DH), DH), :]
         out[...] = dot(grad[...], rows, NT).astype(out.dtype)
-    full[0:WIDTH, :] = dot(xa[0:ROWS, :], grad[...], TN)
+    full[0:WIDTH, :] = dot(x_all[...], grad[...], TN)
     full[WIDTH:, :] = wout_terms[...]
     size = full.shape[0] // 2
     stay_ref[...] = full[pl.ds(pl.multiple_of(core * size, 64), size), :]
     away_ref[...] = full[pl.ds(pl.multiple_of((1 - core) * size, 64), size), :].astype(BF)
 
 
-def gather_kernel(p0, p1, p2, p3, t0, t1, t2, t3, total_ref, grad_ref):
+def sum_kernel(p0, p1, p2, p3, _, __, ___, total_ref, *passed):
     total = p0[...] + p1[...].astype(F32) + p2[...].astype(F32) + p3[...].astype(F32)
     total_ref[...] = total.astype(BF)
+
+
+def both_kernel(a, b, t0, t1, t2, t3, total_ref, grad_ref):
+    total_ref[...] = (a[...].astype(F32) + b[...].astype(F32)).astype(BF)
     grad = t0[...] + t1[...].astype(F32) + t2[...].astype(F32) + t3[...].astype(F32)
     grad_ref[...] = grad.astype(BF)
-
-
-def add_kernel(a_ref, b_ref, _, out_ref):
-    out_ref[...] = (a_ref[...].astype(F32) + b_ref[...].astype(F32)).astype(BF)
 
 
 def split_kernel(meta_ref, stay, got, p0_ref, p1_ref, p2_ref, p3_ref, total):
@@ -321,57 +366,64 @@
         out[...] = total[rows, :].astype(out.dtype)
 
 
-def join_kernel(meta_ref, p0, p1, p2, p3, out_ref):
+def join_kernel(meta_ref, p0, p1, p2, p3, _, out_ref):
     x = meta_ref[2]
     for rel, piece in enumerate((p0, p1, p2, p3)):
         out_ref[pl.ds(pl.multiple_of((x ^ rel) * PIECE, 16), PIECE), :] = piece[...]
 
 
-def final_kernel(scale, meta_ref, mine, other, win_ref, wout_ref, full):
-    core = meta_ref[3]
-    size = full.shape[0] // 2
-    full[pl.ds(pl.multiple_of(core * size, 64), size), :] = mine[...].astype(F32) * scale
-    full[pl.ds(pl.multiple_of((1 - core) * size, 64), size), :] = other[...].astype(F32) * scale
-    win_ref[...] = full[0:WIDTH, :]
-    wout_ref[...] = full[WIDTH:, :]
+def final_kernel(scale, meta_ref, mine, other, grad, win_ref, wout_ref, grad_ref):
+    swapped = meta_ref[3] == 1
+    size = mine.shape[0]
+    low = jnp.where(swapped, other[...].astype(F32), mine[...].astype(F32)) * scale
+    high = jnp.where(swapped, mine[...].astype(F32), other[...].astype(F32)) * scale
+    win_ref[0:size, :] = low
+    win_ref[size:, :] = high[0 : WIDTH - size, :]
+    wout_ref[...] = high[WIDTH - size :, :]
+    grad_ref[0] = grad[...]
 
 
 def body(layer_input, grad_output, weight_in, weight_out, time_table, user_lengths, time_buckets):
-    lengths = jnp.pad(user_lengths, ((0, 0), (0, DH - 3)))
     (xa,) = call(
         prepare_kernel,
-        [((ROWS + 16, WIDTH), BF)],
-        (layer_input[0], time_buckets, lengths),
-    )
-    xa = lax.ppermute(xa, TRANSPOSED, SWAP)
-
+        [((2 * DH + 16, WIDTH), BF)],
+        (layer_input[0], time_buckets, user_lengths, grad_output[0]),
+        held=4,
+        limit=60,
+        scratch=[
+            pltpu.VMEM((1, ROWS), jnp.int32),
+            pltpu.VMEM((1, 3), jnp.int32),
+            pltpu.SemaphoreType.DMA((4,)),
+        ],
+    )
+    xa = lax.ppermute(xa, MOVED, AWAY)
+
+    flip_y = [[(i, i ^ rel) for i in range(4)] for rel in range(4)]
+    x1, x3, x2 = (lax.ppermute(xa, "y", flip_y[rel]) for rel in (1, 3, 2))
     core = lax.axis_index("core")
     x = 2 * lax.axis_index("xh") + lax.axis_index("xl")
     z = lax.axis_index("z0")
-    lengths = PAD_ROWS * xa[ROWS + 1, 0:2].astype(jnp.int32)
+    lengths = PAD_ROWS * xa[DH + 1, 0:2].astype(jnp.int32)
     places = jnp.stack([x, core, z, lax.axis_index("y"), 0 * x, 0 * x])
     meta = jnp.concatenate(
         [lengths[0:1], lengths[0:1] + lengths[1:2], places.astype(jnp.int32)]
     )
 
-    (grad_gated,) = call(
-        gated_kernel, [((ROWS, DH), BF)], (grad_output[0], weight_out)
-    )
-    kv, q, gate, slope, grad_gated = call(
+    (pairs,) = call(list_kernel, [((LIST,), jnp.int32)], (meta,))
+    kv, q, gate, slope, x_all = call(
         project_kernel,
-        [((ROWS + 16, 2 * DH), BF), ((ROWS, 2 * DH), BF), ((ROWS, DH), BF), ((ROWS, WIDTH), F32)],
-        (xa, weight_in, time_table, grad_gated),
-        passed=1,
+        [((ROWS + 16, 2 * DH), BF), ((ROWS, 2 * DH), BF), ((ROWS, DH), BF), ((ROWS, WIDTH), F32)]
+        + [((ROWS, WIDTH), BF)],
+        (pairs, xa, x1, x2, x3, weight_in, time_table),
         flops=2 * ROWS * WIDTH * WIDTH,
     )
     kvs = [kv] + [lax.ppermute(kv, ("xh", "xl"), flip_x(rel)) for rel in (1, 3, 2)]
     kvs = [kvs[0], kvs[1], kvs[3], kvs[2]]
-    grad_gated = lax.ppermute(grad_gated, TRANSPOSED, SWAP)
     q_z = lax.ppermute(q, "z0", FLIP)
     qs = [q, q_z, lax.ppermute(q, "core", FLIP), lax.ppermute(q_z, "core", FLIP)]
 
     blocks = 2 * GROUP
-    keep, send, k_all, v_all, q_all, pairs = call(
+    keep, send, k_all, v_all, q_all = call(
         forward_kernel,
         [
             ((2 * ROWS, DH), F32),
@@ -379,10 +431,8 @@
             ((blocks, HALF, 2 * DH), BF),
             ((blocks, HALF, DH), BF),
             ((blocks, HALF, 2 * DH), BF),
-            ((LIST,), jnp.int32),
         ],
-        (meta, *kvs, *qs, grad_gated),
-        unread=1,
+        (meta, *kvs, *qs, pairs),
         scratch=[pltpu.VMEM((blocks, HALF, DH), F32)],
         flops=20 * 6 * HALF * HALF * DH,
     )
@@ -393,13 +443,12 @@
     grad, grad_gate, gated = call(
         middle_kernel,
         [((ROWS, DH), BF)] * 3,
-        (meta, keep, got_core, got_z, grad_gated, gate, slope),
+        (meta, keep, got_core, got_z, xa, x1, x2, x3, weight_out, gate, slope),
+        scratch=[pltpu.VMEM((ROWS, DH), F32), pltpu.VMEM((ROWS, DH), BF)],
         flops=2 * ROWS * WIDTH * DH,
     )
     grad_z = lax.ppermute(grad, "z0", FLIP)
     grads = [grad, grad_z, lax.ppermute(grad, "core", FLIP), lax.ppermute(grad_z, "core", FLIP)]
-    gated = lax.ppermute(gated, TRANSPOSED, SWAP)
-    wout_terms = dot(gated, grad_output[0], TN)
 
     own, s1, s2, s3, keep, send = call(
         backward_kernel,
@@ -422,18 +471,16 @@
     got_core = lax.ppermute(send, "core", FLIP)
     part = (keep[ROWS:] + got_core[ROWS:].astype(F32)).astype(BF)
     got_z = lax.ppermute(part, "z0", FLIP)
+    (wout_terms,) = call(wout_kernel, [((DH, WIDTH), F32)], (gated, xa, x1, x2, x3))
 
     t0, t1, t2, t3, stay, away = call(
         tail_kernel,
         [((ROWS, DH), F32)] + [((ROWS, DH), BF)] * 3 + [((320, WIDTH), F32), ((320, WIDTH), BF)],
-        (meta, own, r1, r2, r3, keep, got_core, got_z, grad_gate, slope, weight_in, xa, wout_terms),
+        (meta, own, r1, r2, r3, keep, got_core, got_z, grad_gate, slope, weight_in, x_all, wout_terms),
         scratch=[pltpu.VMEM((ROWS, WIDTH), BF), pltpu.VMEM((WIDTH + DH, WIDTH), F32)],
         flops=4 * ROWS * WIDTH * WIDTH,
     )
     got = lax.ppermute(away, "core", FLIP)
-    flip_y = [[(i, i ^ rel) for i in range(4)] for rel in range(4)]
-    u1, u3, u2 = (lax.ppermute(t, "y", flip_y[rel]) for t, rel in ((t1, 1), (t3, 3), (t2, 2)))
-
     p0, p1, p2, p3 = call(
         split_kernel,
         [((PIECE, WIDTH), F32)] + [((PIECE, WIDTH), BF)] * 3,
@@ -443,29 +490,31 @@
     g1, g3, g2 = (
         lax.ppermute(p, ("xh", "xl"), flip_x(rel)) for p, rel in ((p1, 1), (p3, 3), (p2, 2))
     )
-    total, grad_local = call(
-        gather_kernel,
-        [((PIECE, WIDTH), BF), ((ROWS, DH), BF)],
-        (p0, g1, g2, g3, t0, u1, u2, u3),
-    )
-    grad_local = lax.ppermute(grad_local, TRANSPOSED, SWAP)
+    total, t1, t2, t3 = call(
+        sum_kernel, [((PIECE, WIDTH), BF)], (p0, g1, g2, g3, t1, t2, t3), passed=3
+    )
+    u1, u3, u2 = (lax.ppermute(t, "y", flip_y[rel]) for t, rel in ((t1, 1), (t3, 3), (t2, 2)))
     other = lax.ppermute(total, "z0", FLIP)
     total = (total.astype(F32) + other.astype(F32)).astype(BF)
     other = lax.ppermute(total, "z1", FLIP)
+    total, grad_local = call(
+        both_kernel,
+        [((PIECE, WIDTH), BF), ((ROWS, DH), BF)],
+        (total, other, t0, u1, u2, u3),
+    )
+    grad_local = lax.ppermute(grad_local, MOVED, HOME)
+    other = lax.ppermute(total, "z2", FLIP)
     total = (total.astype(F32) + other.astype(F32)).astype(BF)
-    other = lax.ppermute(total, "z2", FLIP)
-    (total,) = call(add_kernel, [((PIECE, WIDTH), BF)], (total, other, grad_local), unread=1)
     h1, h3, h2 = (lax.ppermute(total, ("xh", "xl"), flip_x(rel)) for rel in (1, 3, 2))
-    (mine_half,) = call(join_kernel, [((320, WIDTH), BF)], (meta, total, h1, h2, h3))
+    (mine_half,) = call(join_kernel, [((320, WIDTH), BF)], (meta, total, h1, h2, h3, grad_local), unread=1)
     other_half = lax.ppermute(mine_half, "core", FLIP)
     normalizer = 1.0 / math.sqrt(4 * 16 * ROWS)
-    win, wout = call(
+    win, wout, grad_local = call(
         functools.partial(final_kernel, normalizer),
-        [((WIDTH, WIDTH), F32), ((DH, WIDTH), F32)],
-        (meta, mine_half, other_half),
-        scratch=[pltpu.VMEM((WIDTH + DH, WIDTH), F32)],
-    )
-    return (grad_local[None], win, wout)
+        [((WIDTH, WIDTH), F32), ((DH, WIDTH), F32), ((1, ROWS, DH), BF)],
+        (meta, mine_half, other_half, grad_local),
+    )
+    return (grad_local, win, wout)
 
 
 def solution(mesh):

time: 159 us -> 150 us (0.943)
  starting transfers between devices: 79.7 us -> 67.9 us
  waiting for transfers between devices: 50 us -> 57.6 us
  local copies, waits for them, and re-layouts: 3.71 us -> 1.33 us
    ppermute x3, starting transfers between devices: 16.4 us -> 8.2 us  [body(): lax.ppermute(kv, ('xh', 'xl'), flip_x(rel))]
    ppermute x4 -> x5, waiting for transfers between devices: 17.5 us -> 9.71 us  [the longest x1 6.08 us: body(): xa = lax.ppermute(xa, MOVED, AWAY)]
    ppermute x1, starting transfers between devices: 0.54 us -> 5.58 us  [body(): r2 = lax.ppermute(s2, ('xh', 'xl'), flip_x(2))]
    ppermute x3, waiting for transfers between devices: 5 us -> 9.92 us  [body(): lax.ppermute(kv, ('xh', 'xl'), flip_x(rel))]
    ppermute x1, starting transfers between devices: 5.06 us -> 0.39 us  [body(): r1 = lax.ppermute(s1, ('xh', 'xl'), flip_x(1))]
    ppermute x1, waiting for transfers between devices: 5.62 us -> 10.1 us  [body(): r2 = lax.ppermute(s2, ('xh', 'xl'), flip_x(2))]
    ppermute x1, waiting for transfers between devices: 3.86 us -> 0.01 us  [body(): r1 = lax.ppermute(s1, ('xh', 'xl'), flip_x(1))]
    ppermute x1, starting transfers between devices: 0.68 us -> 4.27 us  [body(): q_z = lax.ppermute(q, 'z0', FLIP)]
  transfers between devices with their start and end apart: 34 -> 35, of which waited for: 18 -> 22; matrix products, arithmetic and copies ran while one was open for 1% -> 1% of each run, Pallas kernels for 1% -> 1%
where the time goes in v2:
time: 150 us
  starting transfers between devices  67.9 us (45%)
  waiting for transfers between devices  57.6 us (38%)
  Pallas kernels  21 us (14%)
  between operations  2.15 us (1%)
    pallas_call x13, Pallas kernels, call(): pl.pallas_call(kernel, out_shape=[jax.ShapeDtypeStruct(s, t) for s, t in...  21 us
    ppermute x1, starting transfers between devices, body(): xa = lax.ppermute(xa, MOVED, AWAY)  10.2 us
    ppermute x1, waiting for transfers between devices, body(): r2 = lax.ppermute(s2, ('xh', 'xl'), flip_x(2))  10.1 us
    ppermute x3, waiting for transfers between devices, body(): lax.ppermute(kv, ('xh', 'xl'), flip_x(rel))  9.92 us
    ppermute x3, starting transfers between devices, body(): lax.ppermute(kv, ('xh', 'xl'), flip_x(rel))  8.2 us
    ppermute x3, waiting for transfers between devices, body(): lax.ppermute(t, 'y', flip_y[rel])  7.54 us
    ppermute x1, waiting for transfers between devices, body(): xa = lax.ppermute(xa, MOVED, AWAY)  6.08 us
    ppermute x1, starting transfers between devices, body(): grad_local = lax.ppermute(grad_local, MOVED, HOME)  5.78 us
  transfers between devices with their start and end apart: 35, of which 22 were waited for; matrix products, arithmetic and copies ran while one was open for 1% of the time, Pallas kernels for 1%

profile of v2, /device:TPU:1, one launch (start us, length us, event | category | flops | bytes accessed | tf_op | source)
XLA Modules:
  0.0 150.2 jit_solution(5768459315557884384)
XLA Ops:
  0.6 1.8 %shard_map.94 = bf16[272,512]{1,0:T(8,128)(2,1)} custom-call(bf16[512,512]{1,0:T(8,128)(2,1)} %bitcast.8, s32[1,512]{1,0:T(1,128)} %times_hbm.1, s32[1,3]{1,0:T(1,128)} %lengths_hbm.1, bf16[512,512]{1,0:T(8,128)(2,1)} %bitcast.9), custom_call_target="tpu_custom_call" | custom-call | bytes 1329164 | tf_op jit(solution)/shard_map/pallas_call | solution.py:73
  2.4 10.2 %collective-permute-start = (bf16[272,512]{1,0:T(8,128)(2,1)}, bf16[272,512]{1,0:T(8,128)(2,1)S(1)}, u32[]{:S(2)}, u32[]{:S(2)}) collective-permute-start(bf16[272,512]{1,0:T(8,128)(2,1)} %shard_map.94), channel_id=1, source_target_pairs={{0,0},{4,64},{8,32},{12,96},{16,24},{20,88},{24,56},{28,120},{32,1... | collective-permute-start | bytes 835592 | tf_op jit(solution)/shard_map/ppermute | solution.py:399
  12.7 6.1 %collective-permute-done.xa_ref.up0 = bf16[272,512]{1,0:T(8,128)(2,1)S(1)} collective-permute-done((bf16[272,512]{1,0:T(8,128)(2,1)}, bf16[272,512]{1,0:T(8,128)(2,1)S(1)}, u32[]{:S(2)}, u32[]{:S(2)}) %collective-permute-start) | collective-permute-done | bytes 278560 | tf_op jit(solution)/shard_map/ppermute | solution.py:399
  18.8 2.7 %collective-permute-start.3 = (bf16[272,512]{1,0:T(8,128)(2,1)S(1)}, bf16[272,512]{1,0:T(8,128)(2,1)S(1)}, u32[]{:S(2)}, u32[]{:S(2)}) collective-permute-start(bf16[272,512]{1,0:T(8,128)(2,1)S(1)} %collective-permute-done.xa_ref.up0), channel_id=1, source_target_pairs={{0,3},{1,2},{2,1},{3,0},{4,7},{5,6},{6,5},{7,4},{8,11},{9,10},{10,... | collective-permute-start | bytes 835592 | tf_op jit(solution)/shard_map/ppermute | solution.py:402
  24.7 1.7 %shard_map.95._.list_ref = s32[128]{0:T(128)S(1)} custom-call(s32[8]{0:T(128)S(1)} %concatenate.3.meta_ref), custom_call_target="tpu_custom_call" | custom-call | bytes 544 | tf_op jit(solution)/shard_map/pallas_call | solution.py:73
  26.4 1.6 %collective-permute-done.3.x3.up3 = bf16[272,512]{1,0:T(8,128)(2,1)S(1)} collective-permute-done((bf16[272,512]{1,0:T(8,128)(2,1)S(1)}, bf16[272,512]{1,0:T(8,128)(2,1)S(1)}, u32[]{:S(2)}, u32[]{:S(2)}) %collective-permute-start.3) | collective-permute-done | bytes 278560 | tf_op jit(solution)/shard_map/ppermute | solution.py:402
  29.0 1.3 shard_map.96
  30.3 4.3 %collective-permute-start.7 = (bf16[512,256]{1,0:T(8,128)(2,1)S(1)}, bf16[512,256]{1,0:T(8,128)(2,1)S(1)}, u32[]{:S(2)}, u32[]{:S(2)}) collective-permute-start(bf16[512,256]{1,0:T(8,128)(2,1)S(1)} %get-tuple-element.42.q0), channel_id=1, source_target_pairs={{0,16},{16,0},{1,17},{17,1},{2,18},{18,2},{3,19},{19,3},{4,20},{20... | collective-permute-start | bytes 786440 | tf_op jit(solution)/shard_map/ppermute | solution.py:422
  34.6 7.5 %collective-permute-start.6 = (bf16[528,256]{1,0:T(8,128)(2,1)S(1)}, bf16[528,256]{1,0:T(8,128)(2,1)S(1)}, u32[]{:S(2)}, u32[]{:S(2)}) collective-permute-start(bf16[528,256]{1,0:T(8,128)(2,1)S(1)} %get-tuple-element.41.kv0), channel_id=1, source_target_pairs={{0,136},{8,128},{128,8},{136,0},{1,137},{9,129},{129,9},{137,1},{2... | collective-permute-start | bytes 811016 | tf_op jit(solution)/shard_map/ppermute | solution.py:420
  43.8 1.2 collective-permute-done.8.q2
  44.9 9.5 %collective-permute-done.6.kv3 = bf16[528,256]{1,0:T(8,128)(2,1)S(1)} collective-permute-done((bf16[528,256]{1,0:T(8,128)(2,1)S(1)}, bf16[528,256]{1,0:T(8,128)(2,1)S(1)}, u32[]{:S(2)}, u32[]{:S(2)}) %collective-permute-start.6) | collective-permute-done | bytes 270368 | tf_op jit(solution)/shard_map/ppermute | solution.py:420
  54.8 3.7 %shard_map.97 = (f32[1024,128]{1,0:T(8,128)S(1)}, bf16[1024,128]{1,0:T(8,128)(2,1)S(1)}, bf16[8,256,256]{2,1,0:T(8,128)(2,1)S(1)}, bf16[8,256,128]{2,1,0:T(8,128)(2,1)S(1)}, bf16[8,256,256]{2,1,0:T(8,128)(2,1)S(1)}) custom-call(s32[8]{0:T(128)S(1)} %concatenate.3.meta_ref, bf16[528,256]{1,0:T(8,128)(2,1)S(1)} %get-tuple-element.41.kv0, ...), custom_call_target="tpu_custom_call" | custom-call | flops 1006632960 | bytes 5538336 | tf_op jit(solution)/shard_map/pallas_call | solution.py:73
  58.5 1.3 collective-permute-start.10
  59.9 1.2 collective-permute-done.10.got_core
  61.1 1.4 collective-permute-start.11
  62.4 3.4 %collective-permute-done.11.got_z = bf16[512,128]{1,0:T(8,128)(2,1)S(1)} collective-permute-done((bf16[512,128]{1,0:T(8,128)(2,1)S(1)}, bf16[512,128]{1,0:T(8,128)(2,1)S(1)}, u32[]{:S(2)}, u32[]{:S(2)}) %collective-permute-start.11) | collective-permute-done | bytes 131104 | tf_op jit(solution)/shard_map/ppermute | solution.py:441
  65.9 1.1 shard_map.98
  67.0 1.4 collective-permute-start.12
  68.3 1.5 collective-permute-start.13
  69.8 1.1 collective-permute-done.12.g1
  70.9 2.4 %collective-permute-start.14 = (bf16[512,128]{1,0:T(8,128)(2,1)S(1)}, bf16[512,128]{1,0:T(8,128)(2,1)S(1)}, u32[]{:S(2)}, u32[]{:S(2)}) collective-permute-start(bf16[512,128]{1,0:T(8,128)(2,1)S(1)} %collective-permute-done.12.g1), channel_id=1, source_target_pairs={{0,4},{4,0},{1,5},{5,1},{2,6},{6,2},{3,7},{7,3},{8,12},{12,8},{9,1... | collective-permute-start | bytes 393224 | tf_op jit(solution)/shard_map/ppermute | solution.py:451
  73.2 1.0 collective-permute-done.14.g3
  74.2 6.5 %shard_map.99 = (f32[512,256]{1,0:T(8,128)S(1)}, bf16[512,256]{1,0:T(8,128)(2,1)S(1)}, bf16[512,256]{1,0:T(8,128)(2,1)S(1)}, bf16[512,256]{1,0:T(8,128)(2,1)S(1)...) custom-call(s32[8]{0:T(128)S(1)} %concatenate.3.meta_ref, s32[128]{0:T(128)S(1)} %shard_map.95._.list_ref, ...), custom_call_target="tpu_custom_call" | custom-call | flops 2013265920 | bytes 5243424 | tf_op jit(solution)/shard_map/pallas_call | solution.py:73
  81.5 5.6 %collective-permute-start.16 = (bf16[512,256]{1,0:T(8,128)(2,1)S(1)}, bf16[512,256]{1,0:T(8,128)(2,1)S(1)}, u32[]{:S(2)}, u32[]{:S(2)}) collective-permute-start(bf16[512,256]{1,0:T(8,128)(2,1)S(1)} %get-tuple-element.53), channel_id=1, source_target_pairs={{0,128},{8,136},{128,0},{136,8},{1,129},{9,137},{129,1},{137,9},{2... | collective-permute-start | bytes 786440 | tf_op jit(solution)/shard_map/ppermute | solution.py:470
  87.1 1.5 collective-permute-start.19
  88.9 10.1 %collective-permute-done.16.r2 = bf16[512,256]{1,0:T(8,128)(2,1)S(1)} collective-permute-done((bf16[512,256]{1,0:T(8,128)(2,1)S(1)}, bf16[512,256]{1,0:T(8,128)(2,1)S(1)}, u32[]{:S(2)}, u32[]{:S(2)}) %collective-permute-start.16) | collective-permute-done | bytes 262176 | tf_op jit(solution)/shard_map/ppermute | solution.py:470
  99.0 2.0 %collective-permute-done.17.r3 = bf16[512,256]{1,0:T(8,128)(2,1)S(1)} collective-permute-done((bf16[512,256]{1,0:T(8,128)(2,1)S(1)}, bf16[512,256]{1,0:T(8,128)(2,1)S(1)}, u32[]{:S(2)}, u32[]{:S(2)}) %collective-permute-start.17) | collective-permute-done | bytes 262176 | tf_op jit(solution)/shard_map/ppermute | solution.py:469
  101.0 1.7 %shard_map.101 = (f32[512,128]{1,0:T(8,128)S(1)}, bf16[512,128]{1,0:T(8,128)(2,1)S(1)}, bf16[512,128]{1,0:T(8,128)(2,1)S(1)}, bf16[512,128]{1,0:T(8,128)(2,1)S(1...) custom-call(s32[8]{0:T(128)S(1)} %concatenate.3.meta_ref, f32[512,256]{1,0:T(8,128)S(1)} %get-tuple-element.51.own, ...), custom_call_target="tpu_custom_call" | custom-call | flops 536870912 | bytes 6357024 | tf_op jit(solution)/shard_map/pallas_call | solution.py:73
  102.7 1.7 %collective-permute-start.20 = (bf16[320,512]{1,0:T(8,128)(2,1)S(1)}, bf16[320,512]{1,0:T(8,128)(2,1)S(1)}, u32[]{:S(2)}, u32[]{:S(2)}) collective-permute-start(bf16[320,512]{1,0:T(8,128)(2,1)S(1)} %get-tuple-element.61), channel_id=1, source_target_pairs={{0,4},{4,0},{1,5},{5,1},{2,6},{6,2},{3,7},{7,3},{8,12},{12,8},{9,1... | collective-permute-start | bytes 983048 | tf_op jit(solution)/shard_map/ppermute | solution.py:483
  104.4 1.3 collective-permute-done.20.got
  106.4 1.2 collective-permute-start.22
  107.6 2.7 %collective-permute-start.23 = (bf16[80,512]{1,0:T(8,128)(2,1)S(1)}, bf16[80,512]{1,0:T(8,128)(2,1)S(1)}, u32[]{:S(2)}, u32[]{:S(2)}) collective-permute-start(bf16[80,512]{1,0:T(8,128)(2,1)S(1)} %get-tuple-element.65), channel_id=1, source_target_pairs={{0,136},{8,128},{128,8},{136,0},{1,137},{9,129},{129,9},{137,1},{2... | collective-permute-start | bytes 245768 | tf_op jit(solution)/shard_map/ppermute | solution.py:491
  110.3 1.4 collective-permute-done.22.p2
  111.7 2.1 %collective-permute-done.23.p3 = bf16[80,512]{1,0:T(8,128)(2,1)S(1)} collective-permute-done((bf16[80,512]{1,0:T(8,128)(2,1)S(1)}, bf16[80,512]{1,0:T(8,128)(2,1)S(1)}, u32[]{:S(2)}, u32[]{:S(2)}) %collective-permute-start.23) | collective-permute-done | bytes 81952 | tf_op jit(solution)/shard_map/ppermute | solution.py:491
  113.8 1.5 collective-permute-start.24
  115.2 1.4 collective-permute-start.26
  116.6 2.6 %collective-permute-start.27 = (bf16[512,128]{1,0:T(8,128)(2,1)S(1)}, bf16[512,128]{1,0:T(8,128)(2,1)S(1)}, u32[]{:S(2)}, u32[]{:S(2)}) collective-permute-start(bf16[512,128]{1,0:T(8,128)(2,1)S(1)} %get-tuple-element.72), channel_id=1, source_target_pairs={{0,2},{1,3},{2,0},{3,1},{4,6},{5,7},{6,4},{7,5},{8,10},{9,11},{10,... | collective-permute-start | bytes 393224 | tf_op jit(solution)/shard_map/ppermute | solution.py:496
  119.4 4.7 %collective-permute-done.27.t2 = bf16[512,128]{1,0:T(8,128)(2,1)S(1)} collective-permute-done((bf16[512,128]{1,0:T(8,128)(2,1)S(1)}, bf16[512,128]{1,0:T(8,128)(2,1)S(1)}, u32[]{:S(2)}, u32[]{:S(2)}) %collective-permute-start.27) | collective-permute-done | bytes 131104 | tf_op jit(solution)/shard_map/ppermute | solution.py:496
  124.1 2.8 %collective-permute-done.28.t3 = bf16[512,128]{1,0:T(8,128)(2,1)S(1)} collective-permute-done((bf16[512,128]{1,0:T(8,128)(2,1)S(1)}, bf16[512,128]{1,0:T(8,128)(2,1)S(1)}, u32[]{:S(2)}, u32[]{:S(2)}) %collective-permute-start.28) | collective-permute-done | bytes 131104 | tf_op jit(solution)/shard_map/ppermute | solution.py:496
  127.0 3.2 %collective-permute-start.29 = (bf16[80,512]{1,0:T(8,128)(2,1)S(1)}, bf16[80,512]{1,0:T(8,128)(2,1)S(1)}, u32[]{:S(2)}, u32[]{:S(2)}) collective-permute-start(bf16[80,512]{1,0:T(8,128)(2,1)S(1)} %get-tuple-element.74), channel_id=1, source_target_pairs={{0,64},{64,0},{1,65},{65,1},{2,66},{66,2},{3,67},{67,3},{4,68},{68... | collective-permute-start | bytes 245768 | tf_op jit(solution)/shard_map/ppermute | solution.py:506
  130.2 5.8 %collective-permute-start.33 = (bf16[512,128]{1,0:T(8,128)(2,1)S(1)}, bf16[512,128]{1,0:T(8,128)(2,1)S(1)}, u32[]{:S(2)}, u32[]{:S(2)}) collective-permute-start(bf16[512,128]{1,0:T(8,128)(2,1)S(1)} %get-tuple-element.75), channel_id=1, source_target_pairs={{0,0},{64,4},{32,8},{96,12},{24,16},{88,20},{56,24},{120,28},{12,3... | collective-permute-start | bytes 393224 | tf_op jit(solution)/shard_map/ppermute | solution.py:505
  136.0 1.5 %collective-permute-start.32 = (bf16[80,512]{1,0:T(8,128)(2,1)S(1)}, bf16[80,512]{1,0:T(8,128)(2,1)S(1)}, u32[]{:S(2)}, u32[]{:S(2)}) collective-permute-start(bf16[80,512]{1,0:T(8,128)(2,1)S(1)} %add_convert_fusion.2.p0), channel_id=1, source_target_pairs={{0,136},{8,128},{128,8},{136,0},{1,137},{9,129},{129,9},{137,1},{2... | collective-permute-start | bytes 245768 | tf_op jit(solution)/shard_map/ppermute | solution.py:508
  137.6 1.8 %collective-permute-start.30 = (bf16[80,512]{1,0:T(8,128)(2,1)S(1)}, bf16[80,512]{1,0:T(8,128)(2,1)S(1)}, u32[]{:S(2)}, u32[]{:S(2)}) collective-permute-start(bf16[80,512]{1,0:T(8,128)(2,1)S(1)} %add_convert_fusion.2.p0), channel_id=1, source_target_pairs={{0,8},{8,0},{128,136},{136,128},{1,9},{9,1},{129,137},{137,129},{2... | collective-permute-start | bytes 245768 | tf_op jit(solution)/shard_map/ppermute | solution.py:508
  139.4 1.0 collective-permute-done.33._.grad
  140.6 4.3 %collective-permute-done.31.p2 = bf16[80,512]{1,0:T(8,128)(2,1)S(1)} collective-permute-done((bf16[80,512]{1,0:T(8,128)(2,1)S(1)}, bf16[80,512]{1,0:T(8,128)(2,1)S(1)}, u32[]{:S(2)}, u32[]{:S(2)}) %collective-permute-start.31) | collective-permute-done | bytes 81952 | tf_op jit(solution)/shard_map/ppermute | solution.py:508
  145.5 1.8 %collective-permute-start.34 = (bf16[320,512]{1,0:T(8,128)(2,1)S(1)}, bf16[320,512]{1,0:T(8,128)(2,1)S(1)}, u32[]{:S(2)}, u32[]{:S(2)}) collective-permute-start(bf16[320,512]{1,0:T(8,128)(2,1)S(1)} %shard_map.105.mine), channel_id=1, source_target_pairs={{0,4},{4,0},{1,5},{5,1},{2,6},{6,2},{3,7},{7,3},{8,12},{12,8},{9,1... | collective-permute-start | bytes 983048 | tf_op jit(solution)/shard_map/ppermute | solution.py:510
  147.2 1.3 collective-permute-done.34.other
  148.5 1.7 %shard_map.106 = (f32[512,512]{1,0:T(8,128)}, f32[128,512]{1,0:T(8,128)}, bf16[1,512,128]{2,1,0:T(8,128)(2,1)}) custom-call(s32[8]{0:T(128)S(1)} %concatenate.3.meta_ref, bf16[320,512]{1,0:T(8,128)(2,1)S(1)} %shard_map.105.mine, bf16[320,512]{1,0:T(8,128)(2,1)S(1)} %collective-permute-done.34.other, bf16[512,128]{1,0:T(8,128)(2,1)S(1)} %collective-permute-done.33._.grad), custom_call_target="tpu_custom_call" | custom-call | bytes 2228256 | tf_op jit(solution)/shard_map/pallas_call | solution.py:73
  (49 shorter events, 8.1 us)
Async XLA Ops:
  0.6 28.4 %copy-start = (bf16[512,512]{1,0:T(8,128)(2,1)S(1)}, bf16[512,512]{1,0:T(8,128)(2,1)}, u32[]{:S(2)}) copy-start(bf16[512,512]{1,0:T(8,128)(2,1)} %w.1) | copy-start | bytes 1572868
  2.4 16.3 %collective-permute-start = (bf16[272,512]{1,0:T(8,128)(2,1)}, bf16[272,512]{1,0:T(8,128)(2,1)S(1)}, u32[]{:S(2)}, u32[]{:S(2)}) collective-permute-start(bf16[272,512]{1,0:T(8,128)(2,1)} %shard_map.94), channel_id=1, source_target_pairs={{0,0},{4,64},{8,32},{12,96},{16,24},{20,88},{24,56},{28,120},{32,1... | collective-permute-start | bytes 835592 | tf_op jit(solution)/shard_map/ppermute | solution.py:399
  18.8 9.2 %collective-permute-start.3 = (bf16[272,512]{1,0:T(8,128)(2,1)S(1)}, bf16[272,512]{1,0:T(8,128)(2,1)S(1)}, u32[]{:S(2)}, u32[]{:S(2)}) collective-permute-start(bf16[272,512]{1,0:T(8,128)(2,1)S(1)} %collective-permute-done.xa_ref.up0), channel_id=1, source_target_pairs={{0,3},{1,2},{2,1},{3,0},{4,7},{5,6},{6,5},{7,4},{8,11},{9,10},{10,... | collective-permute-start | bytes 835592 | tf_op jit(solution)/shard_map/ppermute | solution.py:402
  21.5 6.9 %collective-permute-start.2 = (bf16[272,512]{1,0:T(8,128)(2,1)S(1)}, bf16[272,512]{1,0:T(8,128)(2,1)S(1)}, u32[]{:S(2)}, u32[]{:S(2)}) collective-permute-start(bf16[272,512]{1,0:T(8,128)(2,1)S(1)} %collective-permute-done.xa_ref.up0), channel_id=1, source_target_pairs={{0,2},{1,3},{2,0},{3,1},{4,6},{5,7},{6,4},{7,5},{8,10},{9,11},{10,... | collective-permute-start | bytes 835592 | tf_op jit(solution)/shard_map/ppermute | solution.py:402
  21.8 7.2 %collective-permute-start.1 = (bf16[272,512]{1,0:T(8,128)(2,1)S(1)}, bf16[272,512]{1,0:T(8,128)(2,1)S(1)}, u32[]{:S(2)}, u32[]{:S(2)}) collective-permute-start(bf16[272,512]{1,0:T(8,128)(2,1)S(1)} %collective-permute-done.xa_ref.up0), channel_id=1, source_target_pairs={{0,1},{1,0},{2,3},{3,2},{4,5},{5,4},{6,7},{7,6},{8,9},{9,8},{10,11... | collective-permute-start | bytes 835592 | tf_op jit(solution)/shard_map/ppermute | solution.py:402
  24.7 4.3 %copy-start.2 = (f32[1,128]{1,0:T(1,128)S(1)}, f32[1,128]{1,0:T(1,128)}, u32[]{:S(2)}) copy-start(f32[1,128]{1,0:T(1,128)} %table_ref.1) | copy-start | bytes 1540
  30.3 13.4 %collective-permute-start.7 = (bf16[512,256]{1,0:T(8,128)(2,1)S(1)}, bf16[512,256]{1,0:T(8,128)(2,1)S(1)}, u32[]{:S(2)}, u32[]{:S(2)}) collective-permute-start(bf16[512,256]{1,0:T(8,128)(2,1)S(1)} %get-tuple-element.42.q0), channel_id=1, source_target_pairs={{0,16},{16,0},{1,17},{17,1},{2,18},{18,2},{3,19},{19,3},{4,20},{20... | collective-permute-start | bytes 786440 | tf_op jit(solution)/shard_map/ppermute | solution.py:422
  34.6 19.8 %collective-permute-start.6 = (bf16[528,256]{1,0:T(8,128)(2,1)S(1)}, bf16[528,256]{1,0:T(8,128)(2,1)S(1)}, u32[]{:S(2)}, u32[]{:S(2)}) collective-permute-start(bf16[528,256]{1,0:T(8,128)(2,1)S(1)} %get-tuple-element.41.kv0), channel_id=1, source_target_pairs={{0,136},{8,128},{128,8},{136,0},{1,137},{9,129},{129,9},{137,1},{2... | collective-permute-start | bytes 811016 | tf_op jit(solution)/shard_map/ppermute | solution.py:420
  42.1 12.3 %collective-permute-start.5 = (bf16[528,256]{1,0:T(8,128)(2,1)S(1)}, bf16[528,256]{1,0:T(8,128)(2,1)S(1)}, u32[]{:S(2)}, u32[]{:S(2)}) collective-permute-start(bf16[528,256]{1,0:T(8,128)(2,1)S(1)} %get-tuple-element.41.kv0), channel_id=1, source_target_pairs={{0,128},{8,136},{128,0},{136,8},{1,129},{9,137},{129,1},{137,9},{2... | collective-permute-start | bytes 811016 | tf_op jit(solution)/shard_map/ppermute | solution.py:420
  42.1 12.7 %collective-permute-start.4 = (bf16[528,256]{1,0:T(8,128)(2,1)S(1)}, bf16[528,256]{1,0:T(8,128)(2,1)S(1)}, u32[]{:S(2)}, u32[]{:S(2)}) collective-permute-start(bf16[528,256]{1,0:T(8,128)(2,1)S(1)} %get-tuple-element.41.kv0), channel_id=1, source_target_pairs={{0,8},{8,0},{128,136},{136,128},{1,9},{9,1},{129,137},{137,129},{2... | collective-permute-start | bytes 811016 | tf_op jit(solution)/shard_map/ppermute | solution.py:420
  42.8 2.1 %collective-permute-start.8 = (bf16[512,256]{1,0:T(8,128)(2,1)S(1)}, bf16[512,256]{1,0:T(8,128)(2,1)S(1)}, u32[]{:S(2)}, u32[]{:S(2)}) collective-permute-start(bf16[512,256]{1,0:T(8,128)(2,1)S(1)} %get-tuple-element.42.q0), channel_id=1, source_target_pairs={{0,4},{4,0},{1,5},{5,1},{2,6},{6,2},{3,7},{7,3},{8,12},{12,8},{9,1... | collective-permute-start | bytes 786440 | tf_op jit(solution)/shard_map/ppermute | solution.py:423
  43.8 11.1 %collective-permute-start.9 = (bf16[512,256]{1,0:T(8,128)(2,1)S(1)}, bf16[512,256]{1,0:T(8,128)(2,1)S(1)}, u32[]{:S(2)}, u32[]{:S(2)}) collective-permute-start(bf16[512,256]{1,0:T(8,128)(2,1)S(1)} %collective-permute-done.7.q1), channel_id=1, source_target_pairs={{0,4},{4,0},{1,5},{5,1},{2,6},{6,2},{3,7},{7,3},{8,12},{12,8},{9,1... | collective-permute-start | bytes 786440 | tf_op jit(solution)/shard_map/ppermute | solution.py:423
  58.5 2.5 %collective-permute-start.10 = (bf16[1024,128]{1,0:T(8,128)(2,1)S(1)}, bf16[1024,128]{1,0:T(8,128)(2,1)S(1)}, u32[]{:S(2)}, u32[]{:S(2)}) collective-permute-start(bf16[1024,128]{1,0:T(8,128)(2,1)S(1)} %get-tuple-element.47), channel_id=1, source_target_pairs={{0,4},{4,0},{1,5},{5,1},{2,6},{6,2},{3,7},{7,3},{8,12},{12,8},{9,1... | collective-permute-start | bytes 786440 | tf_op jit(solution)/shard_map/ppermute | solution.py:439
  61.0 4.8 %copy-start.1 = (bf16[128,512]{1,0:T(8,128)(2,1)S(1)}, bf16[128,512]{1,0:T(8,128)(2,1)}, u32[]{:S(2)}) copy-start(bf16[128,512]{1,0:T(8,128)(2,1)} %wout.1) | copy-start | bytes 393220
  61.1 4.8 %collective-permute-start.11 = (bf16[512,128]{1,0:T(8,128)(2,1)S(1)}, bf16[512,128]{1,0:T(8,128)(2,1)S(1)}, u32[]{:S(2)}, u32[]{:S(2)}) collective-permute-start(bf16[512,128]{1,0:T(8,128)(2,1)S(1)} %add_convert_fusion.1), channel_id=1, source_target_pairs={{0,16},{16,0},{1,17},{17,1},{2,18},{18,2},{3,19},{19,3},{4,20},{20... | collective-permute-start | bytes 393224 | tf_op jit(solution)/shard_map/ppermute | solution.py:441
  67.0 3.9 %collective-permute-start.12 = (bf16[512,128]{1,0:T(8,128)(2,1)S(1)}, bf16[512,128]{1,0:T(8,128)(2,1)S(1)}, u32[]{:S(2)}, u32[]{:S(2)}) collective-permute-start(bf16[512,128]{1,0:T(8,128)(2,1)S(1)} %get-tuple-element.50.g0), channel_id=1, source_target_pairs={{0,16},{16,0},{1,17},{17,1},{2,18},{18,2},{3,19},{19,3},{4,20},{20... | collective-permute-start | bytes 393224 | tf_op jit(solution)/shard_map/ppermute | solution.py:450
  68.3 4.9 %collective-permute-start.13 = (bf16[512,128]{1,0:T(8,128)(2,1)S(1)}, bf16[512,128]{1,0:T(8,128)(2,1)S(1)}, u32[]{:S(2)}, u32[]{:S(2)}) collective-permute-start(bf16[512,128]{1,0:T(8,128)(2,1)S(1)} %get-tuple-element.50.g0), channel_id=1, source_target_pairs={{0,4},{4,0},{1,5},{5,1},{2,6},{6,2},{3,7},{7,3},{8,12},{12,8},{9,1... | collective-permute-start | bytes 393224 | tf_op jit(solution)/shard_map/ppermute | solution.py:451
  70.9 3.3 %collective-permute-start.14 = (bf16[512,128]{1,0:T(8,128)(2,1)S(1)}, bf16[512,128]{1,0:T(8,128)(2,1)S(1)}, u32[]{:S(2)}, u32[]{:S(2)}) collective-permute-start(bf16[512,128]{1,0:T(8,128)(2,1)S(1)} %collective-permute-done.12.g1), channel_id=1, source_target_pairs={{0,4},{4,0},{1,5},{5,1},{2,6},{6,2},{3,7},{7,3},{8,12},{12,8},{9,1... | collective-permute-start | bytes 393224 | tf_op jit(solution)/shard_map/ppermute | solution.py:451
  80.7 6.4 %collective-permute-start.18 = (bf16[1024,128]{1,0:T(8,128)(2,1)S(1)}, bf16[1024,128]{1,0:T(8,128)(2,1)S(1)}, u32[]{:S(2)}, u32[]{:S(2)}) collective-permute-start(bf16[1024,128]{1,0:T(8,128)(2,1)S(1)} %get-tuple-element.56), channel_id=1, source_target_pairs={{0,4},{4,0},{1,5},{5,1},{2,6},{6,2},{3,7},{7,3},{8,12},{12,8},{9,1... | collective-permute-start | bytes 786440 | tf_op jit(solution)/shard_map/ppermute | solution.py:471
  81.1 7.8 %collective-permute-start.15 = (bf16[512,256]{1,0:T(8,128)(2,1)S(1)}, bf16[512,256]{1,0:T(8,128)(2,1)S(1)}, u32[]{:S(2)}, u32[]{:S(2)}) collective-permute-start(bf16[512,256]{1,0:T(8,128)(2,1)S(1)} %get-tuple-element.52), channel_id=1, source_target_pairs={{0,8},{8,0},{128,136},{136,128},{1,9},{9,1},{129,137},{137,129},{2... | collective-permute-start | bytes 786440 | tf_op jit(solution)/shard_map/ppermute | solution.py:468
  81.5 17.5 %collective-permute-start.16 = (bf16[512,256]{1,0:T(8,128)(2,1)S(1)}, bf16[512,256]{1,0:T(8,128)(2,1)S(1)}, u32[]{:S(2)}, u32[]{:S(2)}) collective-permute-start(bf16[512,256]{1,0:T(8,128)(2,1)S(1)} %get-tuple-element.53), channel_id=1, source_target_pairs={{0,128},{8,136},{128,0},{136,8},{1,129},{9,137},{129,1},{137,9},{2... | collective-permute-start | bytes 786440 | tf_op jit(solution)/shard_map/ppermute | solution.py:470
  87.1 13.9 %collective-permute-start.17 = (bf16[512,256]{1,0:T(8,128)(2,1)S(1)}, bf16[512,256]{1,0:T(8,128)(2,1)S(1)}, u32[]{:S(2)}, u32[]{:S(2)}) collective-permute-start(bf16[512,256]{1,0:T(8,128)(2,1)S(1)} %get-tuple-element.54), channel_id=1, source_target_pairs={{0,136},{8,128},{128,8},{136,0},{1,137},{9,129},{129,9},{137,1},{2... | collective-permute-start | bytes 786440 | tf_op jit(solution)/shard_map/ppermute | solution.py:469
  87.1 13.9 %collective-permute-start.19 = (bf16[512,128]{1,0:T(8,128)(2,1)S(1)}, bf16[512,128]{1,0:T(8,128)(2,1)S(1)}, u32[]{:S(2)}, u32[]{:S(2)}) collective-permute-start(bf16[512,128]{1,0:T(8,128)(2,1)S(1)} %add_convert_fusion), channel_id=1, source_target_pairs={{0,16},{16,0},{1,17},{17,1},{2,18},{18,2},{3,19},{19,3},{4,20},{20... | collective-permute-start | bytes 393224 | tf_op jit(solution)/shard_map/ppermute | solution.py:473
  102.7 2.9 %collective-permute-start.20 = (bf16[320,512]{1,0:T(8,128)(2,1)S(1)}, bf16[320,512]{1,0:T(8,128)(2,1)S(1)}, u32[]{:S(2)}, u32[]{:S(2)}) collective-permute-start(bf16[320,512]{1,0:T(8,128)(2,1)S(1)} %get-tuple-element.61), channel_id=1, source_target_pairs={{0,4},{4,0},{1,5},{5,1},{2,6},{6,2},{3,7},{7,3},{8,12},{12,8},{9,1... | collective-permute-start | bytes 983048 | tf_op jit(solution)/shard_map/ppermute | solution.py:483
  106.3 3.9 %collective-permute-start.21 = (bf16[80,512]{1,0:T(8,128)(2,1)S(1)}, bf16[80,512]{1,0:T(8,128)(2,1)S(1)}, u32[]{:S(2)}, u32[]{:S(2)}) collective-permute-start(bf16[80,512]{1,0:T(8,128)(2,1)S(1)} %get-tuple-element.63), channel_id=1, source_target_pairs={{0,8},{8,0},{128,136},{136,128},{1,9},{9,1},{129,137},{137,129},{2... | collective-permute-start | bytes 245768 | tf_op jit(solution)/shard_map/ppermute | solution.py:491
  106.4 5.2 %collective-permute-start.22 = (bf16[80,512]{1,0:T(8,128)(2,1)S(1)}, bf16[80,512]{1,0:T(8,128)(2,1)S(1)}, u32[]{:S(2)}, u32[]{:S(2)}) collective-permute-start(bf16[80,512]{1,0:T(8,128)(2,1)S(1)} %get-tuple-element.64), channel_id=1, source_target_pairs={{0,128},{8,136},{128,0},{136,8},{1,129},{9,137},{129,1},{137,9},{2... | collective-permute-start | bytes 245768 | tf_op jit(solution)/shard_map/ppermute | solution.py:491
  107.6 6.2 %collective-permute-start.23 = (bf16[80,512]{1,0:T(8,128)(2,1)S(1)}, bf16[80,512]{1,0:T(8,128)(2,1)S(1)}, u32[]{:S(2)}, u32[]{:S(2)}) collective-permute-start(bf16[80,512]{1,0:T(8,128)(2,1)S(1)} %get-tuple-element.65), channel_id=1, source_target_pairs={{0,136},{8,128},{128,8},{136,0},{1,137},{9,129},{129,9},{137,1},{2... | collective-permute-start | bytes 245768 | tf_op jit(solution)/shard_map/ppermute | solution.py:491
  113.8 5.4 %collective-permute-start.24 = (bf16[80,512]{1,0:T(8,128)(2,1)S(1)}, bf16[80,512]{1,0:T(8,128)(2,1)S(1)}, u32[]{:S(2)}, u32[]{:S(2)}) collective-permute-start(bf16[80,512]{1,0:T(8,128)(2,1)S(1)} %get-tuple-element.69), channel_id=1, source_target_pairs={{0,16},{16,0},{1,17},{17,1},{2,18},{18,2},{3,19},{19,3},{4,20},{20... | collective-permute-start | bytes 245768 | tf_op jit(solution)/shard_map/ppermute | solution.py:497
  115.2 4.1 %collective-permute-start.26 = (bf16[512,128]{1,0:T(8,128)(2,1)S(1)}, bf16[512,128]{1,0:T(8,128)(2,1)S(1)}, u32[]{:S(2)}, u32[]{:S(2)}) collective-permute-start(bf16[512,128]{1,0:T(8,128)(2,1)S(1)} %get-tuple-element.71), channel_id=1, source_target_pairs={{0,1},{1,0},{2,3},{3,2},{4,5},{5,4},{6,7},{7,6},{8,9},{9,8},{10,11... | collective-permute-start | bytes 393224 | tf_op jit(solution)/shard_map/ppermute | solution.py:496
  116.6 7.5 %collective-permute-start.27 = (bf16[512,128]{1,0:T(8,128)(2,1)S(1)}, bf16[512,128]{1,0:T(8,128)(2,1)S(1)}, u32[]{:S(2)}, u32[]{:S(2)}) collective-permute-start(bf16[512,128]{1,0:T(8,128)(2,1)S(1)} %get-tuple-element.72), channel_id=1, source_target_pairs={{0,2},{1,3},{2,0},{3,1},{4,6},{5,7},{6,4},{7,5},{8,10},{9,11},{10,... | collective-permute-start | bytes 393224 | tf_op jit(solution)/shard_map/ppermute | solution.py:496
  119.2 7.7 %collective-permute-start.28 = (bf16[512,128]{1,0:T(8,128)(2,1)S(1)}, bf16[512,128]{1,0:T(8,128)(2,1)S(1)}, u32[]{:S(2)}, u32[]{:S(2)}) collective-permute-start(bf16[512,128]{1,0:T(8,128)(2,1)S(1)} %get-tuple-element.73), channel_id=1, source_target_pairs={{0,3},{1,2},{2,1},{3,0},{4,7},{5,6},{6,5},{7,4},{8,11},{9,10},{10,... | collective-permute-start | bytes 393224 | tf_op jit(solution)/shard_map/ppermute | solution.py:496
  119.2 7.7 %collective-permute-start.25 = (bf16[80,512]{1,0:T(8,128)(2,1)S(1)}, bf16[80,512]{1,0:T(8,128)(2,1)S(1)}, u32[]{:S(2)}, u32[]{:S(2)}) collective-permute-start(bf16[80,512]{1,0:T(8,128)(2,1)S(1)} %add_convert_fusion.3.a), channel_id=1, source_target_pairs={{0,32},{32,0},{1,33},{33,1},{2,34},{34,2},{3,35},{35,3},{4,36},{36... | collective-permute-start | bytes 245768 | tf_op jit(solution)/shard_map/ppermute | solution.py:499
  127.0 9.0 %collective-permute-start.29 = (bf16[80,512]{1,0:T(8,128)(2,1)S(1)}, bf16[80,512]{1,0:T(8,128)(2,1)S(1)}, u32[]{:S(2)}, u32[]{:S(2)}) collective-permute-start(bf16[80,512]{1,0:T(8,128)(2,1)S(1)} %get-tuple-element.74), channel_id=1, source_target_pairs={{0,64},{64,0},{1,65},{65,1},{2,66},{66,2},{3,67},{67,3},{4,68},{68... | collective-permute-start | bytes 245768 | tf_op jit(solution)/shard_map/ppermute | solution.py:506
  130.2 10.2 %collective-permute-start.33 = (bf16[512,128]{1,0:T(8,128)(2,1)S(1)}, bf16[512,128]{1,0:T(8,128)(2,1)S(1)}, u32[]{:S(2)}, u32[]{:S(2)}) collective-permute-start(bf16[512,128]{1,0:T(8,128)(2,1)S(1)} %get-tuple-element.75), channel_id=1, source_target_pairs={{0,0},{64,4},{32,8},{96,12},{24,16},{88,20},{56,24},{120,28},{12,3... | collective-permute-start | bytes 393224 | tf_op jit(solution)/shard_map/ppermute | solution.py:505
  136.0 4.6 %collective-permute-start.32 = (bf16[80,512]{1,0:T(8,128)(2,1)S(1)}, bf16[80,512]{1,0:T(8,128)(2,1)S(1)}, u32[]{:S(2)}, u32[]{:S(2)}) collective-permute-start(bf16[80,512]{1,0:T(8,128)(2,1)S(1)} %add_convert_fusion.2.p0), channel_id=1, source_target_pairs={{0,136},{8,128},{128,8},{136,0},{1,137},{9,129},{129,9},{137,1},{2... | collective-permute-start | bytes 245768 | tf_op jit(solution)/shard_map/ppermute | solution.py:508
  137.5 7.3 %collective-permute-start.31 = (bf16[80,512]{1,0:T(8,128)(2,1)S(1)}, bf16[80,512]{1,0:T(8,128)(2,1)S(1)}, u32[]{:S(2)}, u32[]{:S(2)}) collective-permute-start(bf16[80,512]{1,0:T(8,128)(2,1)S(1)} %add_convert_fusion.2.p0), channel_id=1, source_target_pairs={{0,128},{8,136},{128,0},{136,8},{1,129},{9,137},{129,1},{137,9},{2... | collective-permute-start | bytes 245768 | tf_op jit(solution)/shard_map/ppermute | solution.py:508
  137.6 7.3 %collective-permute-start.30 = (bf16[80,512]{1,0:T(8,128)(2,1)S(1)}, bf16[80,512]{1,0:T(8,128)(2,1)S(1)}, u32[]{:S(2)}, u32[]{:S(2)}) collective-permute-start(bf16[80,512]{1,0:T(8,128)(2,1)S(1)} %add_convert_fusion.2.p0), channel_id=1, source_target_pairs={{0,8},{8,0},{128,136},{136,128},{1,9},{9,1},{129,137},{137,129},{2... | collective-permute-start | bytes 245768 | tf_op jit(solution)/shard_map/ppermute | solution.py:508
  145.5 3.0 %collective-permute-start.34 = (bf16[320,512]{1,0:T(8,128)(2,1)S(1)}, bf16[320,512]{1,0:T(8,128)(2,1)S(1)}, u32[]{:S(2)}, u32[]{:S(2)}) collective-permute-start(bf16[320,512]{1,0:T(8,128)(2,1)S(1)} %shard_map.105.mine), channel_id=1, source_target_pairs={{0,4},{4,0},{1,5},{5,1},{2,6},{6,2},{3,7},{7,3},{8,12},{12,8},{9,1... | collective-permute-start | bytes 983048 | tf_op jit(solution)/shard_map/ppermute | solution.py:510

commit v3 on v2

--- a/solution.py
+++ b/solution.py
@@ -109,7 +109,7 @@
 
 
 def project_kernel(
-    _, xa_ref, x1, x2, x3, w_ref, table_ref, kv_ref, q_ref, gate_ref, slope_ref, x_ref
+    _, xa_ref, x1, x3, x2, w_ref, table_ref, kv_ref, q_ref, gate_ref, slope_ref, x_ref
 ):
     y = lax.axis_index("y")
     for rel, piece in enumerate((xa_ref, x1, x2, x3)):
@@ -206,7 +206,7 @@
 
 
 def forward_kernel(
-    meta_ref, kv0, kv1, kv2, kv3, q0, q1, q2, q3, list_ref,
+    meta_ref, kv0, kv1, kv3, kv2, q0, q1, q2, q3, list_ref,
     keep_ref, send_ref, k_ref, v_ref, q_ref, acc,
 ):
     bucket = lax.broadcasted_iota(jnp.int32, (NB, HALF), 0).astype(F32)
@@ -326,7 +326,7 @@
 
 
 def tail_kernel(
-    meta_ref, own, r1, r2, r3, keep, got_core, got_z, grad_gate, slope, w, x_all, wout_terms,
+    meta_ref, own, r2, r1, r3, keep, got_core, got_z, grad_gate, slope, w, x_all, wout_terms,
     t0_ref, t1_ref, t2_ref, t3_ref, stay_ref, away_ref,
     grad, full,
 ):
@@ -366,7 +366,7 @@
         out[...] = total[rows, :].astype(out.dtype)
 
 
-def join_kernel(meta_ref, p0, p1, p2, p3, _, out_ref):
+def join_kernel(meta_ref, p0, p1, p3, p2, _, out_ref):
     x = meta_ref[2]
     for rel, piece in enumerate((p0, p1, p2, p3)):
         out_ref[pl.ds(pl.multiple_of((x ^ rel) * PIECE, 16), PIECE), :] = piece[...]
@@ -414,7 +414,7 @@
         project_kernel,
         [((ROWS + 16, 2 * DH), BF), ((ROWS, 2 * DH), BF), ((ROWS, DH), BF), ((ROWS, WIDTH), F32)]
         + [((ROWS, WIDTH), BF)],
-        (pairs, xa, x1, x2, x3, weight_in, time_table),
+        (pairs, xa, x1, x3, x2, weight_in, time_table),
         flops=2 * ROWS * WIDTH * WIDTH,
     )
     kvs = [kv] + [lax.ppermute(kv, ("xh", "xl"), flip_x(rel)) for rel in (1, 3, 2)]
@@ -432,7 +432,7 @@
             ((blocks, HALF, DH), BF),
             ((blocks, HALF, 2 * DH), BF),
         ],
-        (meta, *kvs, *qs, pairs),
+        (meta, kvs[0], kvs[1], kvs[3], kvs[2], *qs, pairs),
         scratch=[pltpu.VMEM((blocks, HALF, DH), F32)],
         flops=20 * 6 * HALF * HALF * DH,
     )
@@ -476,7 +476,7 @@
     t0, t1, t2, t3, stay, away = call(
         tail_kernel,
         [((ROWS, DH), F32)] + [((ROWS, DH), BF)] * 3 + [((320, WIDTH), F32), ((320, WIDTH), BF)],
-        (meta, own, r1, r2, r3, keep, got_core, got_z, grad_gate, slope, weight_in, x_all, wout_terms),
+        (meta, own, r2, r1, r3, keep, got_core, got_z, grad_gate, slope, weight_in, x_all, wout_terms),
         scratch=[pltpu.VMEM((ROWS, WIDTH), BF), pltpu.VMEM((WIDTH + DH, WIDTH), F32)],
         flops=4 * ROWS * WIDTH * WIDTH,
     )
@@ -491,10 +491,10 @@
         lax.ppermute(p, ("xh", "xl"), flip_x(rel)) for p, rel in ((p1, 1), (p3, 3), (p2, 2))
     )
     total, t1, t2, t3 = call(
-        sum_kernel, [((PIECE, WIDTH), BF)], (p0, g1, g2, g3, t1, t2, t3), passed=3
+        sum_kernel, [((PIECE, WIDTH), BF)], (p0, g2, g1, g3, t1, t2, t3), passed=3
     )
     u1, u3, u2 = (lax.ppermute(t, "y", flip_y[rel]) for t, rel in ((t1, 1), (t3, 3), (t2, 2)))
-    other = lax.ppermute(total, "z0", FLIP)
+    other = lax.ppermute(total, "z2", FLIP)
     total = (total.astype(F32) + other.astype(F32)).astype(BF)
     other = lax.ppermute(total, "z1", FLIP)
     total, grad_local = call(
@@ -503,10 +503,10 @@
         (total, other, t0, u1, u2, u3),
     )
     grad_local = lax.ppermute(grad_local, MOVED, HOME)
-    other = lax.ppermute(total, "z2", FLIP)
+    other = lax.ppermute(total, "z0", FLIP)
     total = (total.astype(F32) + other.astype(F32)).astype(BF)
     h1, h3, h2 = (lax.ppermute(total, ("xh", "xl"), flip_x(rel)) for rel in (1, 3, 2))
-    (mine_half,) = call(join_kernel, [((320, WIDTH), BF)], (meta, total, h1, h2, h3, grad_local), unread=1)
+    (mine_half,) = call(join_kernel, [((320, WIDTH), BF)], (meta, total, h1, h3, h2, grad_local), unread=1)
     other_half = lax.ppermute(mine_half, "core", FLIP)
     normalizer = 1.0 / math.sqrt(4 * 16 * ROWS)
     win, wout, grad_local = call(

time: 150 us -> 145 us (0.967); the launches traced: 150 us -> 143 us
  Pallas kernels: 21 us -> 16.6 us
  waiting for transfers between devices: 57.6 us -> 56 us
    ppermute x1, waiting for transfers between devices: 0.01 us -> 7.63 us  [body(): r1 = lax.ppermute(s1, ('xh', 'xl'), flip_x(1))]
    ppermute x1, waiting for transfers between devices: 10.1 us -> 3.11 us  [body(): r2 = lax.ppermute(s2, ('xh', 'xl'), flip_x(2))]
    ppermute x3, waiting for transfers between devices: 7.54 us -> 0.54 us  [body(): lax.ppermute(t, 'y', flip_y[rel])]
    pallas_call x13, Pallas kernels: 21 us -> 16.6 us  [call(): pl.pallas_call(kernel, out_shape=[jax.ShapeDtypeStruct(s, t) for s, t in...]
    ppermute x1, starting transfers between devices: 3.21 us -> 0.09 us  [body(): other = lax.ppermute(total, 'z2', FLIP)]
    ppermute x1, waiting for transfers between devices: 0.01 us -> 3.12 us  [body(): other = lax.ppermute(total, 'z1', FLIP)]
    ppermute x1, waiting for transfers between devices: 0.01 us -> 3.09 us  [body(): other = lax.ppermute(total, 'z2', FLIP)]
    ppermute x1, starting transfers between devices: 5.78 us -> 8.06 us  [body(): grad_local = lax.ppermute(grad_local, MOVED, HOME)]
  transfers between devices with their start and end apart: 35 -> 35, of which waited for: 22 -> 21; matrix products, arithmetic and copies ran while one was open for 1% -> 1% of each run, Pallas kernels for 1% -> 1%
where the time goes in v3:
time: 145 us; the launch traced here: 143 us
  starting transfers between devices  67.1 us (46%)
  waiting for transfers between devices  56 us (39%)
  Pallas kernels  16.6 us (11%)
  between operations  2.15 us (1%)
    pallas_call x13, Pallas kernels, call(): pl.pallas_call(kernel, out_shape=[jax.ShapeDtypeStruct(s, t) for s, t in...  16.6 us
    ppermute x1, starting transfers between devices, body(): xa = lax.ppermute(xa, MOVED, AWAY)  10.2 us
    ppermute x3, waiting for transfers between devices, body(): lax.ppermute(kv, ('xh', 'xl'), flip_x(rel))  9.96 us
    ppermute x1, starting transfers between devices, body(): grad_local = lax.ppermute(grad_local, MOVED, HOME)  8.06 us
    ppermute x3, starting transfers between devices, body(): lax.ppermute(kv, ('xh', 'xl'), flip_x(rel))  7.97 us
    ppermute x1, waiting for transfers between devices, body(): r1 = lax.ppermute(s1, ('xh', 'xl'), flip_x(1))  7.63 us
    ppermute x1, starting transfers between devices, body(): r2 = lax.ppermute(s2, ('xh', 'xl'), flip_x(2))  7.59 us
    ppermute x1, waiting for transfers between devices, body(): xa = lax.ppermute(xa, MOVED, AWAY)  6.08 us
  transfers between devices with their start and end apart: 35, of which 21 were waited for; matrix products, arithmetic and copies ran while one was open for 1% of the time, Pallas kernels for 1%

profile of v3, /device:TPU:1, one launch (start us, length us, event | category | flops | bytes accessed | tf_op | source)
XLA Modules:
  0.0 143.3 jit_solution(6262270755072340549)
XLA Ops:
  0.6 1.8 %shard_map.94 = bf16[272,512]{1,0:T(8,128)(2,1)} custom-call(bf16[512,512]{1,0:T(8,128)(2,1)} %bitcast.8, s32[1,512]{1,0:T(1,128)} %times_hbm.1, s32[1,3]{1,0:T(1,128)} %lengths_hbm.1, bf16[512,512]{1,0:T(8,128)(2,1)} %bitcast.9), custom_call_target="tpu_custom_call" | custom-call | bytes 1329164 | tf_op jit(solution)/shard_map/pallas_call | solution.py:73
  2.4 10.2 %collective-permute-start = (bf16[272,512]{1,0:T(8,128)(2,1)}, bf16[272,512]{1,0:T(8,128)(2,1)S(1)}, u32[]{:S(2)}, u32[]{:S(2)}) collective-permute-start(bf16[272,512]{1,0:T(8,128)(2,1)} %shard_map.94), channel_id=1, source_target_pairs={{0,0},{4,64},{8,32},{12,96},{16,24},{20,88},{24,56},{28,120},{32,1... | collective-permute-start | bytes 835592 | tf_op jit(solution)/shard_map/ppermute | solution.py:399
  12.7 6.1 %collective-permute-done.xa_ref.up0 = bf16[272,512]{1,0:T(8,128)(2,1)S(1)} collective-permute-done((bf16[272,512]{1,0:T(8,128)(2,1)}, bf16[272,512]{1,0:T(8,128)(2,1)S(1)}, u32[]{:S(2)}, u32[]{:S(2)}) %collective-permute-start) | collective-permute-done | bytes 278560 | tf_op jit(solution)/shard_map/ppermute | solution.py:399
  18.8 2.9 %collective-permute-start.3 = (bf16[272,512]{1,0:T(8,128)(2,1)S(1)}, bf16[272,512]{1,0:T(8,128)(2,1)S(1)}, u32[]{:S(2)}, u32[]{:S(2)}) collective-permute-start(bf16[272,512]{1,0:T(8,128)(2,1)S(1)} %collective-permute-done.xa_ref.up0), channel_id=1, source_target_pairs={{0,2},{1,3},{2,0},{3,1},{4,6},{5,7},{6,4},{7,5},{8,10},{9,11},{10,... | collective-permute-start | bytes 835592 | tf_op jit(solution)/shard_map/ppermute | solution.py:402
  21.7 0.8 collective-permute-start.2
  25.1 1.7 %shard_map.95._.list_ref = s32[128]{0:T(128)S(1)} custom-call(s32[8]{0:T(128)S(1)} %concatenate.3.meta_ref), custom_call_target="tpu_custom_call" | custom-call | bytes 544 | tf_op jit(solution)/shard_map/pallas_call | solution.py:73
  26.8 1.8 %collective-permute-done.2.x3.up3 = bf16[272,512]{1,0:T(8,128)(2,1)S(1)} collective-permute-done((bf16[272,512]{1,0:T(8,128)(2,1)S(1)}, bf16[272,512]{1,0:T(8,128)(2,1)S(1)}, u32[]{:S(2)}, u32[]{:S(2)}) %collective-permute-start.2) | collective-permute-done | bytes 278560 | tf_op jit(solution)/shard_map/ppermute | solution.py:402
  29.0 1.3 shard_map.96
  30.3 4.1 %collective-permute-start.7 = (bf16[512,256]{1,0:T(8,128)(2,1)S(1)}, bf16[512,256]{1,0:T(8,128)(2,1)S(1)}, u32[]{:S(2)}, u32[]{:S(2)}) collective-permute-start(bf16[512,256]{1,0:T(8,128)(2,1)S(1)} %get-tuple-element.42.q0), channel_id=1, source_target_pairs={{0,16},{16,0},{1,17},{17,1},{2,18},{18,2},{3,19},{19,3},{4,20},{20... | collective-permute-start | bytes 786440 | tf_op jit(solution)/shard_map/ppermute | solution.py:422
  34.4 2.2 %collective-permute-start.6 = (bf16[528,256]{1,0:T(8,128)(2,1)S(1)}, bf16[528,256]{1,0:T(8,128)(2,1)S(1)}, u32[]{:S(2)}, u32[]{:S(2)}) collective-permute-start(bf16[528,256]{1,0:T(8,128)(2,1)S(1)} %get-tuple-element.41.kv0), channel_id=1, source_target_pairs={{0,128},{8,136},{128,0},{136,8},{1,129},{9,137},{129,1},{137,9},{2... | collective-permute-start | bytes 811016 | tf_op jit(solution)/shard_map/ppermute | solution.py:420
  36.6 5.8 %collective-permute-start.5 = (bf16[528,256]{1,0:T(8,128)(2,1)S(1)}, bf16[528,256]{1,0:T(8,128)(2,1)S(1)}, u32[]{:S(2)}, u32[]{:S(2)}) collective-permute-start(bf16[528,256]{1,0:T(8,128)(2,1)S(1)} %get-tuple-element.41.kv0), channel_id=1, source_target_pairs={{0,136},{8,128},{128,8},{136,0},{1,137},{9,129},{129,9},{137,1},{2... | collective-permute-start | bytes 811016 | tf_op jit(solution)/shard_map/ppermute | solution.py:420
  42.4 0.9 collective-permute-start.8
  43.3 1.1 collective-permute-done.8.q2
  44.4 9.6 %collective-permute-done.5.kv3 = bf16[528,256]{1,0:T(8,128)(2,1)S(1)} collective-permute-done((bf16[528,256]{1,0:T(8,128)(2,1)S(1)}, bf16[528,256]{1,0:T(8,128)(2,1)S(1)}, u32[]{:S(2)}, u32[]{:S(2)}) %collective-permute-start.5) | collective-permute-done | bytes 270368 | tf_op jit(solution)/shard_map/ppermute | solution.py:420
  54.3 2.2 %shard_map.97 = (f32[1024,128]{1,0:T(8,128)S(1)}, bf16[1024,128]{1,0:T(8,128)(2,1)S(1)}, bf16[8,256,256]{2,1,0:T(8,128)(2,1)S(1)}, bf16[8,256,128]{2,1,0:T(8,128)(2,1)S(1)}, bf16[8,256,256]{2,1,0:T(8,128)(2,1)S(1)}) custom-call(s32[8]{0:T(128)S(1)} %concatenate.3.meta_ref, bf16[528,256]{1,0:T(8,128)(2,1)S(1)} %get-tuple-element.41.kv0, ...), custom_call_target="tpu_custom_call" | custom-call | flops 1006632960 | bytes 5538336 | tf_op jit(solution)/shard_map/pallas_call | solution.py:73
  56.5 0.9 collective-permute-start.10
  57.5 1.2 collective-permute-done.10.got_core
  58.6 1.1 collective-permute-start.11
  59.7 3.7 %collective-permute-done.11.got_z = bf16[512,128]{1,0:T(8,128)(2,1)S(1)} collective-permute-done((bf16[512,128]{1,0:T(8,128)(2,1)S(1)}, bf16[512,128]{1,0:T(8,128)(2,1)S(1)}, u32[]{:S(2)}, u32[]{:S(2)}) %collective-permute-start.11) | collective-permute-done | bytes 131104 | tf_op jit(solution)/shard_map/ppermute | solution.py:441
  63.4 1.1 shard_map.98
  64.6 1.1 collective-permute-start.12
  65.6 1.5 %collective-permute-start.13 = (bf16[512,128]{1,0:T(8,128)(2,1)S(1)}, bf16[512,128]{1,0:T(8,128)(2,1)S(1)}, u32[]{:S(2)}, u32[]{:S(2)}) collective-permute-start(bf16[512,128]{1,0:T(8,128)(2,1)S(1)} %get-tuple-element.50.g0), channel_id=1, source_target_pairs={{0,4},{4,0},{1,5},{5,1},{2,6},{6,2},{3,7},{7,3},{8,12},{12,8},{9,1... | collective-permute-start | bytes 393224 | tf_op jit(solution)/shard_map/ppermute | solution.py:451
  67.1 1.4 collective-permute-done.12.g1
  68.5 2.3 %collective-permute-start.14 = (bf16[512,128]{1,0:T(8,128)(2,1)S(1)}, bf16[512,128]{1,0:T(8,128)(2,1)S(1)}, u32[]{:S(2)}, u32[]{:S(2)}) collective-permute-start(bf16[512,128]{1,0:T(8,128)(2,1)S(1)} %collective-permute-done.12.g1), channel_id=1, source_target_pairs={{0,4},{4,0},{1,5},{5,1},{2,6},{6,2},{3,7},{7,3},{8,12},{12,8},{9,1... | collective-permute-start | bytes 393224 | tf_op jit(solution)/shard_map/ppermute | solution.py:451
  70.8 1.0 collective-permute-done.14.g3
  71.8 3.5 %shard_map.99 = (f32[512,256]{1,0:T(8,128)S(1)}, bf16[512,256]{1,0:T(8,128)(2,1)S(1)}, bf16[512,256]{1,0:T(8,128)(2,1)S(1)}, bf16[512,256]{1,0:T(8,128)(2,1)S(1)...) custom-call(s32[8]{0:T(128)S(1)} %concatenate.3.meta_ref, s32[128]{0:T(128)S(1)} %shard_map.95._.list_ref, ...), custom_call_target="tpu_custom_call" | custom-call | flops 2013265920 | bytes 5243424 | tf_op jit(solution)/shard_map/pallas_call | solution.py:73
  75.5 7.6 %collective-permute-start.15 = (bf16[512,256]{1,0:T(8,128)(2,1)S(1)}, bf16[512,256]{1,0:T(8,128)(2,1)S(1)}, u32[]{:S(2)}, u32[]{:S(2)}) collective-permute-start(bf16[512,256]{1,0:T(8,128)(2,1)S(1)} %get-tuple-element.52), channel_id=1, source_target_pairs={{0,128},{8,136},{128,0},{136,8},{1,129},{9,137},{129,1},{137,9},{2... | collective-permute-start | bytes 786440 | tf_op jit(solution)/shard_map/ppermute | solution.py:470
  83.1 2.3 %collective-permute-start.16 = (bf16[512,256]{1,0:T(8,128)(2,1)S(1)}, bf16[512,256]{1,0:T(8,128)(2,1)S(1)}, u32[]{:S(2)}, u32[]{:S(2)}) collective-permute-start(bf16[512,256]{1,0:T(8,128)(2,1)S(1)} %get-tuple-element.53), channel_id=1, source_target_pairs={{0,8},{8,0},{128,136},{136,128},{1,9},{9,1},{129,137},{137,129},{2... | collective-permute-start | bytes 786440 | tf_op jit(solution)/shard_map/ppermute | solution.py:468
  86.3 3.1 %collective-permute-done.15.r2 = bf16[512,256]{1,0:T(8,128)(2,1)S(1)} collective-permute-done((bf16[512,256]{1,0:T(8,128)(2,1)S(1)}, bf16[512,256]{1,0:T(8,128)(2,1)S(1)}, u32[]{:S(2)}, u32[]{:S(2)}) %collective-permute-start.15) | collective-permute-done | bytes 262176 | tf_op jit(solution)/shard_map/ppermute | solution.py:470
  89.4 7.6 %collective-permute-done.16.r1 = bf16[512,256]{1,0:T(8,128)(2,1)S(1)} collective-permute-done((bf16[512,256]{1,0:T(8,128)(2,1)S(1)}, bf16[512,256]{1,0:T(8,128)(2,1)S(1)}, u32[]{:S(2)}, u32[]{:S(2)}) %collective-permute-start.16) | collective-permute-done | bytes 262176 | tf_op jit(solution)/shard_map/ppermute | solution.py:468
  97.0 1.7 %shard_map.101 = (f32[512,128]{1,0:T(8,128)S(1)}, bf16[512,128]{1,0:T(8,128)(2,1)S(1)}, bf16[512,128]{1,0:T(8,128)(2,1)S(1)}, bf16[512,128]{1,0:T(8,128)(2,1)S(1...) custom-call(s32[8]{0:T(128)S(1)} %concatenate.3.meta_ref, f32[512,256]{1,0:T(8,128)S(1)} %get-tuple-element.51.own, ...), custom_call_target="tpu_custom_call" | custom-call | flops 536870912 | bytes 6357024 | tf_op jit(solution)/shard_map/pallas_call | solution.py:73
  98.7 1.3 collective-permute-start.20
  100.0 1.3 collective-permute-done.20.got
  102.7 2.3 %collective-permute-start.22 = (bf16[80,512]{1,0:T(8,128)(2,1)S(1)}, bf16[80,512]{1,0:T(8,128)(2,1)S(1)}, u32[]{:S(2)}, u32[]{:S(2)}) collective-permute-start(bf16[80,512]{1,0:T(8,128)(2,1)S(1)} %get-tuple-element.64), channel_id=1, source_target_pairs={{0,8},{8,0},{128,136},{136,128},{1,9},{9,1},{129,137},{137,129},{2... | collective-permute-start | bytes 245768 | tf_op jit(solution)/shard_map/ppermute | solution.py:491
  105.3 1.9 %collective-permute-done.21.p1 = bf16[80,512]{1,0:T(8,128)(2,1)S(1)} collective-permute-done((bf16[80,512]{1,0:T(8,128)(2,1)S(1)}, bf16[80,512]{1,0:T(8,128)(2,1)S(1)}, u32[]{:S(2)}, u32[]{:S(2)}) %collective-permute-start.21) | collective-permute-done | bytes 81952 | tf_op jit(solution)/shard_map/ppermute | solution.py:491
  107.2 1.7 %collective-permute-done.22.p2 = bf16[80,512]{1,0:T(8,128)(2,1)S(1)} collective-permute-done((bf16[80,512]{1,0:T(8,128)(2,1)S(1)}, bf16[80,512]{1,0:T(8,128)(2,1)S(1)}, u32[]{:S(2)}, u32[]{:S(2)}) %collective-permute-start.22) | collective-permute-done | bytes 81952 | tf_op jit(solution)/shard_map/ppermute | solution.py:491
  109.6 1.6 %collective-permute-start.26 = (bf16[512,128]{1,0:T(8,128)(2,1)S(1)}, bf16[512,128]{1,0:T(8,128)(2,1)S(1)}, u32[]{:S(2)}, u32[]{:S(2)}) collective-permute-start(bf16[512,128]{1,0:T(8,128)(2,1)S(1)} %get-tuple-element.71), channel_id=1, source_target_pairs={{0,1},{1,0},{2,3},{3,2},{4,5},{5,4},{6,7},{7,6},{8,9},{9,8},{10,11... | collective-permute-start | bytes 393224 | tf_op jit(solution)/shard_map/ppermute | solution.py:496
  111.2 2.5 %collective-permute-start.27 = (bf16[512,128]{1,0:T(8,128)(2,1)S(1)}, bf16[512,128]{1,0:T(8,128)(2,1)S(1)}, u32[]{:S(2)}, u32[]{:S(2)}) collective-permute-start(bf16[512,128]{1,0:T(8,128)(2,1)S(1)} %get-tuple-element.72), channel_id=1, source_target_pairs={{0,2},{1,3},{2,0},{3,1},{4,6},{5,7},{6,4},{7,5},{8,10},{9,11},{10,... | collective-permute-start | bytes 393224 | tf_op jit(solution)/shard_map/ppermute | solution.py:496
  113.8 3.1 %collective-permute-done.24 = bf16[80,512]{1,0:T(8,128)(2,1)S(1)} collective-permute-done((bf16[80,512]{1,0:T(8,128)(2,1)S(1)}, bf16[80,512]{1,0:T(8,128)(2,1)S(1)}, u32[]{:S(2)}, u32[]{:S(2)}) %collective-permute-start.24) | collective-permute-done | bytes 81952 | tf_op jit(solution)/shard_map/ppermute | solution.py:497
  116.9 1.8 %collective-permute-start.25 = (bf16[80,512]{1,0:T(8,128)(2,1)S(1)}, bf16[80,512]{1,0:T(8,128)(2,1)S(1)}, u32[]{:S(2)}, u32[]{:S(2)}) collective-permute-start(bf16[80,512]{1,0:T(8,128)(2,1)S(1)} %add_convert_fusion.3.a), channel_id=1, source_target_pairs={{0,32},{32,0},{1,33},{33,1},{2,34},{34,2},{3,35},{35,3},{4,36},{36... | collective-permute-start | bytes 245768 | tf_op jit(solution)/shard_map/ppermute | solution.py:499
  119.2 3.1 %collective-permute-done.25.b = bf16[80,512]{1,0:T(8,128)(2,1)S(1)} collective-permute-done((bf16[80,512]{1,0:T(8,128)(2,1)S(1)}, bf16[80,512]{1,0:T(8,128)(2,1)S(1)}, u32[]{:S(2)}, u32[]{:S(2)}) %collective-permute-start.25) | collective-permute-done | bytes 81952 | tf_op jit(solution)/shard_map/ppermute | solution.py:499
  122.5 8.1 %collective-permute-start.33 = (bf16[512,128]{1,0:T(8,128)(2,1)S(1)}, bf16[512,128]{1,0:T(8,128)(2,1)S(1)}, u32[]{:S(2)}, u32[]{:S(2)}) collective-permute-start(bf16[512,128]{1,0:T(8,128)(2,1)S(1)} %get-tuple-element.75), channel_id=1, source_target_pairs={{0,0},{64,4},{32,8},{96,12},{24,16},{88,20},{56,24},{120,28},{12,3... | collective-permute-start | bytes 393224 | tf_op jit(solution)/shard_map/ppermute | solution.py:505
  130.7 0.9 collective-permute-start.32
  131.5 2.1 %collective-permute-start.31 = (bf16[80,512]{1,0:T(8,128)(2,1)S(1)}, bf16[80,512]{1,0:T(8,128)(2,1)S(1)}, u32[]{:S(2)}, u32[]{:S(2)}) collective-permute-start(bf16[80,512]{1,0:T(8,128)(2,1)S(1)} %add_convert_fusion.2.p0), channel_id=1, source_target_pairs={{0,136},{8,128},{128,8},{136,0},{1,137},{9,129},{129,9},{137,1},{2... | collective-permute-start | bytes 245768 | tf_op jit(solution)/shard_map/ppermute | solution.py:508
  133.7 5.2 %collective-permute-done.32.p2 = bf16[80,512]{1,0:T(8,128)(2,1)S(1)} collective-permute-done((bf16[80,512]{1,0:T(8,128)(2,1)S(1)}, bf16[80,512]{1,0:T(8,128)(2,1)S(1)}, u32[]{:S(2)}, u32[]{:S(2)}) %collective-permute-start.32) | collective-permute-done | bytes 81952 | tf_op jit(solution)/shard_map/ppermute | solution.py:508
  139.5 0.9 collective-permute-start.34
  140.4 1.3 collective-permute-done.34.other
  141.6 1.7 %shard_map.106 = (f32[512,512]{1,0:T(8,128)}, f32[128,512]{1,0:T(8,128)}, bf16[1,512,128]{2,1,0:T(8,128)(2,1)}) custom-call(s32[8]{0:T(128)S(1)} %concatenate.3.meta_ref, bf16[320,512]{1,0:T(8,128)(2,1)S(1)} %shard_map.105.mine, bf16[320,512]{1,0:T(8,128)(2,1)S(1)} %collective-permute-done.34.other, bf16[512,128]{1,0:T(8,128)(2,1)S(1)} %collective-permute-done.33._.grad), custom_call_target="tpu_custom_call" | custom-call | bytes 2228256 | tf_op jit(solution)/shard_map/pallas_call | solution.py:73
  (49 shorter events, 6.9 us)
Async XLA Ops:
  0.6 28.4 %copy-start = (bf16[512,512]{1,0:T(8,128)(2,1)S(1)}, bf16[512,512]{1,0:T(8,128)(2,1)}, u32[]{:S(2)}) copy-start(bf16[512,512]{1,0:T(8,128)(2,1)} %w.1) | copy-start | bytes 1572868
  2.4 16.3 %collective-permute-start = (bf16[272,512]{1,0:T(8,128)(2,1)}, bf16[272,512]{1,0:T(8,128)(2,1)S(1)}, u32[]{:S(2)}, u32[]{:S(2)}) collective-permute-start(bf16[272,512]{1,0:T(8,128)(2,1)} %shard_map.94), channel_id=1, source_target_pairs={{0,0},{4,64},{8,32},{12,96},{16,24},{20,88},{24,56},{28,120},{32,1... | collective-permute-start | bytes 835592 | tf_op jit(solution)/shard_map/ppermute | solution.py:399
  18.8 8.0 %collective-permute-start.3 = (bf16[272,512]{1,0:T(8,128)(2,1)S(1)}, bf16[272,512]{1,0:T(8,128)(2,1)S(1)}, u32[]{:S(2)}, u32[]{:S(2)}) collective-permute-start(bf16[272,512]{1,0:T(8,128)(2,1)S(1)} %collective-permute-done.xa_ref.up0), channel_id=1, source_target_pairs={{0,2},{1,3},{2,0},{3,1},{4,6},{5,7},{6,4},{7,5},{8,10},{9,11},{10,... | collective-permute-start | bytes 835592 | tf_op jit(solution)/shard_map/ppermute | solution.py:402
  21.7 7.0 %collective-permute-start.2 = (bf16[272,512]{1,0:T(8,128)(2,1)S(1)}, bf16[272,512]{1,0:T(8,128)(2,1)S(1)}, u32[]{:S(2)}, u32[]{:S(2)}) collective-permute-start(bf16[272,512]{1,0:T(8,128)(2,1)S(1)} %collective-permute-done.xa_ref.up0), channel_id=1, source_target_pairs={{0,3},{1,2},{2,1},{3,0},{4,7},{5,6},{6,5},{7,4},{8,11},{9,10},{10,... | collective-permute-start | bytes 835592 | tf_op jit(solution)/shard_map/ppermute | solution.py:402
  22.4 6.6 %collective-permute-start.1 = (bf16[272,512]{1,0:T(8,128)(2,1)S(1)}, bf16[272,512]{1,0:T(8,128)(2,1)S(1)}, u32[]{:S(2)}, u32[]{:S(2)}) collective-permute-start(bf16[272,512]{1,0:T(8,128)(2,1)S(1)} %collective-permute-done.xa_ref.up0), channel_id=1, source_target_pairs={{0,1},{1,0},{2,3},{3,2},{4,5},{5,4},{6,7},{7,6},{8,9},{9,8},{10,11... | collective-permute-start | bytes 835592 | tf_op jit(solution)/shard_map/ppermute | solution.py:402
  25.1 3.9 %copy-start.2 = (f32[1,128]{1,0:T(1,128)S(1)}, f32[1,128]{1,0:T(1,128)}, u32[]{:S(2)}) copy-start(f32[1,128]{1,0:T(1,128)} %table_ref.1) | copy-start | bytes 1540
  30.3 12.9 %collective-permute-start.7 = (bf16[512,256]{1,0:T(8,128)(2,1)S(1)}, bf16[512,256]{1,0:T(8,128)(2,1)S(1)}, u32[]{:S(2)}, u32[]{:S(2)}) collective-permute-start(bf16[512,256]{1,0:T(8,128)(2,1)S(1)} %get-tuple-element.42.q0), channel_id=1, source_target_pairs={{0,16},{16,0},{1,17},{17,1},{2,18},{18,2},{3,19},{19,3},{4,20},{20... | collective-permute-start | bytes 786440 | tf_op jit(solution)/shard_map/ppermute | solution.py:422
  34.4 10.0 %collective-permute-start.6 = (bf16[528,256]{1,0:T(8,128)(2,1)S(1)}, bf16[528,256]{1,0:T(8,128)(2,1)S(1)}, u32[]{:S(2)}, u32[]{:S(2)}) collective-permute-start(bf16[528,256]{1,0:T(8,128)(2,1)S(1)} %get-tuple-element.41.kv0), channel_id=1, source_target_pairs={{0,128},{8,136},{128,0},{136,8},{1,129},{9,137},{129,1},{137,9},{2... | collective-permute-start | bytes 811016 | tf_op jit(solution)/shard_map/ppermute | solution.py:420
  36.6 17.4 %collective-permute-start.5 = (bf16[528,256]{1,0:T(8,128)(2,1)S(1)}, bf16[528,256]{1,0:T(8,128)(2,1)S(1)}, u32[]{:S(2)}, u32[]{:S(2)}) collective-permute-start(bf16[528,256]{1,0:T(8,128)(2,1)S(1)} %get-tuple-element.41.kv0), channel_id=1, source_target_pairs={{0,136},{8,128},{128,8},{136,0},{1,137},{9,129},{129,9},{137,1},{2... | collective-permute-start | bytes 811016 | tf_op jit(solution)/shard_map/ppermute | solution.py:420
  42.3 12.0 %collective-permute-start.4 = (bf16[528,256]{1,0:T(8,128)(2,1)S(1)}, bf16[528,256]{1,0:T(8,128)(2,1)S(1)}, u32[]{:S(2)}, u32[]{:S(2)}) collective-permute-start(bf16[528,256]{1,0:T(8,128)(2,1)S(1)} %get-tuple-element.41.kv0), channel_id=1, source_target_pairs={{0,8},{8,0},{128,136},{136,128},{1,9},{9,1},{129,137},{137,129},{2... | collective-permute-start | bytes 811016 | tf_op jit(solution)/shard_map/ppermute | solution.py:420
  42.4 2.0 %collective-permute-start.8 = (bf16[512,256]{1,0:T(8,128)(2,1)S(1)}, bf16[512,256]{1,0:T(8,128)(2,1)S(1)}, u32[]{:S(2)}, u32[]{:S(2)}) collective-permute-start(bf16[512,256]{1,0:T(8,128)(2,1)S(1)} %get-tuple-element.42.q0), channel_id=1, source_target_pairs={{0,4},{4,0},{1,5},{5,1},{2,6},{6,2},{3,7},{7,3},{8,12},{12,8},{9,1... | collective-permute-start | bytes 786440 | tf_op jit(solution)/shard_map/ppermute | solution.py:423
  43.2 11.1 %collective-permute-start.9 = (bf16[512,256]{1,0:T(8,128)(2,1)S(1)}, bf16[512,256]{1,0:T(8,128)(2,1)S(1)}, u32[]{:S(2)}, u32[]{:S(2)}) collective-permute-start(bf16[512,256]{1,0:T(8,128)(2,1)S(1)} %collective-permute-done.7.q1), channel_id=1, source_target_pairs={{0,4},{4,0},{1,5},{5,1},{2,6},{6,2},{3,7},{7,3},{8,12},{12,8},{9,1... | collective-permute-start | bytes 786440 | tf_op jit(solution)/shard_map/ppermute | solution.py:423
  56.5 2.1 %collective-permute-start.10 = (bf16[1024,128]{1,0:T(8,128)(2,1)S(1)}, bf16[1024,128]{1,0:T(8,128)(2,1)S(1)}, u32[]{:S(2)}, u32[]{:S(2)}) collective-permute-start(bf16[1024,128]{1,0:T(8,128)(2,1)S(1)} %get-tuple-element.47), channel_id=1, source_target_pairs={{0,4},{4,0},{1,5},{5,1},{2,6},{6,2},{3,7},{7,3},{8,12},{12,8},{9,1... | collective-permute-start | bytes 786440 | tf_op jit(solution)/shard_map/ppermute | solution.py:439
  58.6 4.8 %copy-start.1 = (bf16[128,512]{1,0:T(8,128)(2,1)S(1)}, bf16[128,512]{1,0:T(8,128)(2,1)}, u32[]{:S(2)}) copy-start(bf16[128,512]{1,0:T(8,128)(2,1)} %wout.1) | copy-start | bytes 393220
  58.6 4.8 %collective-permute-start.11 = (bf16[512,128]{1,0:T(8,128)(2,1)S(1)}, bf16[512,128]{1,0:T(8,128)(2,1)S(1)}, u32[]{:S(2)}, u32[]{:S(2)}) collective-permute-start(bf16[512,128]{1,0:T(8,128)(2,1)S(1)} %add_convert_fusion.1), channel_id=1, source_target_pairs={{0,16},{16,0},{1,17},{17,1},{2,18},{18,2},{3,19},{19,3},{4,20},{20... | collective-permute-start | bytes 393224 | tf_op jit(solution)/shard_map/ppermute | solution.py:441
  64.6 3.9 %collective-permute-start.12 = (bf16[512,128]{1,0:T(8,128)(2,1)S(1)}, bf16[512,128]{1,0:T(8,128)(2,1)S(1)}, u32[]{:S(2)}, u32[]{:S(2)}) collective-permute-start(bf16[512,128]{1,0:T(8,128)(2,1)S(1)} %get-tuple-element.50.g0), channel_id=1, source_target_pairs={{0,16},{16,0},{1,17},{17,1},{2,18},{18,2},{3,19},{19,3},{4,20},{20... | collective-permute-start | bytes 393224 | tf_op jit(solution)/shard_map/ppermute | solution.py:450
  65.6 5.2 %collective-permute-start.13 = (bf16[512,128]{1,0:T(8,128)(2,1)S(1)}, bf16[512,128]{1,0:T(8,128)(2,1)S(1)}, u32[]{:S(2)}, u32[]{:S(2)}) collective-permute-start(bf16[512,128]{1,0:T(8,128)(2,1)S(1)} %get-tuple-element.50.g0), channel_id=1, source_target_pairs={{0,4},{4,0},{1,5},{5,1},{2,6},{6,2},{3,7},{7,3},{8,12},{12,8},{9,1... | collective-permute-start | bytes 393224 | tf_op jit(solution)/shard_map/ppermute | solution.py:451
  68.5 3.3 %collective-permute-start.14 = (bf16[512,128]{1,0:T(8,128)(2,1)S(1)}, bf16[512,128]{1,0:T(8,128)(2,1)S(1)}, u32[]{:S(2)}, u32[]{:S(2)}) collective-permute-start(bf16[512,128]{1,0:T(8,128)(2,1)S(1)} %collective-permute-done.12.g1), channel_id=1, source_target_pairs={{0,4},{4,0},{1,5},{5,1},{2,6},{6,2},{3,7},{7,3},{8,12},{12,8},{9,1... | collective-permute-start | bytes 393224 | tf_op jit(solution)/shard_map/ppermute | solution.py:451
  75.4 10.0 %collective-permute-start.18 = (bf16[1024,128]{1,0:T(8,128)(2,1)S(1)}, bf16[1024,128]{1,0:T(8,128)(2,1)S(1)}, u32[]{:S(2)}, u32[]{:S(2)}) collective-permute-start(bf16[1024,128]{1,0:T(8,128)(2,1)S(1)} %get-tuple-element.56), channel_id=1, source_target_pairs={{0,4},{4,0},{1,5},{5,1},{2,6},{6,2},{3,7},{7,3},{8,12},{12,8},{9,1... | collective-permute-start | bytes 786440 | tf_op jit(solution)/shard_map/ppermute | solution.py:471
  75.5 13.9 %collective-permute-start.15 = (bf16[512,256]{1,0:T(8,128)(2,1)S(1)}, bf16[512,256]{1,0:T(8,128)(2,1)S(1)}, u32[]{:S(2)}, u32[]{:S(2)}) collective-permute-start(bf16[512,256]{1,0:T(8,128)(2,1)S(1)} %get-tuple-element.52), channel_id=1, source_target_pairs={{0,128},{8,136},{128,0},{136,8},{1,129},{9,137},{129,1},{137,9},{2... | collective-permute-start | bytes 786440 | tf_op jit(solution)/shard_map/ppermute | solution.py:470
  83.1 14.0 %collective-permute-start.16 = (bf16[512,256]{1,0:T(8,128)(2,1)S(1)}, bf16[512,256]{1,0:T(8,128)(2,1)S(1)}, u32[]{:S(2)}, u32[]{:S(2)}) collective-permute-start(bf16[512,256]{1,0:T(8,128)(2,1)S(1)} %get-tuple-element.53), channel_id=1, source_target_pairs={{0,8},{8,0},{128,136},{136,128},{1,9},{9,1},{129,137},{137,129},{2... | collective-permute-start | bytes 786440 | tf_op jit(solution)/shard_map/ppermute | solution.py:468
  85.3 11.7 %collective-permute-start.17 = (bf16[512,256]{1,0:T(8,128)(2,1)S(1)}, bf16[512,256]{1,0:T(8,128)(2,1)S(1)}, u32[]{:S(2)}, u32[]{:S(2)}) collective-permute-start(bf16[512,256]{1,0:T(8,128)(2,1)S(1)} %get-tuple-element.54), channel_id=1, source_target_pairs={{0,136},{8,128},{128,8},{136,0},{1,137},{9,129},{129,9},{137,1},{2... | collective-permute-start | bytes 786440 | tf_op jit(solution)/shard_map/ppermute | solution.py:469
  85.4 11.6 %collective-permute-start.19 = (bf16[512,128]{1,0:T(8,128)(2,1)S(1)}, bf16[512,128]{1,0:T(8,128)(2,1)S(1)}, u32[]{:S(2)}, u32[]{:S(2)}) collective-permute-start(bf16[512,128]{1,0:T(8,128)(2,1)S(1)} %add_convert_fusion), channel_id=1, source_target_pairs={{0,16},{16,0},{1,17},{17,1},{2,18},{18,2},{3,19},{19,3},{4,20},{20... | collective-permute-start | bytes 393224 | tf_op jit(solution)/shard_map/ppermute | solution.py:473
  98.7 2.6 %collective-permute-start.20 = (bf16[320,512]{1,0:T(8,128)(2,1)S(1)}, bf16[320,512]{1,0:T(8,128)(2,1)S(1)}, u32[]{:S(2)}, u32[]{:S(2)}) collective-permute-start(bf16[320,512]{1,0:T(8,128)(2,1)S(1)} %get-tuple-element.61), channel_id=1, source_target_pairs={{0,4},{4,0},{1,5},{5,1},{2,6},{6,2},{3,7},{7,3},{8,12},{12,8},{9,1... | collective-permute-start | bytes 983048 | tf_op jit(solution)/shard_map/ppermute | solution.py:483
  101.9 5.2 %collective-permute-start.21 = (bf16[80,512]{1,0:T(8,128)(2,1)S(1)}, bf16[80,512]{1,0:T(8,128)(2,1)S(1)}, u32[]{:S(2)}, u32[]{:S(2)}) collective-permute-start(bf16[80,512]{1,0:T(8,128)(2,1)S(1)} %get-tuple-element.63), channel_id=1, source_target_pairs={{0,128},{8,136},{128,0},{136,8},{1,129},{9,137},{129,1},{137,9},{2... | collective-permute-start | bytes 245768 | tf_op jit(solution)/shard_map/ppermute | solution.py:491
  102.7 6.2 %collective-permute-start.22 = (bf16[80,512]{1,0:T(8,128)(2,1)S(1)}, bf16[80,512]{1,0:T(8,128)(2,1)S(1)}, u32[]{:S(2)}, u32[]{:S(2)}) collective-permute-start(bf16[80,512]{1,0:T(8,128)(2,1)S(1)} %get-tuple-element.64), channel_id=1, source_target_pairs={{0,8},{8,0},{128,136},{136,128},{1,9},{9,1},{129,137},{137,129},{2... | collective-permute-start | bytes 245768 | tf_op jit(solution)/shard_map/ppermute | solution.py:491
  105.0 4.5 %collective-permute-start.23 = (bf16[80,512]{1,0:T(8,128)(2,1)S(1)}, bf16[80,512]{1,0:T(8,128)(2,1)S(1)}, u32[]{:S(2)}, u32[]{:S(2)}) collective-permute-start(bf16[80,512]{1,0:T(8,128)(2,1)S(1)} %get-tuple-element.65), channel_id=1, source_target_pairs={{0,136},{8,128},{128,8},{136,0},{1,137},{9,129},{129,9},{137,1},{2... | collective-permute-start | bytes 245768 | tf_op jit(solution)/shard_map/ppermute | solution.py:491
  109.5 7.4 %collective-permute-start.24 = (bf16[80,512]{1,0:T(8,128)(2,1)S(1)}, bf16[80,512]{1,0:T(8,128)(2,1)S(1)}, u32[]{:S(2)}, u32[]{:S(2)}) collective-permute-start(bf16[80,512]{1,0:T(8,128)(2,1)S(1)} %get-tuple-element.69), channel_id=1, source_target_pairs={{0,64},{64,0},{1,65},{65,1},{2,66},{66,2},{3,67},{67,3},{4,68},{68... | collective-permute-start | bytes 245768 | tf_op jit(solution)/shard_map/ppermute | solution.py:497
  109.6 9.1 %collective-permute-start.26 = (bf16[512,128]{1,0:T(8,128)(2,1)S(1)}, bf16[512,128]{1,0:T(8,128)(2,1)S(1)}, u32[]{:S(2)}, u32[]{:S(2)}) collective-permute-start(bf16[512,128]{1,0:T(8,128)(2,1)S(1)} %get-tuple-element.71), channel_id=1, source_target_pairs={{0,1},{1,0},{2,3},{3,2},{4,5},{5,4},{6,7},{7,6},{8,9},{9,8},{10,11... | collective-permute-start | bytes 393224 | tf_op jit(solution)/shard_map/ppermute | solution.py:496
  111.2 7.5 %collective-permute-start.27 = (bf16[512,128]{1,0:T(8,128)(2,1)S(1)}, bf16[512,128]{1,0:T(8,128)(2,1)S(1)}, u32[]{:S(2)}, u32[]{:S(2)}) collective-permute-start(bf16[512,128]{1,0:T(8,128)(2,1)S(1)} %get-tuple-element.72), channel_id=1, source_target_pairs={{0,2},{1,3},{2,0},{3,1},{4,6},{5,7},{6,4},{7,5},{8,10},{9,11},{10,... | collective-permute-start | bytes 393224 | tf_op jit(solution)/shard_map/ppermute | solution.py:496
  113.8 5.5 %collective-permute-start.28 = (bf16[512,128]{1,0:T(8,128)(2,1)S(1)}, bf16[512,128]{1,0:T(8,128)(2,1)S(1)}, u32[]{:S(2)}, u32[]{:S(2)}) collective-permute-start(bf16[512,128]{1,0:T(8,128)(2,1)S(1)} %get-tuple-element.73), channel_id=1, source_target_pairs={{0,3},{1,2},{2,1},{3,0},{4,7},{5,6},{6,5},{7,4},{8,11},{9,10},{10,... | collective-permute-start | bytes 393224 | tf_op jit(solution)/shard_map/ppermute | solution.py:496
  116.9 5.5 %collective-permute-start.25 = (bf16[80,512]{1,0:T(8,128)(2,1)S(1)}, bf16[80,512]{1,0:T(8,128)(2,1)S(1)}, u32[]{:S(2)}, u32[]{:S(2)}) collective-permute-start(bf16[80,512]{1,0:T(8,128)(2,1)S(1)} %add_convert_fusion.3.a), channel_id=1, source_target_pairs={{0,32},{32,0},{1,33},{33,1},{2,34},{34,2},{3,35},{35,3},{4,36},{36... | collective-permute-start | bytes 245768 | tf_op jit(solution)/shard_map/ppermute | solution.py:499
  122.4 8.2 %collective-permute-start.29 = (bf16[80,512]{1,0:T(8,128)(2,1)S(1)}, bf16[80,512]{1,0:T(8,128)(2,1)S(1)}, u32[]{:S(2)}, u32[]{:S(2)}) collective-permute-start(bf16[80,512]{1,0:T(8,128)(2,1)S(1)} %get-tuple-element.74), channel_id=1, source_target_pairs={{0,16},{16,0},{1,17},{17,1},{2,18},{18,2},{3,19},{19,3},{4,20},{20... | collective-permute-start | bytes 245768 | tf_op jit(solution)/shard_map/ppermute | solution.py:506
  122.5 11.1 %collective-permute-start.33 = (bf16[512,128]{1,0:T(8,128)(2,1)S(1)}, bf16[512,128]{1,0:T(8,128)(2,1)S(1)}, u32[]{:S(2)}, u32[]{:S(2)}) collective-permute-start(bf16[512,128]{1,0:T(8,128)(2,1)S(1)} %get-tuple-element.75), channel_id=1, source_target_pairs={{0,0},{64,4},{32,8},{96,12},{24,16},{88,20},{56,24},{120,28},{12,3... | collective-permute-start | bytes 393224 | tf_op jit(solution)/shard_map/ppermute | solution.py:505
  130.7 8.2 %collective-permute-start.32 = (bf16[80,512]{1,0:T(8,128)(2,1)S(1)}, bf16[80,512]{1,0:T(8,128)(2,1)S(1)}, u32[]{:S(2)}, u32[]{:S(2)}) collective-permute-start(bf16[80,512]{1,0:T(8,128)(2,1)S(1)} %add_convert_fusion.2.p0), channel_id=1, source_target_pairs={{0,128},{8,136},{128,0},{136,8},{1,129},{9,137},{129,1},{137,9},{2... | collective-permute-start | bytes 245768 | tf_op jit(solution)/shard_map/ppermute | solution.py:508
  131.5 7.4 %collective-permute-start.31 = (bf16[80,512]{1,0:T(8,128)(2,1)S(1)}, bf16[80,512]{1,0:T(8,128)(2,1)S(1)}, u32[]{:S(2)}, u32[]{:S(2)}) collective-permute-start(bf16[80,512]{1,0:T(8,128)(2,1)S(1)} %add_convert_fusion.2.p0), channel_id=1, source_target_pairs={{0,136},{8,128},{128,8},{136,0},{1,137},{9,129},{129,9},{137,1},{2... | collective-permute-start | bytes 245768 | tf_op jit(solution)/shard_map/ppermute | solution.py:508
  133.6 5.2 %collective-permute-start.30 = (bf16[80,512]{1,0:T(8,128)(2,1)S(1)}, bf16[80,512]{1,0:T(8,128)(2,1)S(1)}, u32[]{:S(2)}, u32[]{:S(2)}) collective-permute-start(bf16[80,512]{1,0:T(8,128)(2,1)S(1)} %add_convert_fusion.2.p0), channel_id=1, source_target_pairs={{0,8},{8,0},{128,136},{136,128},{1,9},{9,1},{129,137},{137,129},{2... | collective-permute-start | bytes 245768 | tf_op jit(solution)/shard_map/ppermute | solution.py:508
  139.5 2.2 %collective-permute-start.34 = (bf16[320,512]{1,0:T(8,128)(2,1)S(1)}, bf16[320,512]{1,0:T(8,128)(2,1)S(1)}, u32[]{:S(2)}, u32[]{:S(2)}) collective-permute-start(bf16[320,512]{1,0:T(8,128)(2,1)S(1)} %shard_map.105.mine), channel_id=1, source_target_pairs={{0,4},{4,0},{1,5},{5,1},{2,6},{6,2},{3,7},{7,3},{8,12},{12,8},{9,1... | collective-permute-start | bytes 983048 | tf_op jit(solution)/shard_map/ppermute | solution.py:510

commit v4 on v3

--- a/solution.py
+++ b/solution.py
@@ -109,7 +109,7 @@
 
 
 def project_kernel(
-    _, xa_ref, x1, x3, x2, w_ref, table_ref, kv_ref, q_ref, gate_ref, slope_ref, x_ref
+    _, xa_ref, x1, x2, x3, w_ref, table_ref, kv_ref, q_ref, gate_ref, slope_ref, x_ref
 ):
     y = lax.axis_index("y")
     for rel, piece in enumerate((xa_ref, x1, x2, x3)):
@@ -414,7 +414,7 @@
         project_kernel,
         [((ROWS + 16, 2 * DH), BF), ((ROWS, 2 * DH), BF), ((ROWS, DH), BF), ((ROWS, WIDTH), F32)]
         + [((ROWS, WIDTH), BF)],
-        (pairs, xa, x1, x3, x2, weight_in, time_table),
+        (pairs, xa, x1, x2, x3, weight_in, time_table),
         flops=2 * ROWS * WIDTH * WIDTH,
     )
     kvs = [kv] + [lax.ppermute(kv, ("xh", "xl"), flip_x(rel)) for rel in (1, 3, 2)]

time: 145 us -> 144 us (level); the launches traced: 143 us -> 144 us
  starting transfers between devices: 67.1 us -> 72.3 us
  waiting for transfers between devices: 56 us -> 51.4 us
    ppermute x1, starting transfers between devices: 7.59 us -> 1.08 us  [body(): r2 = lax.ppermute(s2, ('xh', 'xl'), flip_x(2))]
    ppermute x1, starting transfers between devices: 1.79 us -> 7.31 us  [body(): other = lax.ppermute(total, 'z1', FLIP)]
    ppermute x1, starting transfers between devices: 0.09 us -> 3.26 us  [body(): other = lax.ppermute(total, 'z2', FLIP)]
    ppermute x1, waiting for transfers between devices: 3.09 us -> 0.01 us  [body(): other = lax.ppermute(total, 'z2', FLIP)]
    ppermute x1, waiting for transfers between devices: 7.63 us -> 5.58 us  [body(): r1 = lax.ppermute(s1, ('xh', 'xl'), flip_x(1))]
    ppermute x1, waiting for transfers between devices: 3.11 us -> 5.13 us  [body(): r2 = lax.ppermute(s2, ('xh', 'xl'), flip_x(2))]
    ppermute x1, starting transfers between devices: 0.9 us -> 2.46 us  [body(): other_half = lax.ppermute(mine_half, 'core', FLIP)]
where the time goes in v4:
time: 144 us
  starting transfers between devices  72.3 us (50%)
  waiting for transfers between devices  51.4 us (36%)
  Pallas kernels  16.6 us (12%)
  between operations  2.13 us (1%)
    pallas_call x13, Pallas kernels, call(): pl.pallas_call(kernel, out_shape=[jax.ShapeDtypeStruct(s, t) for s, t in...  16.6 us
    ppermute x1, starting transfers between devices, body(): xa = lax.ppermute(xa, MOVED, AWAY)  10.2 us
    ppermute x3, waiting for transfers between devices, body(): lax.ppermute(kv, ('xh', 'xl'), flip_x(rel))  9.92 us
    ppermute x1, starting transfers between devices, body(): grad_local = lax.ppermute(grad_local, MOVED, HOME)  9.34 us
    ppermute x3, starting transfers between devices, body(): lax.ppermute(kv, ('xh', 'xl'), flip_x(rel))  8.1 us
    ppermute x1, starting transfers between devices, body(): other = lax.ppermute(total, 'z1', FLIP)  7.31 us
    ppermute x1, waiting for transfers between devices, body(): xa = lax.ppermute(xa, MOVED, AWAY)  6.08 us
    ppermute x1, waiting for transfers between devices, body(): r1 = lax.ppermute(s1, ('xh', 'xl'), flip_x(1))  5.58 us
  transfers between devices with their start and end apart: 35, of which 21 were waited for; matrix products, arithmetic and copies ran while one was open for 1% of the time, Pallas kernels for 1%

profile of v4, /device:TPU:1, one launch (start us, length us, event | category | flops | bytes accessed | tf_op | source)
XLA Modules:
  0.0 143.8 jit_solution(5076030916154071842)
XLA Ops:
  0.6 1.8 %shard_map.94 = bf16[272,512]{1,0:T(8,128)(2,1)} custom-call(bf16[512,512]{1,0:T(8,128)(2,1)} %bitcast.8, s32[1,512]{1,0:T(1,128)} %times_hbm.1, s32[1,3]{1,0:T(1,128)} %lengths_hbm.1, bf16[512,512]{1,0:T(8,128)(2,1)} %bitcast.9), custom_call_target="tpu_custom_call" | custom-call | bytes 1329164 | tf_op jit(solution)/shard_map/pallas_call | solution.py:73
  2.4 10.2 %collective-permute-start = (bf16[272,512]{1,0:T(8,128)(2,1)}, bf16[272,512]{1,0:T(8,128)(2,1)S(1)}, u32[]{:S(2)}, u32[]{:S(2)}) collective-permute-start(bf16[272,512]{1,0:T(8,128)(2,1)} %shard_map.94), channel_id=1, source_target_pairs={{0,0},{4,64},{8,32},{12,96},{16,24},{20,88},{24,56},{28,120},{32,1... | collective-permute-start | bytes 835592 | tf_op jit(solution)/shard_map/ppermute | solution.py:399
  12.7 6.1 %collective-permute-done.xa_ref.up0 = bf16[272,512]{1,0:T(8,128)(2,1)S(1)} collective-permute-done((bf16[272,512]{1,0:T(8,128)(2,1)}, bf16[272,512]{1,0:T(8,128)(2,1)S(1)}, u32[]{:S(2)}, u32[]{:S(2)}) %collective-permute-start) | collective-permute-done | bytes 278560 | tf_op jit(solution)/shard_map/ppermute | solution.py:399
  18.8 2.7 %collective-permute-start.3 = (bf16[272,512]{1,0:T(8,128)(2,1)S(1)}, bf16[272,512]{1,0:T(8,128)(2,1)S(1)}, u32[]{:S(2)}, u32[]{:S(2)}) collective-permute-start(bf16[272,512]{1,0:T(8,128)(2,1)S(1)} %collective-permute-done.xa_ref.up0), channel_id=1, source_target_pairs={{0,3},{1,2},{2,1},{3,0},{4,7},{5,6},{6,5},{7,4},{8,11},{9,10},{10,... | collective-permute-start | bytes 835592 | tf_op jit(solution)/shard_map/ppermute | solution.py:402
  24.0 0.7 concatenate.3.meta_ref
  24.7 1.7 %shard_map.95._.list_ref = s32[128]{0:T(128)S(1)} custom-call(s32[8]{0:T(128)S(1)} %concatenate.3.meta_ref), custom_call_target="tpu_custom_call" | custom-call | bytes 544 | tf_op jit(solution)/shard_map/pallas_call | solution.py:73
  26.4 1.6 %collective-permute-done.3.x3.up3 = bf16[272,512]{1,0:T(8,128)(2,1)S(1)} collective-permute-done((bf16[272,512]{1,0:T(8,128)(2,1)S(1)}, bf16[272,512]{1,0:T(8,128)(2,1)S(1)}, u32[]{:S(2)}, u32[]{:S(2)}) %collective-permute-start.3) | collective-permute-done | bytes 278560 | tf_op jit(solution)/shard_map/ppermute | solution.py:402
  28.4 0.6 collective-permute-done.1.x1.up1
  29.0 1.3 shard_map.96
  30.3 4.3 %collective-permute-start.7 = (bf16[512,256]{1,0:T(8,128)(2,1)S(1)}, bf16[512,256]{1,0:T(8,128)(2,1)S(1)}, u32[]{:S(2)}, u32[]{:S(2)}) collective-permute-start(bf16[512,256]{1,0:T(8,128)(2,1)S(1)} %get-tuple-element.42.q0), channel_id=1, source_target_pairs={{0,16},{16,0},{1,17},{17,1},{2,18},{18,2},{3,19},{19,3},{4,20},{20... | collective-permute-start | bytes 786440 | tf_op jit(solution)/shard_map/ppermute | solution.py:422
  34.6 2.2 %collective-permute-start.6 = (bf16[528,256]{1,0:T(8,128)(2,1)S(1)}, bf16[528,256]{1,0:T(8,128)(2,1)S(1)}, u32[]{:S(2)}, u32[]{:S(2)}) collective-permute-start(bf16[528,256]{1,0:T(8,128)(2,1)S(1)} %get-tuple-element.41.kv0), channel_id=1, source_target_pairs={{0,128},{8,136},{128,0},{136,8},{1,129},{9,137},{129,1},{137,9},{2... | collective-permute-start | bytes 811016 | tf_op jit(solution)/shard_map/ppermute | solution.py:420
  36.8 5.8 %collective-permute-start.5 = (bf16[528,256]{1,0:T(8,128)(2,1)S(1)}, bf16[528,256]{1,0:T(8,128)(2,1)S(1)}, u32[]{:S(2)}, u32[]{:S(2)}) collective-permute-start(bf16[528,256]{1,0:T(8,128)(2,1)S(1)} %get-tuple-element.41.kv0), channel_id=1, source_target_pairs={{0,136},{8,128},{128,8},{136,0},{1,137},{9,129},{129,9},{137,1},{2... | collective-permute-start | bytes 811016 | tf_op jit(solution)/shard_map/ppermute | solution.py:420
  42.7 1.0 collective-permute-start.8
  43.7 1.2 collective-permute-done.8.q2
  44.8 9.6 %collective-permute-done.5.kv3 = bf16[528,256]{1,0:T(8,128)(2,1)S(1)} collective-permute-done((bf16[528,256]{1,0:T(8,128)(2,1)S(1)}, bf16[528,256]{1,0:T(8,128)(2,1)S(1)}, u32[]{:S(2)}, u32[]{:S(2)}) %collective-permute-start.5) | collective-permute-done | bytes 270368 | tf_op jit(solution)/shard_map/ppermute | solution.py:420
  54.7 2.2 %shard_map.97 = (f32[1024,128]{1,0:T(8,128)S(1)}, bf16[1024,128]{1,0:T(8,128)(2,1)S(1)}, bf16[8,256,256]{2,1,0:T(8,128)(2,1)S(1)}, bf16[8,256,128]{2,1,0:T(8,128)(2,1)S(1)}, bf16[8,256,256]{2,1,0:T(8,128)(2,1)S(1)}) custom-call(s32[8]{0:T(128)S(1)} %concatenate.3.meta_ref, bf16[528,256]{1,0:T(8,128)(2,1)S(1)} %get-tuple-element.41.kv0, ...), custom_call_target="tpu_custom_call" | custom-call | flops 1006632960 | bytes 5538336 | tf_op jit(solution)/shard_map/pallas_call | solution.py:73
  56.9 1.3 collective-permute-start.10
  58.2 1.2 collective-permute-done.10.got_core
  59.4 1.1 collective-permute-start.11
  60.5 3.7 %collective-permute-done.11.got_z = bf16[512,128]{1,0:T(8,128)(2,1)S(1)} collective-permute-done((bf16[512,128]{1,0:T(8,128)(2,1)S(1)}, bf16[512,128]{1,0:T(8,128)(2,1)S(1)}, u32[]{:S(2)}, u32[]{:S(2)}) %collective-permute-start.11) | collective-permute-done | bytes 131104 | tf_op jit(solution)/shard_map/ppermute | solution.py:441
  64.2 1.1 shard_map.98
  65.4 1.1 collective-permute-start.12
  66.4 1.5 %collective-permute-start.13 = (bf16[512,128]{1,0:T(8,128)(2,1)S(1)}, bf16[512,128]{1,0:T(8,128)(2,1)S(1)}, u32[]{:S(2)}, u32[]{:S(2)}) collective-permute-start(bf16[512,128]{1,0:T(8,128)(2,1)S(1)} %get-tuple-element.50.g0), channel_id=1, source_target_pairs={{0,4},{4,0},{1,5},{5,1},{2,6},{6,2},{3,7},{7,3},{8,12},{12,8},{9,1... | collective-permute-start | bytes 393224 | tf_op jit(solution)/shard_map/ppermute | solution.py:451
  67.9 1.4 collective-permute-done.12.g1
  69.3 2.3 %collective-permute-start.14 = (bf16[512,128]{1,0:T(8,128)(2,1)S(1)}, bf16[512,128]{1,0:T(8,128)(2,1)S(1)}, u32[]{:S(2)}, u32[]{:S(2)}) collective-permute-start(bf16[512,128]{1,0:T(8,128)(2,1)S(1)} %collective-permute-done.12.g1), channel_id=1, source_target_pairs={{0,4},{4,0},{1,5},{5,1},{2,6},{6,2},{3,7},{7,3},{8,12},{12,8},{9,1... | collective-permute-start | bytes 393224 | tf_op jit(solution)/shard_map/ppermute | solution.py:451
  71.6 1.0 collective-permute-done.14.g3
  72.6 3.5 %shard_map.99 = (f32[512,256]{1,0:T(8,128)S(1)}, bf16[512,256]{1,0:T(8,128)(2,1)S(1)}, bf16[512,256]{1,0:T(8,128)(2,1)S(1)}, bf16[512,256]{1,0:T(8,128)(2,1)S(1)...) custom-call(s32[8]{0:T(128)S(1)} %concatenate.3.meta_ref, s32[128]{0:T(128)S(1)} %shard_map.95._.list_ref, ...), custom_call_target="tpu_custom_call" | custom-call | flops 2013265920 | bytes 5243424 | tf_op jit(solution)/shard_map/pallas_call | solution.py:73
  76.6 1.1 collective-permute-start.15
  77.7 1.9 %collective-permute-start.16 = (bf16[512,256]{1,0:T(8,128)(2,1)S(1)}, bf16[512,256]{1,0:T(8,128)(2,1)S(1)}, u32[]{:S(2)}, u32[]{:S(2)}) collective-permute-start(bf16[512,256]{1,0:T(8,128)(2,1)S(1)} %get-tuple-element.53), channel_id=1, source_target_pairs={{0,8},{8,0},{128,136},{136,128},{1,9},{9,1},{129,137},{137,129},{2... | collective-permute-start | bytes 786440 | tf_op jit(solution)/shard_map/ppermute | solution.py:468
  80.8 5.1 %collective-permute-done.15.r2 = bf16[512,256]{1,0:T(8,128)(2,1)S(1)} collective-permute-done((bf16[512,256]{1,0:T(8,128)(2,1)S(1)}, bf16[512,256]{1,0:T(8,128)(2,1)S(1)}, u32[]{:S(2)}, u32[]{:S(2)}) %collective-permute-start.15) | collective-permute-done | bytes 262176 | tf_op jit(solution)/shard_map/ppermute | solution.py:470
  85.9 5.6 %collective-permute-done.16.r1 = bf16[512,256]{1,0:T(8,128)(2,1)S(1)} collective-permute-done((bf16[512,256]{1,0:T(8,128)(2,1)S(1)}, bf16[512,256]{1,0:T(8,128)(2,1)S(1)}, u32[]{:S(2)}, u32[]{:S(2)}) %collective-permute-start.16) | collective-permute-done | bytes 262176 | tf_op jit(solution)/shard_map/ppermute | solution.py:468
  92.0 1.7 %shard_map.101 = (f32[512,128]{1,0:T(8,128)S(1)}, bf16[512,128]{1,0:T(8,128)(2,1)S(1)}, bf16[512,128]{1,0:T(8,128)(2,1)S(1)}, bf16[512,128]{1,0:T(8,128)(2,1)S(1...) custom-call(s32[8]{0:T(128)S(1)} %concatenate.3.meta_ref, f32[512,256]{1,0:T(8,128)S(1)} %get-tuple-element.51.own, ...), custom_call_target="tpu_custom_call" | custom-call | flops 536870912 | bytes 6357024 | tf_op jit(solution)/shard_map/pallas_call | solution.py:73
  94.2 1.3 collective-permute-done.20.got
  95.5 0.7 shard_map.102
  96.1 1.2 collective-permute-start.21
  97.3 1.9 %collective-permute-start.22 = (bf16[80,512]{1,0:T(8,128)(2,1)S(1)}, bf16[80,512]{1,0:T(8,128)(2,1)S(1)}, u32[]{:S(2)}, u32[]{:S(2)}) collective-permute-start(bf16[80,512]{1,0:T(8,128)(2,1)S(1)} %get-tuple-element.64), channel_id=1, source_target_pairs={{0,8},{8,0},{128,136},{136,128},{1,9},{9,1},{129,137},{137,129},{2... | collective-permute-start | bytes 245768 | tf_op jit(solution)/shard_map/ppermute | solution.py:491
  99.5 1.9 %collective-permute-done.21.p1 = bf16[80,512]{1,0:T(8,128)(2,1)S(1)} collective-permute-done((bf16[80,512]{1,0:T(8,128)(2,1)S(1)}, bf16[80,512]{1,0:T(8,128)(2,1)S(1)}, u32[]{:S(2)}, u32[]{:S(2)}) %collective-permute-start.21) | collective-permute-done | bytes 81952 | tf_op jit(solution)/shard_map/ppermute | solution.py:491
  101.4 1.7 %collective-permute-done.22.p2 = bf16[80,512]{1,0:T(8,128)(2,1)S(1)} collective-permute-done((bf16[80,512]{1,0:T(8,128)(2,1)S(1)}, bf16[80,512]{1,0:T(8,128)(2,1)S(1)}, u32[]{:S(2)}, u32[]{:S(2)}) %collective-permute-start.22) | collective-permute-done | bytes 81952 | tf_op jit(solution)/shard_map/ppermute | solution.py:491
  103.7 3.3 %collective-permute-start.24 = (bf16[80,512]{1,0:T(8,128)(2,1)S(1)}, bf16[80,512]{1,0:T(8,128)(2,1)S(1)}, u32[]{:S(2)}, u32[]{:S(2)}) collective-permute-start(bf16[80,512]{1,0:T(8,128)(2,1)S(1)} %get-tuple-element.69), channel_id=1, source_target_pairs={{0,64},{64,0},{1,65},{65,1},{2,66},{66,2},{3,67},{67,3},{4,68},{68... | collective-permute-start | bytes 245768 | tf_op jit(solution)/shard_map/ppermute | solution.py:497
  107.0 4.6 %collective-permute-start.27 = (bf16[512,128]{1,0:T(8,128)(2,1)S(1)}, bf16[512,128]{1,0:T(8,128)(2,1)S(1)}, u32[]{:S(2)}, u32[]{:S(2)}) collective-permute-start(bf16[512,128]{1,0:T(8,128)(2,1)S(1)} %get-tuple-element.72), channel_id=1, source_target_pairs={{0,2},{1,3},{2,0},{3,1},{4,6},{5,7},{6,4},{7,5},{8,10},{9,11},{10,... | collective-permute-start | bytes 393224 | tf_op jit(solution)/shard_map/ppermute | solution.py:496
  111.6 7.3 %collective-permute-start.25 = (bf16[80,512]{1,0:T(8,128)(2,1)S(1)}, bf16[80,512]{1,0:T(8,128)(2,1)S(1)}, u32[]{:S(2)}, u32[]{:S(2)}) collective-permute-start(bf16[80,512]{1,0:T(8,128)(2,1)S(1)} %add_convert_fusion.3.a), channel_id=1, source_target_pairs={{0,32},{32,0},{1,33},{33,1},{2,34},{34,2},{3,35},{35,3},{4,36},{36... | collective-permute-start | bytes 245768 | tf_op jit(solution)/shard_map/ppermute | solution.py:499
  118.9 2.5 %collective-permute-done.25.b = bf16[80,512]{1,0:T(8,128)(2,1)S(1)} collective-permute-done((bf16[80,512]{1,0:T(8,128)(2,1)S(1)}, bf16[80,512]{1,0:T(8,128)(2,1)S(1)}, u32[]{:S(2)}, u32[]{:S(2)}) %collective-permute-start.25) | collective-permute-done | bytes 81952 | tf_op jit(solution)/shard_map/ppermute | solution.py:499
  121.6 9.3 %collective-permute-start.33 = (bf16[512,128]{1,0:T(8,128)(2,1)S(1)}, bf16[512,128]{1,0:T(8,128)(2,1)S(1)}, u32[]{:S(2)}, u32[]{:S(2)}) collective-permute-start(bf16[512,128]{1,0:T(8,128)(2,1)S(1)} %get-tuple-element.75), channel_id=1, source_target_pairs={{0,0},{64,4},{32,8},{96,12},{24,16},{88,20},{56,24},{120,28},{12,3... | collective-permute-start | bytes 393224 | tf_op jit(solution)/shard_map/ppermute | solution.py:505
  131.3 2.6 %collective-permute-start.31 = (bf16[80,512]{1,0:T(8,128)(2,1)S(1)}, bf16[80,512]{1,0:T(8,128)(2,1)S(1)}, u32[]{:S(2)}, u32[]{:S(2)}) collective-permute-start(bf16[80,512]{1,0:T(8,128)(2,1)S(1)} %add_convert_fusion.2.p0), channel_id=1, source_target_pairs={{0,136},{8,128},{128,8},{136,0},{1,137},{9,129},{129,9},{137,1},{2... | collective-permute-start | bytes 245768 | tf_op jit(solution)/shard_map/ppermute | solution.py:508
  133.9 4.0 %collective-permute-done.32.p2 = bf16[80,512]{1,0:T(8,128)(2,1)S(1)} collective-permute-done((bf16[80,512]{1,0:T(8,128)(2,1)S(1)}, bf16[80,512]{1,0:T(8,128)(2,1)S(1)}, u32[]{:S(2)}, u32[]{:S(2)}) %collective-permute-start.32) | collective-permute-done | bytes 81952 | tf_op jit(solution)/shard_map/ppermute | solution.py:508
  138.4 2.5 %collective-permute-start.34 = (bf16[320,512]{1,0:T(8,128)(2,1)S(1)}, bf16[320,512]{1,0:T(8,128)(2,1)S(1)}, u32[]{:S(2)}, u32[]{:S(2)}) collective-permute-start(bf16[320,512]{1,0:T(8,128)(2,1)S(1)} %shard_map.105.mine), channel_id=1, source_target_pairs={{0,4},{4,0},{1,5},{5,1},{2,6},{6,2},{3,7},{7,3},{8,12},{12,8},{9,1... | collective-permute-start | bytes 983048 | tf_op jit(solution)/shard_map/ppermute | solution.py:510
  140.9 1.3 collective-permute-done.34.other
  142.1 1.7 %shard_map.106 = (f32[512,512]{1,0:T(8,128)}, f32[128,512]{1,0:T(8,128)}, bf16[1,512,128]{2,1,0:T(8,128)(2,1)}) custom-call(s32[8]{0:T(128)S(1)} %concatenate.3.meta_ref, bf16[320,512]{1,0:T(8,128)(2,1)S(1)} %shard_map.105.mine, bf16[320,512]{1,0:T(8,128)(2,1)S(1)} %collective-permute-done.34.other, bf16[512,128]{1,0:T(8,128)(2,1)S(1)} %collective-permute-done.33._.grad), custom_call_target="tpu_custom_call" | custom-call | bytes 2228256 | tf_op jit(solution)/shard_map/pallas_call | solution.py:73
  (49 shorter events, 6.9 us)
Async XLA Ops:
  0.6 28.4 %copy-start = (bf16[512,512]{1,0:T(8,128)(2,1)S(1)}, bf16[512,512]{1,0:T(8,128)(2,1)}, u32[]{:S(2)}) copy-start(bf16[512,512]{1,0:T(8,128)(2,1)} %w.1) | copy-start | bytes 1572868
  2.4 16.3 %collective-permute-start = (bf16[272,512]{1,0:T(8,128)(2,1)}, bf16[272,512]{1,0:T(8,128)(2,1)S(1)}, u32[]{:S(2)}, u32[]{:S(2)}) collective-permute-start(bf16[272,512]{1,0:T(8,128)(2,1)} %shard_map.94), channel_id=1, source_target_pairs={{0,0},{4,64},{8,32},{12,96},{16,24},{20,88},{24,56},{28,120},{32,1... | collective-permute-start | bytes 835592 | tf_op jit(solution)/shard_map/ppermute | solution.py:399
  18.8 9.2 %collective-permute-start.3 = (bf16[272,512]{1,0:T(8,128)(2,1)S(1)}, bf16[272,512]{1,0:T(8,128)(2,1)S(1)}, u32[]{:S(2)}, u32[]{:S(2)}) collective-permute-start(bf16[272,512]{1,0:T(8,128)(2,1)S(1)} %collective-permute-done.xa_ref.up0), channel_id=1, source_target_pairs={{0,3},{1,2},{2,1},{3,0},{4,7},{5,6},{6,5},{7,4},{8,11},{9,10},{10,... | collective-permute-start | bytes 835592 | tf_op jit(solution)/shard_map/ppermute | solution.py:402
  21.5 6.9 %collective-permute-start.2 = (bf16[272,512]{1,0:T(8,128)(2,1)S(1)}, bf16[272,512]{1,0:T(8,128)(2,1)S(1)}, u32[]{:S(2)}, u32[]{:S(2)}) collective-permute-start(bf16[272,512]{1,0:T(8,128)(2,1)S(1)} %collective-permute-done.xa_ref.up0), channel_id=1, source_target_pairs={{0,2},{1,3},{2,0},{3,1},{4,6},{5,7},{6,4},{7,5},{8,10},{9,11},{10,... | collective-permute-start | bytes 835592 | tf_op jit(solution)/shard_map/ppermute | solution.py:402
  21.8 7.2 %collective-permute-start.1 = (bf16[272,512]{1,0:T(8,128)(2,1)S(1)}, bf16[272,512]{1,0:T(8,128)(2,1)S(1)}, u32[]{:S(2)}, u32[]{:S(2)}) collective-permute-start(bf16[272,512]{1,0:T(8,128)(2,1)S(1)} %collective-permute-done.xa_ref.up0), channel_id=1, source_target_pairs={{0,1},{1,0},{2,3},{3,2},{4,5},{5,4},{6,7},{7,6},{8,9},{9,8},{10,11... | collective-permute-start | bytes 835592 | tf_op jit(solution)/shard_map/ppermute | solution.py:402
  24.7 4.3 %copy-start.2 = (f32[1,128]{1,0:T(1,128)S(1)}, f32[1,128]{1,0:T(1,128)}, u32[]{:S(2)}) copy-start(f32[1,128]{1,0:T(1,128)} %table_ref.1) | copy-start | bytes 1540
  30.3 13.3 %collective-permute-start.7 = (bf16[512,256]{1,0:T(8,128)(2,1)S(1)}, bf16[512,256]{1,0:T(8,128)(2,1)S(1)}, u32[]{:S(2)}, u32[]{:S(2)}) collective-permute-start(bf16[512,256]{1,0:T(8,128)(2,1)S(1)} %get-tuple-element.42.q0), channel_id=1, source_target_pairs={{0,16},{16,0},{1,17},{17,1},{2,18},{18,2},{3,19},{19,3},{4,20},{20... | collective-permute-start | bytes 786440 | tf_op jit(solution)/shard_map/ppermute | solution.py:422
  34.6 10.2 %collective-permute-start.6 = (bf16[528,256]{1,0:T(8,128)(2,1)S(1)}, bf16[528,256]{1,0:T(8,128)(2,1)S(1)}, u32[]{:S(2)}, u32[]{:S(2)}) collective-permute-start(bf16[528,256]{1,0:T(8,128)(2,1)S(1)} %get-tuple-element.41.kv0), channel_id=1, source_target_pairs={{0,128},{8,136},{128,0},{136,8},{1,129},{9,137},{129,1},{137,9},{2... | collective-permute-start | bytes 811016 | tf_op jit(solution)/shard_map/ppermute | solution.py:420
  36.8 17.6 %collective-permute-start.5 = (bf16[528,256]{1,0:T(8,128)(2,1)S(1)}, bf16[528,256]{1,0:T(8,128)(2,1)S(1)}, u32[]{:S(2)}, u32[]{:S(2)}) collective-permute-start(bf16[528,256]{1,0:T(8,128)(2,1)S(1)} %get-tuple-element.41.kv0), channel_id=1, source_target_pairs={{0,136},{8,128},{128,8},{136,0},{1,137},{9,129},{129,9},{137,1},{2... | collective-permute-start | bytes 811016 | tf_op jit(solution)/shard_map/ppermute | solution.py:420
  42.6 12.1 %collective-permute-start.4 = (bf16[528,256]{1,0:T(8,128)(2,1)S(1)}, bf16[528,256]{1,0:T(8,128)(2,1)S(1)}, u32[]{:S(2)}, u32[]{:S(2)}) collective-permute-start(bf16[528,256]{1,0:T(8,128)(2,1)S(1)} %get-tuple-element.41.kv0), channel_id=1, source_target_pairs={{0,8},{8,0},{128,136},{136,128},{1,9},{9,1},{129,137},{137,129},{2... | collective-permute-start | bytes 811016 | tf_op jit(solution)/shard_map/ppermute | solution.py:420
  42.7 2.1 %collective-permute-start.8 = (bf16[512,256]{1,0:T(8,128)(2,1)S(1)}, bf16[512,256]{1,0:T(8,128)(2,1)S(1)}, u32[]{:S(2)}, u32[]{:S(2)}) collective-permute-start(bf16[512,256]{1,0:T(8,128)(2,1)S(1)} %get-tuple-element.42.q0), channel_id=1, source_target_pairs={{0,4},{4,0},{1,5},{5,1},{2,6},{6,2},{3,7},{7,3},{8,12},{12,8},{9,1... | collective-permute-start | bytes 786440 | tf_op jit(solution)/shard_map/ppermute | solution.py:423
  43.7 11.1 %collective-permute-start.9 = (bf16[512,256]{1,0:T(8,128)(2,1)S(1)}, bf16[512,256]{1,0:T(8,128)(2,1)S(1)}, u32[]{:S(2)}, u32[]{:S(2)}) collective-permute-start(bf16[512,256]{1,0:T(8,128)(2,1)S(1)} %collective-permute-done.7.q1), channel_id=1, source_target_pairs={{0,4},{4,0},{1,5},{5,1},{2,6},{6,2},{3,7},{7,3},{8,12},{12,8},{9,1... | collective-permute-start | bytes 786440 | tf_op jit(solution)/shard_map/ppermute | solution.py:423
  56.9 2.5 %collective-permute-start.10 = (bf16[1024,128]{1,0:T(8,128)(2,1)S(1)}, bf16[1024,128]{1,0:T(8,128)(2,1)S(1)}, u32[]{:S(2)}, u32[]{:S(2)}) collective-permute-start(bf16[1024,128]{1,0:T(8,128)(2,1)S(1)} %get-tuple-element.47), channel_id=1, source_target_pairs={{0,4},{4,0},{1,5},{5,1},{2,6},{6,2},{3,7},{7,3},{8,12},{12,8},{9,1... | collective-permute-start | bytes 786440 | tf_op jit(solution)/shard_map/ppermute | solution.py:439
  59.4 4.8 %copy-start.1 = (bf16[128,512]{1,0:T(8,128)(2,1)S(1)}, bf16[128,512]{1,0:T(8,128)(2,1)}, u32[]{:S(2)}) copy-start(bf16[128,512]{1,0:T(8,128)(2,1)} %wout.1) | copy-start | bytes 393220
  59.4 4.8 %collective-permute-start.11 = (bf16[512,128]{1,0:T(8,128)(2,1)S(1)}, bf16[512,128]{1,0:T(8,128)(2,1)S(1)}, u32[]{:S(2)}, u32[]{:S(2)}) collective-permute-start(bf16[512,128]{1,0:T(8,128)(2,1)S(1)} %add_convert_fusion.1), channel_id=1, source_target_pairs={{0,16},{16,0},{1,17},{17,1},{2,18},{18,2},{3,19},{19,3},{4,20},{20... | collective-permute-start | bytes 393224 | tf_op jit(solution)/shard_map/ppermute | solution.py:441
  65.4 3.9 %collective-permute-start.12 = (bf16[512,128]{1,0:T(8,128)(2,1)S(1)}, bf16[512,128]{1,0:T(8,128)(2,1)S(1)}, u32[]{:S(2)}, u32[]{:S(2)}) collective-permute-start(bf16[512,128]{1,0:T(8,128)(2,1)S(1)} %get-tuple-element.50.g0), channel_id=1, source_target_pairs={{0,16},{16,0},{1,17},{17,1},{2,18},{18,2},{3,19},{19,3},{4,20},{20... | collective-permute-start | bytes 393224 | tf_op jit(solution)/shard_map/ppermute | solution.py:450
  66.4 5.2 %collective-permute-start.13 = (bf16[512,128]{1,0:T(8,128)(2,1)S(1)}, bf16[512,128]{1,0:T(8,128)(2,1)S(1)}, u32[]{:S(2)}, u32[]{:S(2)}) collective-permute-start(bf16[512,128]{1,0:T(8,128)(2,1)S(1)} %get-tuple-element.50.g0), channel_id=1, source_target_pairs={{0,4},{4,0},{1,5},{5,1},{2,6},{6,2},{3,7},{7,3},{8,12},{12,8},{9,1... | collective-permute-start | bytes 393224 | tf_op jit(solution)/shard_map/ppermute | solution.py:451
  69.3 3.3 %collective-permute-start.14 = (bf16[512,128]{1,0:T(8,128)(2,1)S(1)}, bf16[512,128]{1,0:T(8,128)(2,1)S(1)}, u32[]{:S(2)}, u32[]{:S(2)}) collective-permute-start(bf16[512,128]{1,0:T(8,128)(2,1)S(1)} %collective-permute-done.12.g1), channel_id=1, source_target_pairs={{0,4},{4,0},{1,5},{5,1},{2,6},{6,2},{3,7},{7,3},{8,12},{12,8},{9,1... | collective-permute-start | bytes 393224 | tf_op jit(solution)/shard_map/ppermute | solution.py:451
  76.2 3.7 %collective-permute-start.18 = (bf16[1024,128]{1,0:T(8,128)(2,1)S(1)}, bf16[1024,128]{1,0:T(8,128)(2,1)S(1)}, u32[]{:S(2)}, u32[]{:S(2)}) collective-permute-start(bf16[1024,128]{1,0:T(8,128)(2,1)S(1)} %get-tuple-element.56), channel_id=1, source_target_pairs={{0,4},{4,0},{1,5},{5,1},{2,6},{6,2},{3,7},{7,3},{8,12},{12,8},{9,1... | collective-permute-start | bytes 786440 | tf_op jit(solution)/shard_map/ppermute | solution.py:471
  76.6 9.3 %collective-permute-start.15 = (bf16[512,256]{1,0:T(8,128)(2,1)S(1)}, bf16[512,256]{1,0:T(8,128)(2,1)S(1)}, u32[]{:S(2)}, u32[]{:S(2)}) collective-permute-start(bf16[512,256]{1,0:T(8,128)(2,1)S(1)} %get-tuple-element.52), channel_id=1, source_target_pairs={{0,128},{8,136},{128,0},{136,8},{1,129},{9,137},{129,1},{137,9},{2... | collective-permute-start | bytes 786440 | tf_op jit(solution)/shard_map/ppermute | solution.py:470
  77.7 13.8 %collective-permute-start.16 = (bf16[512,256]{1,0:T(8,128)(2,1)S(1)}, bf16[512,256]{1,0:T(8,128)(2,1)S(1)}, u32[]{:S(2)}, u32[]{:S(2)}) collective-permute-start(bf16[512,256]{1,0:T(8,128)(2,1)S(1)} %get-tuple-element.53), channel_id=1, source_target_pairs={{0,8},{8,0},{128,136},{136,128},{1,9},{9,1},{129,137},{137,129},{2... | collective-permute-start | bytes 786440 | tf_op jit(solution)/shard_map/ppermute | solution.py:468
  79.5 12.4 %collective-permute-start.17 = (bf16[512,256]{1,0:T(8,128)(2,1)S(1)}, bf16[512,256]{1,0:T(8,128)(2,1)S(1)}, u32[]{:S(2)}, u32[]{:S(2)}) collective-permute-start(bf16[512,256]{1,0:T(8,128)(2,1)S(1)} %get-tuple-element.54), channel_id=1, source_target_pairs={{0,136},{8,128},{128,8},{136,0},{1,137},{9,129},{129,9},{137,1},{2... | collective-permute-start | bytes 786440 | tf_op jit(solution)/shard_map/ppermute | solution.py:469
  79.9 12.1 %collective-permute-start.19 = (bf16[512,128]{1,0:T(8,128)(2,1)S(1)}, bf16[512,128]{1,0:T(8,128)(2,1)S(1)}, u32[]{:S(2)}, u32[]{:S(2)}) collective-permute-start(bf16[512,128]{1,0:T(8,128)(2,1)S(1)} %add_convert_fusion), channel_id=1, source_target_pairs={{0,16},{16,0},{1,17},{17,1},{2,18},{18,2},{3,19},{19,3},{4,20},{20... | collective-permute-start | bytes 393224 | tf_op jit(solution)/shard_map/ppermute | solution.py:473
  93.6 1.9 %collective-permute-start.20 = (bf16[320,512]{1,0:T(8,128)(2,1)S(1)}, bf16[320,512]{1,0:T(8,128)(2,1)S(1)}, u32[]{:S(2)}, u32[]{:S(2)}) collective-permute-start(bf16[320,512]{1,0:T(8,128)(2,1)S(1)} %get-tuple-element.61), channel_id=1, source_target_pairs={{0,4},{4,0},{1,5},{5,1},{2,6},{6,2},{3,7},{7,3},{8,12},{12,8},{9,1... | collective-permute-start | bytes 983048 | tf_op jit(solution)/shard_map/ppermute | solution.py:483
  96.1 5.2 %collective-permute-start.21 = (bf16[80,512]{1,0:T(8,128)(2,1)S(1)}, bf16[80,512]{1,0:T(8,128)(2,1)S(1)}, u32[]{:S(2)}, u32[]{:S(2)}) collective-permute-start(bf16[80,512]{1,0:T(8,128)(2,1)S(1)} %get-tuple-element.63), channel_id=1, source_target_pairs={{0,128},{8,136},{128,0},{136,8},{1,129},{9,137},{129,1},{137,9},{2... | collective-permute-start | bytes 245768 | tf_op jit(solution)/shard_map/ppermute | solution.py:491
  97.3 5.8 %collective-permute-start.22 = (bf16[80,512]{1,0:T(8,128)(2,1)S(1)}, bf16[80,512]{1,0:T(8,128)(2,1)S(1)}, u32[]{:S(2)}, u32[]{:S(2)}) collective-permute-start(bf16[80,512]{1,0:T(8,128)(2,1)S(1)} %get-tuple-element.64), channel_id=1, source_target_pairs={{0,8},{8,0},{128,136},{136,128},{1,9},{9,1},{129,137},{137,129},{2... | collective-permute-start | bytes 245768 | tf_op jit(solution)/shard_map/ppermute | solution.py:491
  99.2 4.5 %collective-permute-start.23 = (bf16[80,512]{1,0:T(8,128)(2,1)S(1)}, bf16[80,512]{1,0:T(8,128)(2,1)S(1)}, u32[]{:S(2)}, u32[]{:S(2)}) collective-permute-start(bf16[80,512]{1,0:T(8,128)(2,1)S(1)} %get-tuple-element.65), channel_id=1, source_target_pairs={{0,136},{8,128},{128,8},{136,0},{1,137},{9,129},{129,9},{137,1},{2... | collective-permute-start | bytes 245768 | tf_op jit(solution)/shard_map/ppermute | solution.py:491
  103.7 7.9 %collective-permute-start.24 = (bf16[80,512]{1,0:T(8,128)(2,1)S(1)}, bf16[80,512]{1,0:T(8,128)(2,1)S(1)}, u32[]{:S(2)}, u32[]{:S(2)}) collective-permute-start(bf16[80,512]{1,0:T(8,128)(2,1)S(1)} %get-tuple-element.69), channel_id=1, source_target_pairs={{0,64},{64,0},{1,65},{65,1},{2,66},{66,2},{3,67},{67,3},{4,68},{68... | collective-permute-start | bytes 245768 | tf_op jit(solution)/shard_map/ppermute | solution.py:497
  107.0 11.9 %collective-permute-start.26 = (bf16[512,128]{1,0:T(8,128)(2,1)S(1)}, bf16[512,128]{1,0:T(8,128)(2,1)S(1)}, u32[]{:S(2)}, u32[]{:S(2)}) collective-permute-start(bf16[512,128]{1,0:T(8,128)(2,1)S(1)} %get-tuple-element.71), channel_id=1, source_target_pairs={{0,1},{1,0},{2,3},{3,2},{4,5},{5,4},{6,7},{7,6},{8,9},{9,8},{10,11... | collective-permute-start | bytes 393224 | tf_op jit(solution)/shard_map/ppermute | solution.py:496
  107.0 11.9 %collective-permute-start.27 = (bf16[512,128]{1,0:T(8,128)(2,1)S(1)}, bf16[512,128]{1,0:T(8,128)(2,1)S(1)}, u32[]{:S(2)}, u32[]{:S(2)}) collective-permute-start(bf16[512,128]{1,0:T(8,128)(2,1)S(1)} %get-tuple-element.72), channel_id=1, source_target_pairs={{0,2},{1,3},{2,0},{3,1},{4,6},{5,7},{6,4},{7,5},{8,10},{9,11},{10,... | collective-permute-start | bytes 393224 | tf_op jit(solution)/shard_map/ppermute | solution.py:496
  111.5 7.4 %collective-permute-start.28 = (bf16[512,128]{1,0:T(8,128)(2,1)S(1)}, bf16[512,128]{1,0:T(8,128)(2,1)S(1)}, u32[]{:S(2)}, u32[]{:S(2)}) collective-permute-start(bf16[512,128]{1,0:T(8,128)(2,1)S(1)} %get-tuple-element.73), channel_id=1, source_target_pairs={{0,3},{1,2},{2,1},{3,0},{4,7},{5,6},{6,5},{7,4},{8,11},{9,10},{10,... | collective-permute-start | bytes 393224 | tf_op jit(solution)/shard_map/ppermute | solution.py:496
  111.6 9.8 %collective-permute-start.25 = (bf16[80,512]{1,0:T(8,128)(2,1)S(1)}, bf16[80,512]{1,0:T(8,128)(2,1)S(1)}, u32[]{:S(2)}, u32[]{:S(2)}) collective-permute-start(bf16[80,512]{1,0:T(8,128)(2,1)S(1)} %add_convert_fusion.3.a), channel_id=1, source_target_pairs={{0,32},{32,0},{1,33},{33,1},{2,34},{34,2},{3,35},{35,3},{4,36},{36... | collective-permute-start | bytes 245768 | tf_op jit(solution)/shard_map/ppermute | solution.py:499
  121.5 9.5 %collective-permute-start.29 = (bf16[80,512]{1,0:T(8,128)(2,1)S(1)}, bf16[80,512]{1,0:T(8,128)(2,1)S(1)}, u32[]{:S(2)}, u32[]{:S(2)}) collective-permute-start(bf16[80,512]{1,0:T(8,128)(2,1)S(1)} %get-tuple-element.74), channel_id=1, source_target_pairs={{0,16},{16,0},{1,17},{17,1},{2,18},{18,2},{3,19},{19,3},{4,20},{20... | collective-permute-start | bytes 245768 | tf_op jit(solution)/shard_map/ppermute | solution.py:506
  121.6 12.3 %collective-permute-start.33 = (bf16[512,128]{1,0:T(8,128)(2,1)S(1)}, bf16[512,128]{1,0:T(8,128)(2,1)S(1)}, u32[]{:S(2)}, u32[]{:S(2)}) collective-permute-start(bf16[512,128]{1,0:T(8,128)(2,1)S(1)} %get-tuple-element.75), channel_id=1, source_target_pairs={{0,0},{64,4},{32,8},{96,12},{24,16},{88,20},{56,24},{120,28},{12,3... | collective-permute-start | bytes 393224 | tf_op jit(solution)/shard_map/ppermute | solution.py:505
  131.0 6.8 %collective-permute-start.32 = (bf16[80,512]{1,0:T(8,128)(2,1)S(1)}, bf16[80,512]{1,0:T(8,128)(2,1)S(1)}, u32[]{:S(2)}, u32[]{:S(2)}) collective-permute-start(bf16[80,512]{1,0:T(8,128)(2,1)S(1)} %add_convert_fusion.2.p0), channel_id=1, source_target_pairs={{0,128},{8,136},{128,0},{136,8},{1,129},{9,137},{129,1},{137,9},{2... | collective-permute-start | bytes 245768 | tf_op jit(solution)/shard_map/ppermute | solution.py:508
  131.3 6.6 %collective-permute-start.31 = (bf16[80,512]{1,0:T(8,128)(2,1)S(1)}, bf16[80,512]{1,0:T(8,128)(2,1)S(1)}, u32[]{:S(2)}, u32[]{:S(2)}) collective-permute-start(bf16[80,512]{1,0:T(8,128)(2,1)S(1)} %add_convert_fusion.2.p0), channel_id=1, source_target_pairs={{0,136},{8,128},{128,8},{136,0},{1,137},{9,129},{129,9},{137,1},{2... | collective-permute-start | bytes 245768 | tf_op jit(solution)/shard_map/ppermute | solution.py:508
  133.9 4.0 %collective-permute-start.30 = (bf16[80,512]{1,0:T(8,128)(2,1)S(1)}, bf16[80,512]{1,0:T(8,128)(2,1)S(1)}, u32[]{:S(2)}, u32[]{:S(2)}) collective-permute-start(bf16[80,512]{1,0:T(8,128)(2,1)S(1)} %add_convert_fusion.2.p0), channel_id=1, source_target_pairs={{0,8},{8,0},{128,136},{136,128},{1,9},{9,1},{129,137},{137,129},{2... | collective-permute-start | bytes 245768 | tf_op jit(solution)/shard_map/ppermute | solution.py:508
  138.4 3.7 %collective-permute-start.34 = (bf16[320,512]{1,0:T(8,128)(2,1)S(1)}, bf16[320,512]{1,0:T(8,128)(2,1)S(1)}, u32[]{:S(2)}, u32[]{:S(2)}) collective-permute-start(bf16[320,512]{1,0:T(8,128)(2,1)S(1)} %shard_map.105.mine), channel_id=1, source_target_pairs={{0,4},{4,0},{1,5},{5,1},{2,6},{6,2},{3,7},{7,3},{8,12},{12,8},{9,1... | collective-permute-start | bytes 983048 | tf_op jit(solution)/shard_map/ppermute | solution.py:510

commit v5 on v4

--- a/solution.py
+++ b/solution.py
@@ -358,6 +358,10 @@
     grad_ref[...] = grad.astype(BF)
 
 
+def add_kernel(a, b, _, out_ref, __):
+    out_ref[...] = (a[...].astype(F32) + b[...].astype(F32)).astype(BF)
+
+
 def split_kernel(meta_ref, stay, got, p0_ref, p1_ref, p2_ref, p3_ref, total):
     x = meta_ref[2]
     total[...] = stay[...] + got[...].astype(F32)
@@ -366,7 +370,7 @@
         out[...] = total[rows, :].astype(out.dtype)
 
 
-def join_kernel(meta_ref, p0, p1, p3, p2, _, out_ref):
+def join_kernel(meta_ref, p0, p1, p3, p2, out_ref):
     x = meta_ref[2]
     for rel, piece in enumerate((p0, p1, p2, p3)):
         out_ref[pl.ds(pl.multiple_of((x ^ rel) * PIECE, 16), PIECE), :] = piece[...]
@@ -502,11 +506,13 @@
         [((PIECE, WIDTH), BF), ((ROWS, DH), BF)],
         (total, other, t0, u1, u2, u3),
     )
+    other = lax.ppermute(total, "z0", FLIP)
+    total, grad_local = call(
+        add_kernel, [((PIECE, WIDTH), BF)], (total, other, grad_local), passed=1
+    )
     grad_local = lax.ppermute(grad_local, MOVED, HOME)
-    other = lax.ppermute(total, "z0", FLIP)
-    total = (total.astype(F32) + other.astype(F32)).astype(BF)
     h1, h3, h2 = (lax.ppermute(total, ("xh", "xl"), flip_x(rel)) for rel in (1, 3, 2))
-    (mine_half,) = call(join_kernel, [((320, WIDTH), BF)], (meta, total, h1, h3, h2, grad_local), unread=1)
+    (mine_half,) = call(join_kernel, [((320, WIDTH), BF)], (meta, total, h1, h3, h2))
     other_half = lax.ppermute(mine_half, "core", FLIP)
     normalizer = 1.0 / math.sqrt(4 * 16 * ROWS)
     win, wout, grad_local = call(

time: 144 us -> 152 us (1.056)
  waiting for transfers between devices: 51.4 us -> 59.6 us
    ppermute x1, starting transfers between devices: 7.31 us -> 0.09 us  [body(): other = lax.ppermute(total, 'z1', FLIP)]
    ppermute x1, starting transfers between devices: 1.08 us -> 7.22 us  [body(): r2 = lax.ppermute(s2, ('xh', 'xl'), flip_x(2))]
    ppermute x1, waiting for transfers between devices: 0.01 us -> 5.3 us  [body(): grad_local = lax.ppermute(grad_local, MOVED, HOME)]
    ppermute x1, waiting for transfers between devices: 5.13 us -> 0.13 us  [body(): r2 = lax.ppermute(s2, ('xh', 'xl'), flip_x(2))]
    ppermute x1, starting transfers between devices: 9.34 us -> 4.97 us  [body(): grad_local = lax.ppermute(grad_local, MOVED, HOME)]
    ppermute x1, starting transfers between devices: 2.46 us -> 5.94 us  [body(): other_half = lax.ppermute(mine_half, 'core', FLIP)]
    ppermute x1, waiting for transfers between devices: 5.58 us -> 9.05 us  [body(): r1 = lax.ppermute(s1, ('xh', 'xl'), flip_x(1))]
    ppermute x1, starting transfers between devices: 3.26 us -> 0.26 us  [body(): other = lax.ppermute(total, 'z2', FLIP)]
  transfers between devices with their start and end apart: 35 -> 35, of which waited for: 21 -> 25; matrix products, arithmetic and copies ran while one was open for 1% -> 1% of each run, Pallas kernels for 1% -> 1%
where the time goes in v5:
time: 152 us
  starting transfers between devices  72.5 us (48%)
  waiting for transfers between devices  59.6 us (39%)
  Pallas kernels  16.2 us (11%)
  between operations  2.12 us (1%)
    pallas_call x14, Pallas kernels, call(): pl.pallas_call(kernel, out_shape=[jax.ShapeDtypeStruct(s, t) for s, t in...  16.2 us
    ppermute x1, starting transfers between devices, body(): xa = lax.ppermute(xa, MOVED, AWAY)  10.2 us
    ppermute x3, waiting for transfers between devices, body(): lax.ppermute(kv, ('xh', 'xl'), flip_x(rel))  9.92 us
    ppermute x1, waiting for transfers between devices, body(): r1 = lax.ppermute(s1, ('xh', 'xl'), flip_x(1))  9.05 us
    ppermute x3, starting transfers between devices, body(): lax.ppermute(kv, ('xh', 'xl'), flip_x(rel))  8.1 us
    ppermute x1, starting transfers between devices, body(): r2 = lax.ppermute(s2, ('xh', 'xl'), flip_x(2))  7.22 us
    ppermute x1, waiting for transfers between devices, body(): xa = lax.ppermute(xa, MOVED, AWAY)  6.08 us
    ppermute x1, starting transfers between devices, body(): other_half = lax.ppermute(mine_half, 'core', FLIP)  5.94 us
  transfers between devices with their start and end apart: 35, of which 25 were waited for; matrix products, arithmetic and copies ran while one was open for 1% of the time, Pallas kernels for 1%

profile of v5, /device:TPU:1, one launch (start us, length us, event | category | flops | bytes accessed | tf_op | source)
XLA Modules:
  0.0 151.8 jit_solution(7483562665668880269)
XLA Ops:
  0.6 1.8 %shard_map.94 = bf16[272,512]{1,0:T(8,128)(2,1)} custom-call(bf16[512,512]{1,0:T(8,128)(2,1)} %bitcast.8, s32[1,512]{1,0:T(1,128)} %times_hbm.1, s32[1,3]{1,0:T(1,128)} %lengths_hbm.1, bf16[512,512]{1,0:T(8,128)(2,1)} %bitcast.9), custom_call_target="tpu_custom_call" | custom-call | bytes 1329164 | tf_op jit(solution)/shard_map/pallas_call | solution.py:73
  2.4 10.2 %collective-permute-start = (bf16[272,512]{1,0:T(8,128)(2,1)}, bf16[272,512]{1,0:T(8,128)(2,1)S(1)}, u32[]{:S(2)}, u32[]{:S(2)}) collective-permute-start(bf16[272,512]{1,0:T(8,128)(2,1)} %shard_map.94), channel_id=1, source_target_pairs={{0,0},{4,64},{8,32},{12,96},{16,24},{20,88},{24,56},{28,120},{32,1... | collective-permute-start | bytes 835592 | tf_op jit(solution)/shard_map/ppermute | solution.py:403
  12.7 6.1 %collective-permute-done.xa_ref.up0 = bf16[272,512]{1,0:T(8,128)(2,1)S(1)} collective-permute-done((bf16[272,512]{1,0:T(8,128)(2,1)}, bf16[272,512]{1,0:T(8,128)(2,1)S(1)}, u32[]{:S(2)}, u32[]{:S(2)}) %collective-permute-start) | collective-permute-done | bytes 278560 | tf_op jit(solution)/shard_map/ppermute | solution.py:403
  18.8 2.7 %collective-permute-start.3 = (bf16[272,512]{1,0:T(8,128)(2,1)S(1)}, bf16[272,512]{1,0:T(8,128)(2,1)S(1)}, u32[]{:S(2)}, u32[]{:S(2)}) collective-permute-start(bf16[272,512]{1,0:T(8,128)(2,1)S(1)} %collective-permute-done.xa_ref.up0), channel_id=1, source_target_pairs={{0,3},{1,2},{2,1},{3,0},{4,7},{5,6},{6,5},{7,4},{8,11},{9,10},{10,... | collective-permute-start | bytes 835592 | tf_op jit(solution)/shard_map/ppermute | solution.py:406
  24.7 1.7 %shard_map.95._.list_ref = s32[128]{0:T(128)S(1)} custom-call(s32[8]{0:T(128)S(1)} %concatenate.3.meta_ref), custom_call_target="tpu_custom_call" | custom-call | bytes 544 | tf_op jit(solution)/shard_map/pallas_call | solution.py:73
  26.4 1.6 %collective-permute-done.3.x3.up3 = bf16[272,512]{1,0:T(8,128)(2,1)S(1)} collective-permute-done((bf16[272,512]{1,0:T(8,128)(2,1)S(1)}, bf16[272,512]{1,0:T(8,128)(2,1)S(1)}, u32[]{:S(2)}, u32[]{:S(2)}) %collective-permute-start.3) | collective-permute-done | bytes 278560 | tf_op jit(solution)/shard_map/ppermute | solution.py:406
  29.0 1.3 shard_map.96
  30.3 4.3 %collective-permute-start.7 = (bf16[512,256]{1,0:T(8,128)(2,1)S(1)}, bf16[512,256]{1,0:T(8,128)(2,1)S(1)}, u32[]{:S(2)}, u32[]{:S(2)}) collective-permute-start(bf16[512,256]{1,0:T(8,128)(2,1)S(1)} %get-tuple-element.44.q0), channel_id=1, source_target_pairs={{0,16},{16,0},{1,17},{17,1},{2,18},{18,2},{3,19},{19,3},{4,20},{20... | collective-permute-start | bytes 786440 | tf_op jit(solution)/shard_map/ppermute | solution.py:426
  34.6 2.2 %collective-permute-start.6 = (bf16[528,256]{1,0:T(8,128)(2,1)S(1)}, bf16[528,256]{1,0:T(8,128)(2,1)S(1)}, u32[]{:S(2)}, u32[]{:S(2)}) collective-permute-start(bf16[528,256]{1,0:T(8,128)(2,1)S(1)} %get-tuple-element.43.kv0), channel_id=1, source_target_pairs={{0,128},{8,136},{128,0},{136,8},{1,129},{9,137},{129,1},{137,9},{2... | collective-permute-start | bytes 811016 | tf_op jit(solution)/shard_map/ppermute | solution.py:424
  36.8 5.8 %collective-permute-start.5 = (bf16[528,256]{1,0:T(8,128)(2,1)S(1)}, bf16[528,256]{1,0:T(8,128)(2,1)S(1)}, u32[]{:S(2)}, u32[]{:S(2)}) collective-permute-start(bf16[528,256]{1,0:T(8,128)(2,1)S(1)} %get-tuple-element.43.kv0), channel_id=1, source_target_pairs={{0,136},{8,128},{128,8},{136,0},{1,137},{9,129},{129,9},{137,1},{2... | collective-permute-start | bytes 811016 | tf_op jit(solution)/shard_map/ppermute | solution.py:424
  43.7 1.2 collective-permute-done.8.q2
  44.8 9.6 %collective-permute-done.5.kv3 = bf16[528,256]{1,0:T(8,128)(2,1)S(1)} collective-permute-done((bf16[528,256]{1,0:T(8,128)(2,1)S(1)}, bf16[528,256]{1,0:T(8,128)(2,1)S(1)}, u32[]{:S(2)}, u32[]{:S(2)}) %collective-permute-start.5) | collective-permute-done | bytes 270368 | tf_op jit(solution)/shard_map/ppermute | solution.py:424
  54.7 2.2 %shard_map.97 = (f32[1024,128]{1,0:T(8,128)S(1)}, bf16[1024,128]{1,0:T(8,128)(2,1)S(1)}, bf16[8,256,256]{2,1,0:T(8,128)(2,1)S(1)}, bf16[8,256,128]{2,1,0:T(8,128)(2,1)S(1)}, bf16[8,256,256]{2,1,0:T(8,128)(2,1)S(1)}) custom-call(s32[8]{0:T(128)S(1)} %concatenate.3.meta_ref, bf16[528,256]{1,0:T(8,128)(2,1)S(1)} %get-tuple-element.43.kv0, ...), custom_call_target="tpu_custom_call" | custom-call | flops 1006632960 | bytes 5538336 | tf_op jit(solution)/shard_map/pallas_call | solution.py:73
  56.9 1.3 collective-permute-start.10
  58.3 1.2 collective-permute-done.10.got_core
  59.5 1.1 collective-permute-start.11
  60.5 3.7 %collective-permute-done.11.got_z = bf16[512,128]{1,0:T(8,128)(2,1)S(1)} collective-permute-done((bf16[512,128]{1,0:T(8,128)(2,1)S(1)}, bf16[512,128]{1,0:T(8,128)(2,1)S(1)}, u32[]{:S(2)}, u32[]{:S(2)}) %collective-permute-start.11) | collective-permute-done | bytes 131104 | tf_op jit(solution)/shard_map/ppermute | solution.py:445
  64.3 1.1 shard_map.98
  65.4 1.1 collective-permute-start.12
  66.4 1.5 collective-permute-start.13
  67.9 1.4 collective-permute-done.12.g1
  69.3 2.3 %collective-permute-start.14 = (bf16[512,128]{1,0:T(8,128)(2,1)S(1)}, bf16[512,128]{1,0:T(8,128)(2,1)S(1)}, u32[]{:S(2)}, u32[]{:S(2)}) collective-permute-start(bf16[512,128]{1,0:T(8,128)(2,1)S(1)} %collective-permute-done.12.g1), channel_id=1, source_target_pairs={{0,4},{4,0},{1,5},{5,1},{2,6},{6,2},{3,7},{7,3},{8,12},{12,8},{9,1... | collective-permute-start | bytes 393224 | tf_op jit(solution)/shard_map/ppermute | solution.py:455
  72.6 3.1 %shard_map.99 = (f32[512,256]{1,0:T(8,128)S(1)}, bf16[512,256]{1,0:T(8,128)(2,1)S(1)}, bf16[512,256]{1,0:T(8,128)(2,1)S(1)}, bf16[512,256]{1,0:T(8,128)(2,1)S(1)...) custom-call(s32[8]{0:T(128)S(1)} %concatenate.3.meta_ref, s32[128]{0:T(128)S(1)} %shard_map.95._.list_ref, ...), custom_call_target="tpu_custom_call" | custom-call | flops 2013265920 | bytes 5243424 | tf_op jit(solution)/shard_map/pallas_call | solution.py:73
  76.2 7.2 %collective-permute-start.15 = (bf16[512,256]{1,0:T(8,128)(2,1)S(1)}, bf16[512,256]{1,0:T(8,128)(2,1)S(1)}, u32[]{:S(2)}, u32[]{:S(2)}) collective-permute-start(bf16[512,256]{1,0:T(8,128)(2,1)S(1)} %get-tuple-element.54), channel_id=1, source_target_pairs={{0,128},{8,136},{128,0},{136,8},{1,129},{9,137},{129,1},{137,9},{2... | collective-permute-start | bytes 786440 | tf_op jit(solution)/shard_map/ppermute | solution.py:474
  83.4 3.5 %collective-permute-start.16 = (bf16[512,256]{1,0:T(8,128)(2,1)S(1)}, bf16[512,256]{1,0:T(8,128)(2,1)S(1)}, u32[]{:S(2)}, u32[]{:S(2)}) collective-permute-start(bf16[512,256]{1,0:T(8,128)(2,1)S(1)} %get-tuple-element.55), channel_id=1, source_target_pairs={{0,8},{8,0},{128,136},{136,128},{1,9},{9,1},{129,137},{137,129},{2... | collective-permute-start | bytes 786440 | tf_op jit(solution)/shard_map/ppermute | solution.py:472
  87.0 2.5 %collective-permute-start.19 = (bf16[512,128]{1,0:T(8,128)(2,1)S(1)}, bf16[512,128]{1,0:T(8,128)(2,1)S(1)}, u32[]{:S(2)}, u32[]{:S(2)}) collective-permute-start(bf16[512,128]{1,0:T(8,128)(2,1)S(1)} %add_convert_fusion), channel_id=1, source_target_pairs={{0,16},{16,0},{1,17},{17,1},{2,18},{18,2},{3,19},{19,3},{4,20},{20... | collective-permute-start | bytes 393224 | tf_op jit(solution)/shard_map/ppermute | solution.py:477
  89.9 9.1 %collective-permute-done.16.r1 = bf16[512,256]{1,0:T(8,128)(2,1)S(1)} collective-permute-done((bf16[512,256]{1,0:T(8,128)(2,1)S(1)}, bf16[512,256]{1,0:T(8,128)(2,1)S(1)}, u32[]{:S(2)}, u32[]{:S(2)}) %collective-permute-start.16) | collective-permute-done | bytes 262176 | tf_op jit(solution)/shard_map/ppermute | solution.py:472
  99.0 1.7 %shard_map.101 = (f32[512,128]{1,0:T(8,128)S(1)}, bf16[512,128]{1,0:T(8,128)(2,1)S(1)}, bf16[512,128]{1,0:T(8,128)(2,1)S(1)}, bf16[512,128]{1,0:T(8,128)(2,1)S(1...) custom-call(s32[8]{0:T(128)S(1)} %concatenate.3.meta_ref, f32[512,256]{1,0:T(8,128)S(1)} %get-tuple-element.53.own, ...), custom_call_target="tpu_custom_call" | custom-call | flops 536870912 | bytes 6357024 | tf_op jit(solution)/shard_map/pallas_call | solution.py:73
  101.6 1.3 collective-permute-done.20.got
  104.2 2.3 %collective-permute-start.22 = (bf16[80,512]{1,0:T(8,128)(2,1)S(1)}, bf16[80,512]{1,0:T(8,128)(2,1)S(1)}, u32[]{:S(2)}, u32[]{:S(2)}) collective-permute-start(bf16[80,512]{1,0:T(8,128)(2,1)S(1)} %get-tuple-element.66), channel_id=1, source_target_pairs={{0,8},{8,0},{128,136},{136,128},{1,9},{9,1},{129,137},{137,129},{2... | collective-permute-start | bytes 245768 | tf_op jit(solution)/shard_map/ppermute | solution.py:495
  106.9 1.9 %collective-permute-done.21.p1 = bf16[80,512]{1,0:T(8,128)(2,1)S(1)} collective-permute-done((bf16[80,512]{1,0:T(8,128)(2,1)S(1)}, bf16[80,512]{1,0:T(8,128)(2,1)S(1)}, u32[]{:S(2)}, u32[]{:S(2)}) %collective-permute-start.21) | collective-permute-done | bytes 81952 | tf_op jit(solution)/shard_map/ppermute | solution.py:495
  108.8 1.7 %collective-permute-done.22.p2 = bf16[80,512]{1,0:T(8,128)(2,1)S(1)} collective-permute-done((bf16[80,512]{1,0:T(8,128)(2,1)S(1)}, bf16[80,512]{1,0:T(8,128)(2,1)S(1)}, u32[]{:S(2)}, u32[]{:S(2)}) %collective-permute-start.22) | collective-permute-done | bytes 81952 | tf_op jit(solution)/shard_map/ppermute | solution.py:495
  111.4 1.3 collective-permute-start.26
  112.6 3.3 %collective-permute-start.27 = (bf16[512,128]{1,0:T(8,128)(2,1)S(1)}, bf16[512,128]{1,0:T(8,128)(2,1)S(1)}, u32[]{:S(2)}, u32[]{:S(2)}) collective-permute-start(bf16[512,128]{1,0:T(8,128)(2,1)S(1)} %get-tuple-element.74), channel_id=1, source_target_pairs={{0,2},{1,3},{2,0},{3,1},{4,6},{5,7},{6,4},{7,5},{8,10},{9,11},{10,... | collective-permute-start | bytes 393224 | tf_op jit(solution)/shard_map/ppermute | solution.py:500
  116.0 2.4 %collective-permute-done.24 = bf16[80,512]{1,0:T(8,128)(2,1)S(1)} collective-permute-done((bf16[80,512]{1,0:T(8,128)(2,1)S(1)}, bf16[80,512]{1,0:T(8,128)(2,1)S(1)}, u32[]{:S(2)}, u32[]{:S(2)}) %collective-permute-start.24) | collective-permute-done | bytes 81952 | tf_op jit(solution)/shard_map/ppermute | solution.py:501
  118.5 1.2 collective-permute-done.27.t2
  119.7 1.5 collective-permute-done.28.t3
  121.2 2.6 %collective-permute-done.25.b = bf16[80,512]{1,0:T(8,128)(2,1)S(1)} collective-permute-done((bf16[80,512]{1,0:T(8,128)(2,1)S(1)}, bf16[80,512]{1,0:T(8,128)(2,1)S(1)}, u32[]{:S(2)}, u32[]{:S(2)}) %collective-permute-start.25) | collective-permute-done | bytes 81952 | tf_op jit(solution)/shard_map/ppermute | solution.py:503
  123.9 1.6 %collective-permute-start.29 = (bf16[80,512]{1,0:T(8,128)(2,1)S(1)}, bf16[80,512]{1,0:T(8,128)(2,1)S(1)}, u32[]{:S(2)}, u32[]{:S(2)}) collective-permute-start(bf16[80,512]{1,0:T(8,128)(2,1)S(1)} %get-tuple-element.76.a), channel_id=1, source_target_pairs={{0,16},{16,0},{1,17},{17,1},{2,18},{18,2},{3,19},{19,3},{4,20},{20... | collective-permute-start | bytes 245768 | tf_op jit(solution)/shard_map/ppermute | solution.py:509
  125.6 1.8 %collective-permute-done.29.b = bf16[80,512]{1,0:T(8,128)(2,1)S(1)} collective-permute-done((bf16[80,512]{1,0:T(8,128)(2,1)S(1)}, bf16[80,512]{1,0:T(8,128)(2,1)S(1)}, u32[]{:S(2)}, u32[]{:S(2)}) %collective-permute-start.29) | collective-permute-done | bytes 81952 | tf_op jit(solution)/shard_map/ppermute | solution.py:509
  127.4 1.4 collective-permute-start.32
  128.8 1.0 collective-permute-start.31
  130.3 2.0 %collective-permute-done.32.p2 = bf16[80,512]{1,0:T(8,128)(2,1)S(1)} collective-permute-done((bf16[80,512]{1,0:T(8,128)(2,1)S(1)}, bf16[80,512]{1,0:T(8,128)(2,1)S(1)}, u32[]{:S(2)}, u32[]{:S(2)}) %collective-permute-start.32) | collective-permute-done | bytes 81952 | tf_op jit(solution)/shard_map/ppermute | solution.py:514
  132.3 1.0 collective-permute-done.31.p3
  133.9 5.9 %collective-permute-start.33 = (bf16[320,512]{1,0:T(8,128)(2,1)S(1)}, bf16[320,512]{1,0:T(8,128)(2,1)S(1)}, u32[]{:S(2)}, u32[]{:S(2)}) collective-permute-start(bf16[320,512]{1,0:T(8,128)(2,1)S(1)} %shard_map.106.mine), channel_id=1, source_target_pairs={{0,4},{4,0},{1,5},{5,1},{2,6},{6,2},{3,7},{7,3},{8,12},{12,8},{9,1... | collective-permute-start | bytes 983048 | tf_op jit(solution)/shard_map/ppermute | solution.py:516
  139.9 5.0 %collective-permute-start.34 = (bf16[512,128]{1,0:T(8,128)(2,1)S(1)}, bf16[512,128]{1,0:T(8,128)(2,1)S(1)}, u32[]{:S(2)}, u32[]{:S(2)}) collective-permute-start(bf16[512,128]{1,0:T(8,128)(2,1)S(1)} %get-tuple-element.79), channel_id=1, source_target_pairs={{0,0},{64,4},{32,8},{96,12},{24,16},{88,20},{56,24},{120,28},{12,3... | collective-permute-start | bytes 393224 | tf_op jit(solution)/shard_map/ppermute | solution.py:513
  144.8 5.3 %collective-permute-done.34.grad = bf16[512,128]{1,0:T(8,128)(2,1)S(1)} collective-permute-done((bf16[512,128]{1,0:T(8,128)(2,1)S(1)}, bf16[512,128]{1,0:T(8,128)(2,1)S(1)}, u32[]{:S(2)}, u32[]{:S(2)}) %collective-permute-start.34) | collective-permute-done | bytes 131104 | tf_op jit(solution)/shard_map/ppermute | solution.py:513
  150.1 1.7 %shard_map.107 = (f32[512,512]{1,0:T(8,128)}, f32[128,512]{1,0:T(8,128)}, bf16[1,512,128]{2,1,0:T(8,128)(2,1)}) custom-call(s32[8]{0:T(128)S(1)} %concatenate.3.meta_ref, bf16[320,512]{1,0:T(8,128)(2,1)S(1)} %shard_map.106.mine, bf16[320,512]{1,0:T(8,128)(2,1)S(1)} %collective-permute-done.33.other, bf16[512,128]{1,0:T(8,128)(2,1)S(1)} %collective-permute-done.34.grad), custom_call_target="tpu_custom_call" | custom-call | bytes 2228256 | tf_op jit(solution)/shard_map/pallas_call | solution.py:73
  (49 shorter events, 11.1 us)
Async XLA Ops:
  0.6 28.4 %copy-start = (bf16[512,512]{1,0:T(8,128)(2,1)S(1)}, bf16[512,512]{1,0:T(8,128)(2,1)}, u32[]{:S(2)}) copy-start(bf16[512,512]{1,0:T(8,128)(2,1)} %w.1) | copy-start | bytes 1572868
  2.4 16.3 %collective-permute-start = (bf16[272,512]{1,0:T(8,128)(2,1)}, bf16[272,512]{1,0:T(8,128)(2,1)S(1)}, u32[]{:S(2)}, u32[]{:S(2)}) collective-permute-start(bf16[272,512]{1,0:T(8,128)(2,1)} %shard_map.94), channel_id=1, source_target_pairs={{0,0},{4,64},{8,32},{12,96},{16,24},{20,88},{24,56},{28,120},{32,1... | collective-permute-start | bytes 835592 | tf_op jit(solution)/shard_map/ppermute | solution.py:403
  18.8 9.2 %collective-permute-start.3 = (bf16[272,512]{1,0:T(8,128)(2,1)S(1)}, bf16[272,512]{1,0:T(8,128)(2,1)S(1)}, u32[]{:S(2)}, u32[]{:S(2)}) collective-permute-start(bf16[272,512]{1,0:T(8,128)(2,1)S(1)} %collective-permute-done.xa_ref.up0), channel_id=1, source_target_pairs={{0,3},{1,2},{2,1},{3,0},{4,7},{5,6},{6,5},{7,4},{8,11},{9,10},{10,... | collective-permute-start | bytes 835592 | tf_op jit(solution)/shard_map/ppermute | solution.py:406
  21.5 6.9 %collective-permute-start.2 = (bf16[272,512]{1,0:T(8,128)(2,1)S(1)}, bf16[272,512]{1,0:T(8,128)(2,1)S(1)}, u32[]{:S(2)}, u32[]{:S(2)}) collective-permute-start(bf16[272,512]{1,0:T(8,128)(2,1)S(1)} %collective-permute-done.xa_ref.up0), channel_id=1, source_target_pairs={{0,2},{1,3},{2,0},{3,1},{4,6},{5,7},{6,4},{7,5},{8,10},{9,11},{10,... | collective-permute-start | bytes 835592 | tf_op jit(solution)/shard_map/ppermute | solution.py:406
  21.8 7.2 %collective-permute-start.1 = (bf16[272,512]{1,0:T(8,128)(2,1)S(1)}, bf16[272,512]{1,0:T(8,128)(2,1)S(1)}, u32[]{:S(2)}, u32[]{:S(2)}) collective-permute-start(bf16[272,512]{1,0:T(8,128)(2,1)S(1)} %collective-permute-done.xa_ref.up0), channel_id=1, source_target_pairs={{0,1},{1,0},{2,3},{3,2},{4,5},{5,4},{6,7},{7,6},{8,9},{9,8},{10,11... | collective-permute-start | bytes 835592 | tf_op jit(solution)/shard_map/ppermute | solution.py:406
  24.7 4.3 %copy-start.2 = (f32[1,128]{1,0:T(1,128)S(1)}, f32[1,128]{1,0:T(1,128)}, u32[]{:S(2)}) copy-start(f32[1,128]{1,0:T(1,128)} %table_ref.1) | copy-start | bytes 1540
  30.3 13.3 %collective-permute-start.7 = (bf16[512,256]{1,0:T(8,128)(2,1)S(1)}, bf16[512,256]{1,0:T(8,128)(2,1)S(1)}, u32[]{:S(2)}, u32[]{:S(2)}) collective-permute-start(bf16[512,256]{1,0:T(8,128)(2,1)S(1)} %get-tuple-element.44.q0), channel_id=1, source_target_pairs={{0,16},{16,0},{1,17},{17,1},{2,18},{18,2},{3,19},{19,3},{4,20},{20... | collective-permute-start | bytes 786440 | tf_op jit(solution)/shard_map/ppermute | solution.py:426
  34.6 10.2 %collective-permute-start.6 = (bf16[528,256]{1,0:T(8,128)(2,1)S(1)}, bf16[528,256]{1,0:T(8,128)(2,1)S(1)}, u32[]{:S(2)}, u32[]{:S(2)}) collective-permute-start(bf16[528,256]{1,0:T(8,128)(2,1)S(1)} %get-tuple-element.43.kv0), channel_id=1, source_target_pairs={{0,128},{8,136},{128,0},{136,8},{1,129},{9,137},{129,1},{137,9},{2... | collective-permute-start | bytes 811016 | tf_op jit(solution)/shard_map/ppermute | solution.py:424
  36.8 17.6 %collective-permute-start.5 = (bf16[528,256]{1,0:T(8,128)(2,1)S(1)}, bf16[528,256]{1,0:T(8,128)(2,1)S(1)}, u32[]{:S(2)}, u32[]{:S(2)}) collective-permute-start(bf16[528,256]{1,0:T(8,128)(2,1)S(1)} %get-tuple-element.43.kv0), channel_id=1, source_target_pairs={{0,136},{8,128},{128,8},{136,0},{1,137},{9,129},{129,9},{137,1},{2... | collective-permute-start | bytes 811016 | tf_op jit(solution)/shard_map/ppermute | solution.py:424
  42.6 12.1 %collective-permute-start.4 = (bf16[528,256]{1,0:T(8,128)(2,1)S(1)}, bf16[528,256]{1,0:T(8,128)(2,1)S(1)}, u32[]{:S(2)}, u32[]{:S(2)}) collective-permute-start(bf16[528,256]{1,0:T(8,128)(2,1)S(1)} %get-tuple-element.43.kv0), channel_id=1, source_target_pairs={{0,8},{8,0},{128,136},{136,128},{1,9},{9,1},{129,137},{137,129},{2... | collective-permute-start | bytes 811016 | tf_op jit(solution)/shard_map/ppermute | solution.py:424
  42.7 2.1 %collective-permute-start.8 = (bf16[512,256]{1,0:T(8,128)(2,1)S(1)}, bf16[512,256]{1,0:T(8,128)(2,1)S(1)}, u32[]{:S(2)}, u32[]{:S(2)}) collective-permute-start(bf16[512,256]{1,0:T(8,128)(2,1)S(1)} %get-tuple-element.44.q0), channel_id=1, source_target_pairs={{0,4},{4,0},{1,5},{5,1},{2,6},{6,2},{3,7},{7,3},{8,12},{12,8},{9,1... | collective-permute-start | bytes 786440 | tf_op jit(solution)/shard_map/ppermute | solution.py:427
  43.7 11.1 %collective-permute-start.9 = (bf16[512,256]{1,0:T(8,128)(2,1)S(1)}, bf16[512,256]{1,0:T(8,128)(2,1)S(1)}, u32[]{:S(2)}, u32[]{:S(2)}) collective-permute-start(bf16[512,256]{1,0:T(8,128)(2,1)S(1)} %collective-permute-done.7.q1), channel_id=1, source_target_pairs={{0,4},{4,0},{1,5},{5,1},{2,6},{6,2},{3,7},{7,3},{8,12},{12,8},{9,1... | collective-permute-start | bytes 786440 | tf_op jit(solution)/shard_map/ppermute | solution.py:427
  56.9 2.5 %collective-permute-start.10 = (bf16[1024,128]{1,0:T(8,128)(2,1)S(1)}, bf16[1024,128]{1,0:T(8,128)(2,1)S(1)}, u32[]{:S(2)}, u32[]{:S(2)}) collective-permute-start(bf16[1024,128]{1,0:T(8,128)(2,1)S(1)} %get-tuple-element.49), channel_id=1, source_target_pairs={{0,4},{4,0},{1,5},{5,1},{2,6},{6,2},{3,7},{7,3},{8,12},{12,8},{9,1... | collective-permute-start | bytes 786440 | tf_op jit(solution)/shard_map/ppermute | solution.py:443
  59.4 4.8 %copy-start.1 = (bf16[128,512]{1,0:T(8,128)(2,1)S(1)}, bf16[128,512]{1,0:T(8,128)(2,1)}, u32[]{:S(2)}) copy-start(bf16[128,512]{1,0:T(8,128)(2,1)} %wout.1) | copy-start | bytes 393220
  59.5 4.8 %collective-permute-start.11 = (bf16[512,128]{1,0:T(8,128)(2,1)S(1)}, bf16[512,128]{1,0:T(8,128)(2,1)S(1)}, u32[]{:S(2)}, u32[]{:S(2)}) collective-permute-start(bf16[512,128]{1,0:T(8,128)(2,1)S(1)} %add_convert_fusion.1), channel_id=1, source_target_pairs={{0,16},{16,0},{1,17},{17,1},{2,18},{18,2},{3,19},{19,3},{4,20},{20... | collective-permute-start | bytes 393224 | tf_op jit(solution)/shard_map/ppermute | solution.py:445
  65.4 3.9 %collective-permute-start.12 = (bf16[512,128]{1,0:T(8,128)(2,1)S(1)}, bf16[512,128]{1,0:T(8,128)(2,1)S(1)}, u32[]{:S(2)}, u32[]{:S(2)}) collective-permute-start(bf16[512,128]{1,0:T(8,128)(2,1)S(1)} %get-tuple-element.52.g0), channel_id=1, source_target_pairs={{0,16},{16,0},{1,17},{17,1},{2,18},{18,2},{3,19},{19,3},{4,20},{20... | collective-permute-start | bytes 393224 | tf_op jit(solution)/shard_map/ppermute | solution.py:454
  66.4 5.2 %collective-permute-start.13 = (bf16[512,128]{1,0:T(8,128)(2,1)S(1)}, bf16[512,128]{1,0:T(8,128)(2,1)S(1)}, u32[]{:S(2)}, u32[]{:S(2)}) collective-permute-start(bf16[512,128]{1,0:T(8,128)(2,1)S(1)} %get-tuple-element.52.g0), channel_id=1, source_target_pairs={{0,4},{4,0},{1,5},{5,1},{2,6},{6,2},{3,7},{7,3},{8,12},{12,8},{9,1... | collective-permute-start | bytes 393224 | tf_op jit(solution)/shard_map/ppermute | solution.py:455
  69.3 3.3 %collective-permute-start.14 = (bf16[512,128]{1,0:T(8,128)(2,1)S(1)}, bf16[512,128]{1,0:T(8,128)(2,1)S(1)}, u32[]{:S(2)}, u32[]{:S(2)}) collective-permute-start(bf16[512,128]{1,0:T(8,128)(2,1)S(1)} %collective-permute-done.12.g1), channel_id=1, source_target_pairs={{0,4},{4,0},{1,5},{5,1},{2,6},{6,2},{3,7},{7,3},{8,12},{12,8},{9,1... | collective-permute-start | bytes 393224 | tf_op jit(solution)/shard_map/ppermute | solution.py:455
  75.7 11.2 %collective-permute-start.18 = (bf16[1024,128]{1,0:T(8,128)(2,1)S(1)}, bf16[1024,128]{1,0:T(8,128)(2,1)S(1)}, u32[]{:S(2)}, u32[]{:S(2)}) collective-permute-start(bf16[1024,128]{1,0:T(8,128)(2,1)S(1)} %get-tuple-element.58), channel_id=1, source_target_pairs={{0,4},{4,0},{1,5},{5,1},{2,6},{6,2},{3,7},{7,3},{8,12},{12,8},{9,1... | collective-permute-start | bytes 786440 | tf_op jit(solution)/shard_map/ppermute | solution.py:475
  76.2 13.8 %collective-permute-start.15 = (bf16[512,256]{1,0:T(8,128)(2,1)S(1)}, bf16[512,256]{1,0:T(8,128)(2,1)S(1)}, u32[]{:S(2)}, u32[]{:S(2)}) collective-permute-start(bf16[512,256]{1,0:T(8,128)(2,1)S(1)} %get-tuple-element.54), channel_id=1, source_target_pairs={{0,128},{8,136},{128,0},{136,8},{1,129},{9,137},{129,1},{137,9},{2... | collective-permute-start | bytes 786440 | tf_op jit(solution)/shard_map/ppermute | solution.py:474
  83.4 15.6 %collective-permute-start.16 = (bf16[512,256]{1,0:T(8,128)(2,1)S(1)}, bf16[512,256]{1,0:T(8,128)(2,1)S(1)}, u32[]{:S(2)}, u32[]{:S(2)}) collective-permute-start(bf16[512,256]{1,0:T(8,128)(2,1)S(1)} %get-tuple-element.55), channel_id=1, source_target_pairs={{0,8},{8,0},{128,136},{136,128},{1,9},{9,1},{129,137},{137,129},{2... | collective-permute-start | bytes 786440 | tf_op jit(solution)/shard_map/ppermute | solution.py:472
  87.0 12.0 %collective-permute-start.17 = (bf16[512,256]{1,0:T(8,128)(2,1)S(1)}, bf16[512,256]{1,0:T(8,128)(2,1)S(1)}, u32[]{:S(2)}, u32[]{:S(2)}) collective-permute-start(bf16[512,256]{1,0:T(8,128)(2,1)S(1)} %get-tuple-element.56), channel_id=1, source_target_pairs={{0,136},{8,128},{128,8},{136,0},{1,137},{9,129},{129,9},{137,1},{2... | collective-permute-start | bytes 786440 | tf_op jit(solution)/shard_map/ppermute | solution.py:473
  87.0 12.0 %collective-permute-start.19 = (bf16[512,128]{1,0:T(8,128)(2,1)S(1)}, bf16[512,128]{1,0:T(8,128)(2,1)S(1)}, u32[]{:S(2)}, u32[]{:S(2)}) collective-permute-start(bf16[512,128]{1,0:T(8,128)(2,1)S(1)} %add_convert_fusion), channel_id=1, source_target_pairs={{0,16},{16,0},{1,17},{17,1},{2,18},{18,2},{3,19},{19,3},{4,20},{20... | collective-permute-start | bytes 393224 | tf_op jit(solution)/shard_map/ppermute | solution.py:477
  100.7 2.2 %collective-permute-start.20 = (bf16[320,512]{1,0:T(8,128)(2,1)S(1)}, bf16[320,512]{1,0:T(8,128)(2,1)S(1)}, u32[]{:S(2)}, u32[]{:S(2)}) collective-permute-start(bf16[320,512]{1,0:T(8,128)(2,1)S(1)} %get-tuple-element.63), channel_id=1, source_target_pairs={{0,4},{4,0},{1,5},{5,1},{2,6},{6,2},{3,7},{7,3},{8,12},{12,8},{9,1... | collective-permute-start | bytes 983048 | tf_op jit(solution)/shard_map/ppermute | solution.py:487
  103.5 5.2 %collective-permute-start.21 = (bf16[80,512]{1,0:T(8,128)(2,1)S(1)}, bf16[80,512]{1,0:T(8,128)(2,1)S(1)}, u32[]{:S(2)}, u32[]{:S(2)}) collective-permute-start(bf16[80,512]{1,0:T(8,128)(2,1)S(1)} %get-tuple-element.65), channel_id=1, source_target_pairs={{0,128},{8,136},{128,0},{136,8},{1,129},{9,137},{129,1},{137,9},{2... | collective-permute-start | bytes 245768 | tf_op jit(solution)/shard_map/ppermute | solution.py:495
  104.2 6.3 %collective-permute-start.22 = (bf16[80,512]{1,0:T(8,128)(2,1)S(1)}, bf16[80,512]{1,0:T(8,128)(2,1)S(1)}, u32[]{:S(2)}, u32[]{:S(2)}) collective-permute-start(bf16[80,512]{1,0:T(8,128)(2,1)S(1)} %get-tuple-element.66), channel_id=1, source_target_pairs={{0,8},{8,0},{128,136},{136,128},{1,9},{9,1},{129,137},{137,129},{2... | collective-permute-start | bytes 245768 | tf_op jit(solution)/shard_map/ppermute | solution.py:495
  106.6 4.5 %collective-permute-start.23 = (bf16[80,512]{1,0:T(8,128)(2,1)S(1)}, bf16[80,512]{1,0:T(8,128)(2,1)S(1)}, u32[]{:S(2)}, u32[]{:S(2)}) collective-permute-start(bf16[80,512]{1,0:T(8,128)(2,1)S(1)} %get-tuple-element.67), channel_id=1, source_target_pairs={{0,136},{8,128},{128,8},{136,0},{1,137},{9,129},{129,9},{137,1},{2... | collective-permute-start | bytes 245768 | tf_op jit(solution)/shard_map/ppermute | solution.py:495
  111.1 7.3 %collective-permute-start.24 = (bf16[80,512]{1,0:T(8,128)(2,1)S(1)}, bf16[80,512]{1,0:T(8,128)(2,1)S(1)}, u32[]{:S(2)}, u32[]{:S(2)}) collective-permute-start(bf16[80,512]{1,0:T(8,128)(2,1)S(1)} %get-tuple-element.71), channel_id=1, source_target_pairs={{0,64},{64,0},{1,65},{65,1},{2,66},{66,2},{3,67},{67,3},{4,68},{68... | collective-permute-start | bytes 245768 | tf_op jit(solution)/shard_map/ppermute | solution.py:501
  111.4 7.2 %collective-permute-start.26 = (bf16[512,128]{1,0:T(8,128)(2,1)S(1)}, bf16[512,128]{1,0:T(8,128)(2,1)S(1)}, u32[]{:S(2)}, u32[]{:S(2)}) collective-permute-start(bf16[512,128]{1,0:T(8,128)(2,1)S(1)} %get-tuple-element.73), channel_id=1, source_target_pairs={{0,1},{1,0},{2,3},{3,2},{4,5},{5,4},{6,7},{7,6},{8,9},{9,8},{10,11... | collective-permute-start | bytes 393224 | tf_op jit(solution)/shard_map/ppermute | solution.py:500
  112.6 7.1 %collective-permute-start.27 = (bf16[512,128]{1,0:T(8,128)(2,1)S(1)}, bf16[512,128]{1,0:T(8,128)(2,1)S(1)}, u32[]{:S(2)}, u32[]{:S(2)}) collective-permute-start(bf16[512,128]{1,0:T(8,128)(2,1)S(1)} %get-tuple-element.74), channel_id=1, source_target_pairs={{0,2},{1,3},{2,0},{3,1},{4,6},{5,7},{6,4},{7,5},{8,10},{9,11},{10,... | collective-permute-start | bytes 393224 | tf_op jit(solution)/shard_map/ppermute | solution.py:500
  115.9 5.3 %collective-permute-start.28 = (bf16[512,128]{1,0:T(8,128)(2,1)S(1)}, bf16[512,128]{1,0:T(8,128)(2,1)S(1)}, u32[]{:S(2)}, u32[]{:S(2)}) collective-permute-start(bf16[512,128]{1,0:T(8,128)(2,1)S(1)} %get-tuple-element.75), channel_id=1, source_target_pairs={{0,3},{1,2},{2,1},{3,0},{4,7},{5,6},{6,5},{7,4},{8,11},{9,10},{10,... | collective-permute-start | bytes 393224 | tf_op jit(solution)/shard_map/ppermute | solution.py:500
  118.4 5.5 %collective-permute-start.25 = (bf16[80,512]{1,0:T(8,128)(2,1)S(1)}, bf16[80,512]{1,0:T(8,128)(2,1)S(1)}, u32[]{:S(2)}, u32[]{:S(2)}) collective-permute-start(bf16[80,512]{1,0:T(8,128)(2,1)S(1)} %add_convert_fusion.2.a), channel_id=1, source_target_pairs={{0,32},{32,0},{1,33},{33,1},{2,34},{34,2},{3,35},{35,3},{4,36},{36... | collective-permute-start | bytes 245768 | tf_op jit(solution)/shard_map/ppermute | solution.py:503
  123.9 3.4 %collective-permute-start.29 = (bf16[80,512]{1,0:T(8,128)(2,1)S(1)}, bf16[80,512]{1,0:T(8,128)(2,1)S(1)}, u32[]{:S(2)}, u32[]{:S(2)}) collective-permute-start(bf16[80,512]{1,0:T(8,128)(2,1)S(1)} %get-tuple-element.76.a), channel_id=1, source_target_pairs={{0,16},{16,0},{1,17},{17,1},{2,18},{18,2},{3,19},{19,3},{4,20},{20... | collective-permute-start | bytes 245768 | tf_op jit(solution)/shard_map/ppermute | solution.py:509
  127.4 4.9 %collective-permute-start.32 = (bf16[80,512]{1,0:T(8,128)(2,1)S(1)}, bf16[80,512]{1,0:T(8,128)(2,1)S(1)}, u32[]{:S(2)}, u32[]{:S(2)}) collective-permute-start(bf16[80,512]{1,0:T(8,128)(2,1)S(1)} %get-tuple-element.78.p0), channel_id=1, source_target_pairs={{0,128},{8,136},{128,0},{136,8},{1,129},{9,137},{129,1},{137,9},{2... | collective-permute-start | bytes 245768 | tf_op jit(solution)/shard_map/ppermute | solution.py:514
  128.8 4.5 %collective-permute-start.31 = (bf16[80,512]{1,0:T(8,128)(2,1)S(1)}, bf16[80,512]{1,0:T(8,128)(2,1)S(1)}, u32[]{:S(2)}, u32[]{:S(2)}) collective-permute-start(bf16[80,512]{1,0:T(8,128)(2,1)S(1)} %get-tuple-element.78.p0), channel_id=1, source_target_pairs={{0,136},{8,128},{128,8},{136,0},{1,137},{9,129},{129,9},{137,1},{2... | collective-permute-start | bytes 245768 | tf_op jit(solution)/shard_map/ppermute | solution.py:514
  129.8 3.5 %collective-permute-start.30 = (bf16[80,512]{1,0:T(8,128)(2,1)S(1)}, bf16[80,512]{1,0:T(8,128)(2,1)S(1)}, u32[]{:S(2)}, u32[]{:S(2)}) collective-permute-start(bf16[80,512]{1,0:T(8,128)(2,1)S(1)} %get-tuple-element.78.p0), channel_id=1, source_target_pairs={{0,8},{8,0},{128,136},{136,128},{1,9},{9,1},{129,137},{137,129},{2... | collective-permute-start | bytes 245768 | tf_op jit(solution)/shard_map/ppermute | solution.py:514
  133.9 16.2 %collective-permute-start.33 = (bf16[320,512]{1,0:T(8,128)(2,1)S(1)}, bf16[320,512]{1,0:T(8,128)(2,1)S(1)}, u32[]{:S(2)}, u32[]{:S(2)}) collective-permute-start(bf16[320,512]{1,0:T(8,128)(2,1)S(1)} %shard_map.106.mine), channel_id=1, source_target_pairs={{0,4},{4,0},{1,5},{5,1},{2,6},{6,2},{3,7},{7,3},{8,12},{12,8},{9,1... | collective-permute-start | bytes 983048 | tf_op jit(solution)/shard_map/ppermute | solution.py:516
  139.9 10.3 %collective-permute-start.34 = (bf16[512,128]{1,0:T(8,128)(2,1)S(1)}, bf16[512,128]{1,0:T(8,128)(2,1)S(1)}, u32[]{:S(2)}, u32[]{:S(2)}) collective-permute-start(bf16[512,128]{1,0:T(8,128)(2,1)S(1)} %get-tuple-element.79), channel_id=1, source_target_pairs={{0,0},{64,4},{32,8},{96,12},{24,16},{88,20},{56,24},{120,28},{12,3... | collective-permute-start | bytes 393224 | tf_op jit(solution)/shard_map/ppermute | solution.py:513

commit v6 on v4

--- a/solution.py
+++ b/solution.py
@@ -494,9 +494,9 @@
         sum_kernel, [((PIECE, WIDTH), BF)], (p0, g2, g1, g3, t1, t2, t3), passed=3
     )
     u1, u3, u2 = (lax.ppermute(t, "y", flip_y[rel]) for t, rel in ((t1, 1), (t3, 3), (t2, 2)))
+    other = lax.ppermute(total, "z1", FLIP)
+    total = (total.astype(F32) + other.astype(F32)).astype(BF)
     other = lax.ppermute(total, "z2", FLIP)
-    total = (total.astype(F32) + other.astype(F32)).astype(BF)
-    other = lax.ppermute(total, "z1", FLIP)
     total, grad_local = call(
         both_kernel,
         [((PIECE, WIDTH), BF), ((ROWS, DH), BF)],

time: 144 us -> 146 us (1.014); the launches traced: 144 us -> 144 us
  starting transfers between devices: 72.3 us -> 65.5 us
  waiting for transfers between devices: 51.4 us -> 55.5 us
  Pallas kernels: 16.6 us -> 19.7 us
    ppermute x1, starting transfers between devices: 7.31 us -> 0.09 us  [body(): other = lax.ppermute(total, 'z1', FLIP)]
    ppermute x3, waiting for transfers between devices: 0.01 us -> 5.24 us  [body(): lax.ppermute(t, 'y', flip_y[rel])]
    ppermute x1, starting transfers between devices: 1.08 us -> 4.59 us  [body(): r2 = lax.ppermute(s2, ('xh', 'xl'), flip_x(2))]
    ppermute x3, starting transfers between devices: 2.87 us -> 6.34 us  [body(): lax.ppermute(total, ('xh', 'xl'), flip_x(rel))]
    ppermute x1, starting transfers between devices: 9.34 us -> 6.08 us  [body(): grad_local = lax.ppermute(grad_local, MOVED, HOME)]
    ppermute x1, starting transfers between devices: 3.26 us -> 0.09 us  [body(): other = lax.ppermute(total, 'z2', FLIP)]
    pallas_call x13, Pallas kernels: 16.6 us -> 19.7 us  [call(): pl.pallas_call(kernel, out_shape=[jax.ShapeDtypeStruct(s, t) for s, t in...]
    ppermute x1, waiting for transfers between devices: 0.01 us -> 2.82 us  [body(): other = lax.ppermute(total, 'z2', FLIP)]
  transfers between devices with their start and end apart: 35 -> 35, of which waited for: 21 -> 24; matrix products, arithmetic and copies ran while one was open for 1% -> 1% of each run, Pallas kernels for 1% -> 1%
where the time goes in v6:
time: 146 us; the launch traced here: 144 us
  starting transfers between devices  65.5 us (45%)
  waiting for transfers between devices  55.5 us (38%)
  Pallas kernels  19.7 us (13%)
  between operations  2.14 us (1%)
    pallas_call x13, Pallas kernels, call(): pl.pallas_call(kernel, out_shape=[jax.ShapeDtypeStruct(s, t) for s, t in...  19.7 us
    ppermute x1, starting transfers between devices, body(): xa = lax.ppermute(xa, MOVED, AWAY)  10.2 us
    ppermute x3, waiting for transfers between devices, body(): lax.ppermute(kv, ('xh', 'xl'), flip_x(rel))  9.92 us
    ppermute x3, starting transfers between devices, body(): lax.ppermute(kv, ('xh', 'xl'), flip_x(rel))  8.1 us
    ppermute x1, waiting for transfers between devices, body(): r1 = lax.ppermute(s1, ('xh', 'xl'), flip_x(1))  7.27 us
    ppermute x3, starting transfers between devices, body(): lax.ppermute(total, ('xh', 'xl'), flip_x(rel))  6.34 us
    ppermute x1, starting transfers between devices, body(): grad_local = lax.ppermute(grad_local, MOVED, HOME)  6.08 us
    ppermute x1, waiting for transfers between devices, body(): xa = lax.ppermute(xa, MOVED, AWAY)  6.08 us
  transfers between devices with their start and end apart: 35, of which 24 were waited for; matrix products, arithmetic and copies ran while one was open for 1% of the time, Pallas kernels for 1%

profile of v6, /device:TPU:1, one launch (start us, length us, event | category | flops | bytes accessed | tf_op | source)
XLA Modules:
  0.0 144.3 jit_solution(524031569058370672)
XLA Ops:
  0.6 1.8 %shard_map.94 = bf16[272,512]{1,0:T(8,128)(2,1)} custom-call(bf16[512,512]{1,0:T(8,128)(2,1)} %bitcast.8, s32[1,512]{1,0:T(1,128)} %times_hbm.1, s32[1,3]{1,0:T(1,128)} %lengths_hbm.1, bf16[512,512]{1,0:T(8,128)(2,1)} %bitcast.9), custom_call_target="tpu_custom_call" | custom-call | bytes 1329164 | tf_op jit(solution)/shard_map/pallas_call | solution.py:73
  2.4 10.2 %collective-permute-start = (bf16[272,512]{1,0:T(8,128)(2,1)}, bf16[272,512]{1,0:T(8,128)(2,1)S(1)}, u32[]{:S(2)}, u32[]{:S(2)}) collective-permute-start(bf16[272,512]{1,0:T(8,128)(2,1)} %shard_map.94), channel_id=1, source_target_pairs={{0,0},{4,64},{8,32},{12,96},{16,24},{20,88},{24,56},{28,120},{32,1... | collective-permute-start | bytes 835592 | tf_op jit(solution)/shard_map/ppermute | solution.py:399
  12.7 6.1 %collective-permute-done.xa_ref.up0 = bf16[272,512]{1,0:T(8,128)(2,1)S(1)} collective-permute-done((bf16[272,512]{1,0:T(8,128)(2,1)}, bf16[272,512]{1,0:T(8,128)(2,1)S(1)}, u32[]{:S(2)}, u32[]{:S(2)}) %collective-permute-start) | collective-permute-done | bytes 278560 | tf_op jit(solution)/shard_map/ppermute | solution.py:399
  18.8 2.7 %collective-permute-start.3 = (bf16[272,512]{1,0:T(8,128)(2,1)S(1)}, bf16[272,512]{1,0:T(8,128)(2,1)S(1)}, u32[]{:S(2)}, u32[]{:S(2)}) collective-permute-start(bf16[272,512]{1,0:T(8,128)(2,1)S(1)} %collective-permute-done.xa_ref.up0), channel_id=1, source_target_pairs={{0,3},{1,2},{2,1},{3,0},{4,7},{5,6},{6,5},{7,4},{8,11},{9,10},{10,... | collective-permute-start | bytes 835592 | tf_op jit(solution)/shard_map/ppermute | solution.py:402
  24.7 1.7 %shard_map.95._.list_ref = s32[128]{0:T(128)S(1)} custom-call(s32[8]{0:T(128)S(1)} %concatenate.3.meta_ref), custom_call_target="tpu_custom_call" | custom-call | bytes 544 | tf_op jit(solution)/shard_map/pallas_call | solution.py:73
  26.4 1.6 %collective-permute-done.3.x3.up3 = bf16[272,512]{1,0:T(8,128)(2,1)S(1)} collective-permute-done((bf16[272,512]{1,0:T(8,128)(2,1)S(1)}, bf16[272,512]{1,0:T(8,128)(2,1)S(1)}, u32[]{:S(2)}, u32[]{:S(2)}) %collective-permute-start.3) | collective-permute-done | bytes 278560 | tf_op jit(solution)/shard_map/ppermute | solution.py:402
  29.0 1.3 shard_map.96
  30.3 4.3 %collective-permute-start.7 = (bf16[512,256]{1,0:T(8,128)(2,1)S(1)}, bf16[512,256]{1,0:T(8,128)(2,1)S(1)}, u32[]{:S(2)}, u32[]{:S(2)}) collective-permute-start(bf16[512,256]{1,0:T(8,128)(2,1)S(1)} %get-tuple-element.42.q0), channel_id=1, source_target_pairs={{0,16},{16,0},{1,17},{17,1},{2,18},{18,2},{3,19},{19,3},{4,20},{20... | collective-permute-start | bytes 786440 | tf_op jit(solution)/shard_map/ppermute | solution.py:422
  34.6 2.2 %collective-permute-start.6 = (bf16[528,256]{1,0:T(8,128)(2,1)S(1)}, bf16[528,256]{1,0:T(8,128)(2,1)S(1)}, u32[]{:S(2)}, u32[]{:S(2)}) collective-permute-start(bf16[528,256]{1,0:T(8,128)(2,1)S(1)} %get-tuple-element.41.kv0), channel_id=1, source_target_pairs={{0,128},{8,136},{128,0},{136,8},{1,129},{9,137},{129,1},{137,9},{2... | collective-permute-start | bytes 811016 | tf_op jit(solution)/shard_map/ppermute | solution.py:420
  36.8 5.8 %collective-permute-start.5 = (bf16[528,256]{1,0:T(8,128)(2,1)S(1)}, bf16[528,256]{1,0:T(8,128)(2,1)S(1)}, u32[]{:S(2)}, u32[]{:S(2)}) collective-permute-start(bf16[528,256]{1,0:T(8,128)(2,1)S(1)} %get-tuple-element.41.kv0), channel_id=1, source_target_pairs={{0,136},{8,128},{128,8},{136,0},{1,137},{9,129},{129,9},{137,1},{2... | collective-permute-start | bytes 811016 | tf_op jit(solution)/shard_map/ppermute | solution.py:420
  42.7 1.0 collective-permute-start.8
  43.7 1.2 collective-permute-done.8.q2
  44.8 9.6 %collective-permute-done.5.kv3 = bf16[528,256]{1,0:T(8,128)(2,1)S(1)} collective-permute-done((bf16[528,256]{1,0:T(8,128)(2,1)S(1)}, bf16[528,256]{1,0:T(8,128)(2,1)S(1)}, u32[]{:S(2)}, u32[]{:S(2)}) %collective-permute-start.5) | collective-permute-done | bytes 270368 | tf_op jit(solution)/shard_map/ppermute | solution.py:420
  54.7 3.3 %shard_map.97 = (f32[1024,128]{1,0:T(8,128)S(1)}, bf16[1024,128]{1,0:T(8,128)(2,1)S(1)}, bf16[8,256,256]{2,1,0:T(8,128)(2,1)S(1)}, bf16[8,256,128]{2,1,0:T(8,128)(2,1)S(1)}, bf16[8,256,256]{2,1,0:T(8,128)(2,1)S(1)}) custom-call(s32[8]{0:T(128)S(1)} %concatenate.3.meta_ref, bf16[528,256]{1,0:T(8,128)(2,1)S(1)} %get-tuple-element.41.kv0, ...), custom_call_target="tpu_custom_call" | custom-call | flops 1006632960 | bytes 5538336 | tf_op jit(solution)/shard_map/pallas_call | solution.py:73
  58.1 1.3 collective-permute-start.10
  59.4 1.2 collective-permute-done.10.got_core
  60.6 1.5 %collective-permute-start.11 = (bf16[512,128]{1,0:T(8,128)(2,1)S(1)}, bf16[512,128]{1,0:T(8,128)(2,1)S(1)}, u32[]{:S(2)}, u32[]{:S(2)}) collective-permute-start(bf16[512,128]{1,0:T(8,128)(2,1)S(1)} %add_convert_fusion.1), channel_id=1, source_target_pairs={{0,16},{16,0},{1,17},{17,1},{2,18},{18,2},{3,19},{19,3},{4,20},{20... | collective-permute-start | bytes 393224 | tf_op jit(solution)/shard_map/ppermute | solution.py:441
  62.0 3.3 %collective-permute-done.11.got_z = bf16[512,128]{1,0:T(8,128)(2,1)S(1)} collective-permute-done((bf16[512,128]{1,0:T(8,128)(2,1)S(1)}, bf16[512,128]{1,0:T(8,128)(2,1)S(1)}, u32[]{:S(2)}, u32[]{:S(2)}) %collective-permute-start.11) | collective-permute-done | bytes 131104 | tf_op jit(solution)/shard_map/ppermute | solution.py:441
  65.4 1.1 shard_map.98
  66.5 1.5 %collective-permute-start.12 = (bf16[512,128]{1,0:T(8,128)(2,1)S(1)}, bf16[512,128]{1,0:T(8,128)(2,1)S(1)}, u32[]{:S(2)}, u32[]{:S(2)}) collective-permute-start(bf16[512,128]{1,0:T(8,128)(2,1)S(1)} %get-tuple-element.50.g0), channel_id=1, source_target_pairs={{0,16},{16,0},{1,17},{17,1},{2,18},{18,2},{3,19},{19,3},{4,20},{20... | collective-permute-start | bytes 393224 | tf_op jit(solution)/shard_map/ppermute | solution.py:450
  67.9 1.5 %collective-permute-start.13 = (bf16[512,128]{1,0:T(8,128)(2,1)S(1)}, bf16[512,128]{1,0:T(8,128)(2,1)S(1)}, u32[]{:S(2)}, u32[]{:S(2)}) collective-permute-start(bf16[512,128]{1,0:T(8,128)(2,1)S(1)} %get-tuple-element.50.g0), channel_id=1, source_target_pairs={{0,4},{4,0},{1,5},{5,1},{2,6},{6,2},{3,7},{7,3},{8,12},{12,8},{9,1... | collective-permute-start | bytes 393224 | tf_op jit(solution)/shard_map/ppermute | solution.py:451
  69.4 1.0 collective-permute-done.12.g1
  70.4 2.4 %collective-permute-start.14 = (bf16[512,128]{1,0:T(8,128)(2,1)S(1)}, bf16[512,128]{1,0:T(8,128)(2,1)S(1)}, u32[]{:S(2)}, u32[]{:S(2)}) collective-permute-start(bf16[512,128]{1,0:T(8,128)(2,1)S(1)} %collective-permute-done.12.g1), channel_id=1, source_target_pairs={{0,4},{4,0},{1,5},{5,1},{2,6},{6,2},{3,7},{7,3},{8,12},{12,8},{9,1... | collective-permute-start | bytes 393224 | tf_op jit(solution)/shard_map/ppermute | solution.py:451
  72.8 1.0 collective-permute-done.14.g3
  73.7 5.5 %shard_map.99 = (f32[512,256]{1,0:T(8,128)S(1)}, bf16[512,256]{1,0:T(8,128)(2,1)S(1)}, bf16[512,256]{1,0:T(8,128)(2,1)S(1)}, bf16[512,256]{1,0:T(8,128)(2,1)S(1)...) custom-call(s32[8]{0:T(128)S(1)} %concatenate.3.meta_ref, s32[128]{0:T(128)S(1)} %shard_map.95._.list_ref, ...), custom_call_target="tpu_custom_call" | custom-call | flops 2013265920 | bytes 5243424 | tf_op jit(solution)/shard_map/pallas_call | solution.py:73
  79.7 4.6 %collective-permute-start.15 = (bf16[512,256]{1,0:T(8,128)(2,1)S(1)}, bf16[512,256]{1,0:T(8,128)(2,1)S(1)}, u32[]{:S(2)}, u32[]{:S(2)}) collective-permute-start(bf16[512,256]{1,0:T(8,128)(2,1)S(1)} %get-tuple-element.52), channel_id=1, source_target_pairs={{0,128},{8,136},{128,0},{136,8},{1,129},{9,137},{129,1},{137,9},{2... | collective-permute-start | bytes 786440 | tf_op jit(solution)/shard_map/ppermute | solution.py:470
  84.3 1.9 %collective-permute-start.16 = (bf16[512,256]{1,0:T(8,128)(2,1)S(1)}, bf16[512,256]{1,0:T(8,128)(2,1)S(1)}, u32[]{:S(2)}, u32[]{:S(2)}) collective-permute-start(bf16[512,256]{1,0:T(8,128)(2,1)S(1)} %get-tuple-element.53), channel_id=1, source_target_pairs={{0,8},{8,0},{128,136},{136,128},{1,9},{9,1},{129,137},{137,129},{2... | collective-permute-start | bytes 786440 | tf_op jit(solution)/shard_map/ppermute | solution.py:468
  86.2 1.4 %collective-permute-start.19 = (bf16[512,128]{1,0:T(8,128)(2,1)S(1)}, bf16[512,128]{1,0:T(8,128)(2,1)S(1)}, u32[]{:S(2)}, u32[]{:S(2)}) collective-permute-start(bf16[512,128]{1,0:T(8,128)(2,1)S(1)} %add_convert_fusion), channel_id=1, source_target_pairs={{0,16},{16,0},{1,17},{17,1},{2,18},{18,2},{3,19},{19,3},{4,20},{20... | collective-permute-start | bytes 393224 | tf_op jit(solution)/shard_map/ppermute | solution.py:473
  88.0 2.9 %collective-permute-done.15.r2 = bf16[512,256]{1,0:T(8,128)(2,1)S(1)} collective-permute-done((bf16[512,256]{1,0:T(8,128)(2,1)S(1)}, bf16[512,256]{1,0:T(8,128)(2,1)S(1)}, u32[]{:S(2)}, u32[]{:S(2)}) %collective-permute-start.15) | collective-permute-done | bytes 262176 | tf_op jit(solution)/shard_map/ppermute | solution.py:470
  90.8 7.3 %collective-permute-done.16.r1 = bf16[512,256]{1,0:T(8,128)(2,1)S(1)} collective-permute-done((bf16[512,256]{1,0:T(8,128)(2,1)S(1)}, bf16[512,256]{1,0:T(8,128)(2,1)S(1)}, u32[]{:S(2)}, u32[]{:S(2)}) %collective-permute-start.16) | collective-permute-done | bytes 262176 | tf_op jit(solution)/shard_map/ppermute | solution.py:468
  98.1 1.7 %shard_map.101 = (f32[512,128]{1,0:T(8,128)S(1)}, bf16[512,128]{1,0:T(8,128)(2,1)S(1)}, bf16[512,128]{1,0:T(8,128)(2,1)S(1)}, bf16[512,128]{1,0:T(8,128)(2,1)S(1...) custom-call(s32[8]{0:T(128)S(1)} %concatenate.3.meta_ref, f32[512,256]{1,0:T(8,128)S(1)} %get-tuple-element.51.own, ...), custom_call_target="tpu_custom_call" | custom-call | flops 536870912 | bytes 6357024 | tf_op jit(solution)/shard_map/pallas_call | solution.py:73
  99.8 1.1 collective-permute-start.20
  100.8 1.3 collective-permute-done.20.got
  102.8 1.2 collective-permute-start.21
  103.9 1.9 %collective-permute-start.22 = (bf16[80,512]{1,0:T(8,128)(2,1)S(1)}, bf16[80,512]{1,0:T(8,128)(2,1)S(1)}, u32[]{:S(2)}, u32[]{:S(2)}) collective-permute-start(bf16[80,512]{1,0:T(8,128)(2,1)S(1)} %get-tuple-element.64), channel_id=1, source_target_pairs={{0,8},{8,0},{128,136},{136,128},{1,9},{9,1},{129,137},{137,129},{2... | collective-permute-start | bytes 245768 | tf_op jit(solution)/shard_map/ppermute | solution.py:491
  106.1 1.9 %collective-permute-done.21.p1 = bf16[80,512]{1,0:T(8,128)(2,1)S(1)} collective-permute-done((bf16[80,512]{1,0:T(8,128)(2,1)S(1)}, bf16[80,512]{1,0:T(8,128)(2,1)S(1)}, u32[]{:S(2)}, u32[]{:S(2)}) %collective-permute-start.21) | collective-permute-done | bytes 81952 | tf_op jit(solution)/shard_map/ppermute | solution.py:491
  108.0 1.7 %collective-permute-done.22.p2 = bf16[80,512]{1,0:T(8,128)(2,1)S(1)} collective-permute-done((bf16[80,512]{1,0:T(8,128)(2,1)S(1)}, bf16[80,512]{1,0:T(8,128)(2,1)S(1)}, u32[]{:S(2)}, u32[]{:S(2)}) %collective-permute-start.22) | collective-permute-done | bytes 81952 | tf_op jit(solution)/shard_map/ppermute | solution.py:491
  110.4 1.4 collective-permute-start.26
  111.9 2.6 %collective-permute-start.27 = (bf16[512,128]{1,0:T(8,128)(2,1)S(1)}, bf16[512,128]{1,0:T(8,128)(2,1)S(1)}, u32[]{:S(2)}, u32[]{:S(2)}) collective-permute-start(bf16[512,128]{1,0:T(8,128)(2,1)S(1)} %get-tuple-element.72), channel_id=1, source_target_pairs={{0,2},{1,3},{2,0},{3,1},{4,6},{5,7},{6,4},{7,5},{8,10},{9,11},{10,... | collective-permute-start | bytes 393224 | tf_op jit(solution)/shard_map/ppermute | solution.py:496
  114.7 3.7 %collective-permute-done.27.t2 = bf16[512,128]{1,0:T(8,128)(2,1)S(1)} collective-permute-done((bf16[512,128]{1,0:T(8,128)(2,1)S(1)}, bf16[512,128]{1,0:T(8,128)(2,1)S(1)}, u32[]{:S(2)}, u32[]{:S(2)}) %collective-permute-start.27) | collective-permute-done | bytes 131104 | tf_op jit(solution)/shard_map/ppermute | solution.py:496
  118.4 1.5 %collective-permute-done.28.t3 = bf16[512,128]{1,0:T(8,128)(2,1)S(1)} collective-permute-done((bf16[512,128]{1,0:T(8,128)(2,1)S(1)}, bf16[512,128]{1,0:T(8,128)(2,1)S(1)}, u32[]{:S(2)}, u32[]{:S(2)}) %collective-permute-start.28) | collective-permute-done | bytes 131104 | tf_op jit(solution)/shard_map/ppermute | solution.py:496
  120.0 2.8 %collective-permute-done.25.b = bf16[80,512]{1,0:T(8,128)(2,1)S(1)} collective-permute-done((bf16[80,512]{1,0:T(8,128)(2,1)S(1)}, bf16[80,512]{1,0:T(8,128)(2,1)S(1)}, u32[]{:S(2)}, u32[]{:S(2)}) %collective-permute-start.25) | collective-permute-done | bytes 81952 | tf_op jit(solution)/shard_map/ppermute | solution.py:499
  123.5 6.1 %collective-permute-start.33 = (bf16[512,128]{1,0:T(8,128)(2,1)S(1)}, bf16[512,128]{1,0:T(8,128)(2,1)S(1)}, u32[]{:S(2)}, u32[]{:S(2)}) collective-permute-start(bf16[512,128]{1,0:T(8,128)(2,1)S(1)} %get-tuple-element.75), channel_id=1, source_target_pairs={{0,0},{64,4},{32,8},{96,12},{24,16},{88,20},{56,24},{120,28},{12,3... | collective-permute-start | bytes 393224 | tf_op jit(solution)/shard_map/ppermute | solution.py:505
  129.7 1.2 collective-permute-start.32
  130.9 5.1 %collective-permute-start.31 = (bf16[80,512]{1,0:T(8,128)(2,1)S(1)}, bf16[80,512]{1,0:T(8,128)(2,1)S(1)}, u32[]{:S(2)}, u32[]{:S(2)}) collective-permute-start(bf16[80,512]{1,0:T(8,128)(2,1)S(1)} %add_convert_fusion.2.p0), channel_id=1, source_target_pairs={{0,136},{8,128},{128,8},{136,0},{1,137},{9,129},{129,9},{137,1},{2... | collective-permute-start | bytes 245768 | tf_op jit(solution)/shard_map/ppermute | solution.py:508
  136.0 3.8 %collective-permute-done.31.p3 = bf16[80,512]{1,0:T(8,128)(2,1)S(1)} collective-permute-done((bf16[80,512]{1,0:T(8,128)(2,1)S(1)}, bf16[80,512]{1,0:T(8,128)(2,1)S(1)}, u32[]{:S(2)}, u32[]{:S(2)}) %collective-permute-start.31) | collective-permute-done | bytes 81952 | tf_op jit(solution)/shard_map/ppermute | solution.py:508
  141.3 1.3 collective-permute-done.34.other
  142.6 1.7 %shard_map.106 = (f32[512,512]{1,0:T(8,128)}, f32[128,512]{1,0:T(8,128)}, bf16[1,512,128]{2,1,0:T(8,128)(2,1)}) custom-call(s32[8]{0:T(128)S(1)} %concatenate.3.meta_ref, bf16[320,512]{1,0:T(8,128)(2,1)S(1)} %shard_map.105.mine, bf16[320,512]{1,0:T(8,128)(2,1)S(1)} %collective-permute-done.34.other, bf16[512,128]{1,0:T(8,128)(2,1)S(1)} %collective-permute-done.33._.grad), custom_call_target="tpu_custom_call" | custom-call | bytes 2228256 | tf_op jit(solution)/shard_map/pallas_call | solution.py:73
  (49 shorter events, 8.5 us)
Async XLA Ops:
  0.6 28.4 %copy-start = (bf16[512,512]{1,0:T(8,128)(2,1)S(1)}, bf16[512,512]{1,0:T(8,128)(2,1)}, u32[]{:S(2)}) copy-start(bf16[512,512]{1,0:T(8,128)(2,1)} %w.1) | copy-start | bytes 1572868
  2.4 16.3 %collective-permute-start = (bf16[272,512]{1,0:T(8,128)(2,1)}, bf16[272,512]{1,0:T(8,128)(2,1)S(1)}, u32[]{:S(2)}, u32[]{:S(2)}) collective-permute-start(bf16[272,512]{1,0:T(8,128)(2,1)} %shard_map.94), channel_id=1, source_target_pairs={{0,0},{4,64},{8,32},{12,96},{16,24},{20,88},{24,56},{28,120},{32,1... | collective-permute-start | bytes 835592 | tf_op jit(solution)/shard_map/ppermute | solution.py:399
  18.8 9.2 %collective-permute-start.3 = (bf16[272,512]{1,0:T(8,128)(2,1)S(1)}, bf16[272,512]{1,0:T(8,128)(2,1)S(1)}, u32[]{:S(2)}, u32[]{:S(2)}) collective-permute-start(bf16[272,512]{1,0:T(8,128)(2,1)S(1)} %collective-permute-done.xa_ref.up0), channel_id=1, source_target_pairs={{0,3},{1,2},{2,1},{3,0},{4,7},{5,6},{6,5},{7,4},{8,11},{9,10},{10,... | collective-permute-start | bytes 835592 | tf_op jit(solution)/shard_map/ppermute | solution.py:402
  21.5 6.9 %collective-permute-start.2 = (bf16[272,512]{1,0:T(8,128)(2,1)S(1)}, bf16[272,512]{1,0:T(8,128)(2,1)S(1)}, u32[]{:S(2)}, u32[]{:S(2)}) collective-permute-start(bf16[272,512]{1,0:T(8,128)(2,1)S(1)} %collective-permute-done.xa_ref.up0), channel_id=1, source_target_pairs={{0,2},{1,3},{2,0},{3,1},{4,6},{5,7},{6,4},{7,5},{8,10},{9,11},{10,... | collective-permute-start | bytes 835592 | tf_op jit(solution)/shard_map/ppermute | solution.py:402
  21.8 7.2 %collective-permute-start.1 = (bf16[272,512]{1,0:T(8,128)(2,1)S(1)}, bf16[272,512]{1,0:T(8,128)(2,1)S(1)}, u32[]{:S(2)}, u32[]{:S(2)}) collective-permute-start(bf16[272,512]{1,0:T(8,128)(2,1)S(1)} %collective-permute-done.xa_ref.up0), channel_id=1, source_target_pairs={{0,1},{1,0},{2,3},{3,2},{4,5},{5,4},{6,7},{7,6},{8,9},{9,8},{10,11... | collective-permute-start | bytes 835592 | tf_op jit(solution)/shard_map/ppermute | solution.py:402
  24.7 4.3 %copy-start.2 = (f32[1,128]{1,0:T(1,128)S(1)}, f32[1,128]{1,0:T(1,128)}, u32[]{:S(2)}) copy-start(f32[1,128]{1,0:T(1,128)} %table_ref.1) | copy-start | bytes 1540
  30.3 13.3 %collective-permute-start.7 = (bf16[512,256]{1,0:T(8,128)(2,1)S(1)}, bf16[512,256]{1,0:T(8,128)(2,1)S(1)}, u32[]{:S(2)}, u32[]{:S(2)}) collective-permute-start(bf16[512,256]{1,0:T(8,128)(2,1)S(1)} %get-tuple-element.42.q0), channel_id=1, source_target_pairs={{0,16},{16,0},{1,17},{17,1},{2,18},{18,2},{3,19},{19,3},{4,20},{20... | collective-permute-start | bytes 786440 | tf_op jit(solution)/shard_map/ppermute | solution.py:422
  34.6 10.2 %collective-permute-start.6 = (bf16[528,256]{1,0:T(8,128)(2,1)S(1)}, bf16[528,256]{1,0:T(8,128)(2,1)S(1)}, u32[]{:S(2)}, u32[]{:S(2)}) collective-permute-start(bf16[528,256]{1,0:T(8,128)(2,1)S(1)} %get-tuple-element.41.kv0), channel_id=1, source_target_pairs={{0,128},{8,136},{128,0},{136,8},{1,129},{9,137},{129,1},{137,9},{2... | collective-permute-start | bytes 811016 | tf_op jit(solution)/shard_map/ppermute | solution.py:420
  36.8 17.6 %collective-permute-start.5 = (bf16[528,256]{1,0:T(8,128)(2,1)S(1)}, bf16[528,256]{1,0:T(8,128)(2,1)S(1)}, u32[]{:S(2)}, u32[]{:S(2)}) collective-permute-start(bf16[528,256]{1,0:T(8,128)(2,1)S(1)} %get-tuple-element.41.kv0), channel_id=1, source_target_pairs={{0,136},{8,128},{128,8},{136,0},{1,137},{9,129},{129,9},{137,1},{2... | collective-permute-start | bytes 811016 | tf_op jit(solution)/shard_map/ppermute | solution.py:420
  42.6 12.1 %collective-permute-start.4 = (bf16[528,256]{1,0:T(8,128)(2,1)S(1)}, bf16[528,256]{1,0:T(8,128)(2,1)S(1)}, u32[]{:S(2)}, u32[]{:S(2)}) collective-permute-start(bf16[528,256]{1,0:T(8,128)(2,1)S(1)} %get-tuple-element.41.kv0), channel_id=1, source_target_pairs={{0,8},{8,0},{128,136},{136,128},{1,9},{9,1},{129,137},{137,129},{2... | collective-permute-start | bytes 811016 | tf_op jit(solution)/shard_map/ppermute | solution.py:420
  42.7 2.1 %collective-permute-start.8 = (bf16[512,256]{1,0:T(8,128)(2,1)S(1)}, bf16[512,256]{1,0:T(8,128)(2,1)S(1)}, u32[]{:S(2)}, u32[]{:S(2)}) collective-permute-start(bf16[512,256]{1,0:T(8,128)(2,1)S(1)} %get-tuple-element.42.q0), channel_id=1, source_target_pairs={{0,4},{4,0},{1,5},{5,1},{2,6},{6,2},{3,7},{7,3},{8,12},{12,8},{9,1... | collective-permute-start | bytes 786440 | tf_op jit(solution)/shard_map/ppermute | solution.py:423
  43.7 11.1 %collective-permute-start.9 = (bf16[512,256]{1,0:T(8,128)(2,1)S(1)}, bf16[512,256]{1,0:T(8,128)(2,1)S(1)}, u32[]{:S(2)}, u32[]{:S(2)}) collective-permute-start(bf16[512,256]{1,0:T(8,128)(2,1)S(1)} %collective-permute-done.7.q1), channel_id=1, source_target_pairs={{0,4},{4,0},{1,5},{5,1},{2,6},{6,2},{3,7},{7,3},{8,12},{12,8},{9,1... | collective-permute-start | bytes 786440 | tf_op jit(solution)/shard_map/ppermute | solution.py:423
  58.1 2.5 %collective-permute-start.10 = (bf16[1024,128]{1,0:T(8,128)(2,1)S(1)}, bf16[1024,128]{1,0:T(8,128)(2,1)S(1)}, u32[]{:S(2)}, u32[]{:S(2)}) collective-permute-start(bf16[1024,128]{1,0:T(8,128)(2,1)S(1)} %get-tuple-element.47), channel_id=1, source_target_pairs={{0,4},{4,0},{1,5},{5,1},{2,6},{6,2},{3,7},{7,3},{8,12},{12,8},{9,1... | collective-permute-start | bytes 786440 | tf_op jit(solution)/shard_map/ppermute | solution.py:439
  60.5 4.8 %copy-start.1 = (bf16[128,512]{1,0:T(8,128)(2,1)S(1)}, bf16[128,512]{1,0:T(8,128)(2,1)}, u32[]{:S(2)}) copy-start(bf16[128,512]{1,0:T(8,128)(2,1)} %wout.1) | copy-start | bytes 393220
  60.6 4.8 %collective-permute-start.11 = (bf16[512,128]{1,0:T(8,128)(2,1)S(1)}, bf16[512,128]{1,0:T(8,128)(2,1)S(1)}, u32[]{:S(2)}, u32[]{:S(2)}) collective-permute-start(bf16[512,128]{1,0:T(8,128)(2,1)S(1)} %add_convert_fusion.1), channel_id=1, source_target_pairs={{0,16},{16,0},{1,17},{17,1},{2,18},{18,2},{3,19},{19,3},{4,20},{20... | collective-permute-start | bytes 393224 | tf_op jit(solution)/shard_map/ppermute | solution.py:441
  66.5 3.9 %collective-permute-start.12 = (bf16[512,128]{1,0:T(8,128)(2,1)S(1)}, bf16[512,128]{1,0:T(8,128)(2,1)S(1)}, u32[]{:S(2)}, u32[]{:S(2)}) collective-permute-start(bf16[512,128]{1,0:T(8,128)(2,1)S(1)} %get-tuple-element.50.g0), channel_id=1, source_target_pairs={{0,16},{16,0},{1,17},{17,1},{2,18},{18,2},{3,19},{19,3},{4,20},{20... | collective-permute-start | bytes 393224 | tf_op jit(solution)/shard_map/ppermute | solution.py:450
  67.9 4.8 %collective-permute-start.13 = (bf16[512,128]{1,0:T(8,128)(2,1)S(1)}, bf16[512,128]{1,0:T(8,128)(2,1)S(1)}, u32[]{:S(2)}, u32[]{:S(2)}) collective-permute-start(bf16[512,128]{1,0:T(8,128)(2,1)S(1)} %get-tuple-element.50.g0), channel_id=1, source_target_pairs={{0,4},{4,0},{1,5},{5,1},{2,6},{6,2},{3,7},{7,3},{8,12},{12,8},{9,1... | collective-permute-start | bytes 393224 | tf_op jit(solution)/shard_map/ppermute | solution.py:451
  70.4 3.3 %collective-permute-start.14 = (bf16[512,128]{1,0:T(8,128)(2,1)S(1)}, bf16[512,128]{1,0:T(8,128)(2,1)S(1)}, u32[]{:S(2)}, u32[]{:S(2)}) collective-permute-start(bf16[512,128]{1,0:T(8,128)(2,1)S(1)} %collective-permute-done.12.g1), channel_id=1, source_target_pairs={{0,4},{4,0},{1,5},{5,1},{2,6},{6,2},{3,7},{7,3},{8,12},{12,8},{9,1... | collective-permute-start | bytes 393224 | tf_op jit(solution)/shard_map/ppermute | solution.py:451
  79.3 6.9 %collective-permute-start.18 = (bf16[1024,128]{1,0:T(8,128)(2,1)S(1)}, bf16[1024,128]{1,0:T(8,128)(2,1)S(1)}, u32[]{:S(2)}, u32[]{:S(2)}) collective-permute-start(bf16[1024,128]{1,0:T(8,128)(2,1)S(1)} %get-tuple-element.56), channel_id=1, source_target_pairs={{0,4},{4,0},{1,5},{5,1},{2,6},{6,2},{3,7},{7,3},{8,12},{12,8},{9,1... | collective-permute-start | bytes 786440 | tf_op jit(solution)/shard_map/ppermute | solution.py:471
  79.7 11.1 %collective-permute-start.15 = (bf16[512,256]{1,0:T(8,128)(2,1)S(1)}, bf16[512,256]{1,0:T(8,128)(2,1)S(1)}, u32[]{:S(2)}, u32[]{:S(2)}) collective-permute-start(bf16[512,256]{1,0:T(8,128)(2,1)S(1)} %get-tuple-element.52), channel_id=1, source_target_pairs={{0,128},{8,136},{128,0},{136,8},{1,129},{9,137},{129,1},{137,9},{2... | collective-permute-start | bytes 786440 | tf_op jit(solution)/shard_map/ppermute | solution.py:470
  84.3 13.8 %collective-permute-start.16 = (bf16[512,256]{1,0:T(8,128)(2,1)S(1)}, bf16[512,256]{1,0:T(8,128)(2,1)S(1)}, u32[]{:S(2)}, u32[]{:S(2)}) collective-permute-start(bf16[512,256]{1,0:T(8,128)(2,1)S(1)} %get-tuple-element.53), channel_id=1, source_target_pairs={{0,8},{8,0},{128,136},{136,128},{1,9},{9,1},{129,137},{137,129},{2... | collective-permute-start | bytes 786440 | tf_op jit(solution)/shard_map/ppermute | solution.py:468
  86.2 12.0 %collective-permute-start.17 = (bf16[512,256]{1,0:T(8,128)(2,1)S(1)}, bf16[512,256]{1,0:T(8,128)(2,1)S(1)}, u32[]{:S(2)}, u32[]{:S(2)}) collective-permute-start(bf16[512,256]{1,0:T(8,128)(2,1)S(1)} %get-tuple-element.54), channel_id=1, source_target_pairs={{0,136},{8,128},{128,8},{136,0},{1,137},{9,129},{129,9},{137,1},{2... | collective-permute-start | bytes 786440 | tf_op jit(solution)/shard_map/ppermute | solution.py:469
  86.2 11.9 %collective-permute-start.19 = (bf16[512,128]{1,0:T(8,128)(2,1)S(1)}, bf16[512,128]{1,0:T(8,128)(2,1)S(1)}, u32[]{:S(2)}, u32[]{:S(2)}) collective-permute-start(bf16[512,128]{1,0:T(8,128)(2,1)S(1)} %add_convert_fusion), channel_id=1, source_target_pairs={{0,16},{16,0},{1,17},{17,1},{2,18},{18,2},{3,19},{19,3},{4,20},{20... | collective-permute-start | bytes 393224 | tf_op jit(solution)/shard_map/ppermute | solution.py:473
  99.8 2.3 %collective-permute-start.20 = (bf16[320,512]{1,0:T(8,128)(2,1)S(1)}, bf16[320,512]{1,0:T(8,128)(2,1)S(1)}, u32[]{:S(2)}, u32[]{:S(2)}) collective-permute-start(bf16[320,512]{1,0:T(8,128)(2,1)S(1)} %get-tuple-element.61), channel_id=1, source_target_pairs={{0,4},{4,0},{1,5},{5,1},{2,6},{6,2},{3,7},{7,3},{8,12},{12,8},{9,1... | collective-permute-start | bytes 983048 | tf_op jit(solution)/shard_map/ppermute | solution.py:483
  102.8 5.2 %collective-permute-start.21 = (bf16[80,512]{1,0:T(8,128)(2,1)S(1)}, bf16[80,512]{1,0:T(8,128)(2,1)S(1)}, u32[]{:S(2)}, u32[]{:S(2)}) collective-permute-start(bf16[80,512]{1,0:T(8,128)(2,1)S(1)} %get-tuple-element.63), channel_id=1, source_target_pairs={{0,128},{8,136},{128,0},{136,8},{1,129},{9,137},{129,1},{137,9},{2... | collective-permute-start | bytes 245768 | tf_op jit(solution)/shard_map/ppermute | solution.py:491
  103.9 5.8 %collective-permute-start.22 = (bf16[80,512]{1,0:T(8,128)(2,1)S(1)}, bf16[80,512]{1,0:T(8,128)(2,1)S(1)}, u32[]{:S(2)}, u32[]{:S(2)}) collective-permute-start(bf16[80,512]{1,0:T(8,128)(2,1)S(1)} %get-tuple-element.64), channel_id=1, source_target_pairs={{0,8},{8,0},{128,136},{136,128},{1,9},{9,1},{129,137},{137,129},{2... | collective-permute-start | bytes 245768 | tf_op jit(solution)/shard_map/ppermute | solution.py:491
  105.8 4.5 %collective-permute-start.23 = (bf16[80,512]{1,0:T(8,128)(2,1)S(1)}, bf16[80,512]{1,0:T(8,128)(2,1)S(1)}, u32[]{:S(2)}, u32[]{:S(2)}) collective-permute-start(bf16[80,512]{1,0:T(8,128)(2,1)S(1)} %get-tuple-element.65), channel_id=1, source_target_pairs={{0,136},{8,128},{128,8},{136,0},{1,137},{9,129},{129,9},{137,1},{2... | collective-permute-start | bytes 245768 | tf_op jit(solution)/shard_map/ppermute | solution.py:491
  110.3 4.3 %collective-permute-start.24 = (bf16[80,512]{1,0:T(8,128)(2,1)S(1)}, bf16[80,512]{1,0:T(8,128)(2,1)S(1)}, u32[]{:S(2)}, u32[]{:S(2)}) collective-permute-start(bf16[80,512]{1,0:T(8,128)(2,1)S(1)} %get-tuple-element.69), channel_id=1, source_target_pairs={{0,32},{32,0},{1,33},{33,1},{2,34},{34,2},{3,35},{35,3},{4,36},{36... | collective-permute-start | bytes 245768 | tf_op jit(solution)/shard_map/ppermute | solution.py:497
  110.4 4.3 %collective-permute-start.26 = (bf16[512,128]{1,0:T(8,128)(2,1)S(1)}, bf16[512,128]{1,0:T(8,128)(2,1)S(1)}, u32[]{:S(2)}, u32[]{:S(2)}) collective-permute-start(bf16[512,128]{1,0:T(8,128)(2,1)S(1)} %get-tuple-element.71), channel_id=1, source_target_pairs={{0,1},{1,0},{2,3},{3,2},{4,5},{5,4},{6,7},{7,6},{8,9},{9,8},{10,11... | collective-permute-start | bytes 393224 | tf_op jit(solution)/shard_map/ppermute | solution.py:496
  111.9 6.6 %collective-permute-start.27 = (bf16[512,128]{1,0:T(8,128)(2,1)S(1)}, bf16[512,128]{1,0:T(8,128)(2,1)S(1)}, u32[]{:S(2)}, u32[]{:S(2)}) collective-permute-start(bf16[512,128]{1,0:T(8,128)(2,1)S(1)} %get-tuple-element.72), channel_id=1, source_target_pairs={{0,2},{1,3},{2,0},{3,1},{4,6},{5,7},{6,4},{7,5},{8,10},{9,11},{10,... | collective-permute-start | bytes 393224 | tf_op jit(solution)/shard_map/ppermute | solution.py:496
  114.5 5.5 %collective-permute-start.28 = (bf16[512,128]{1,0:T(8,128)(2,1)S(1)}, bf16[512,128]{1,0:T(8,128)(2,1)S(1)}, u32[]{:S(2)}, u32[]{:S(2)}) collective-permute-start(bf16[512,128]{1,0:T(8,128)(2,1)S(1)} %get-tuple-element.73), channel_id=1, source_target_pairs={{0,3},{1,2},{2,1},{3,0},{4,7},{5,6},{6,5},{7,4},{8,11},{9,10},{10,... | collective-permute-start | bytes 393224 | tf_op jit(solution)/shard_map/ppermute | solution.py:496
  114.6 8.2 %collective-permute-start.25 = (bf16[80,512]{1,0:T(8,128)(2,1)S(1)}, bf16[80,512]{1,0:T(8,128)(2,1)S(1)}, u32[]{:S(2)}, u32[]{:S(2)}) collective-permute-start(bf16[80,512]{1,0:T(8,128)(2,1)S(1)} %add_convert_fusion.3.a), channel_id=1, source_target_pairs={{0,64},{64,0},{1,65},{65,1},{2,66},{66,2},{3,67},{67,3},{4,68},{68... | collective-permute-start | bytes 245768 | tf_op jit(solution)/shard_map/ppermute | solution.py:499
  122.9 6.7 %collective-permute-start.29 = (bf16[80,512]{1,0:T(8,128)(2,1)S(1)}, bf16[80,512]{1,0:T(8,128)(2,1)S(1)}, u32[]{:S(2)}, u32[]{:S(2)}) collective-permute-start(bf16[80,512]{1,0:T(8,128)(2,1)S(1)} %get-tuple-element.74), channel_id=1, source_target_pairs={{0,16},{16,0},{1,17},{17,1},{2,18},{18,2},{3,19},{19,3},{4,20},{20... | collective-permute-start | bytes 245768 | tf_op jit(solution)/shard_map/ppermute | solution.py:506
  123.5 12.5 %collective-permute-start.33 = (bf16[512,128]{1,0:T(8,128)(2,1)S(1)}, bf16[512,128]{1,0:T(8,128)(2,1)S(1)}, u32[]{:S(2)}, u32[]{:S(2)}) collective-permute-start(bf16[512,128]{1,0:T(8,128)(2,1)S(1)} %get-tuple-element.75), channel_id=1, source_target_pairs={{0,0},{64,4},{32,8},{96,12},{24,16},{88,20},{56,24},{120,28},{12,3... | collective-permute-start | bytes 393224 | tf_op jit(solution)/shard_map/ppermute | solution.py:505
  129.7 6.3 %collective-permute-start.32 = (bf16[80,512]{1,0:T(8,128)(2,1)S(1)}, bf16[80,512]{1,0:T(8,128)(2,1)S(1)}, u32[]{:S(2)}, u32[]{:S(2)}) collective-permute-start(bf16[80,512]{1,0:T(8,128)(2,1)S(1)} %add_convert_fusion.2.p0), channel_id=1, source_target_pairs={{0,128},{8,136},{128,0},{136,8},{1,129},{9,137},{129,1},{137,9},{2... | collective-permute-start | bytes 245768 | tf_op jit(solution)/shard_map/ppermute | solution.py:508
  130.9 8.9 %collective-permute-start.31 = (bf16[80,512]{1,0:T(8,128)(2,1)S(1)}, bf16[80,512]{1,0:T(8,128)(2,1)S(1)}, u32[]{:S(2)}, u32[]{:S(2)}) collective-permute-start(bf16[80,512]{1,0:T(8,128)(2,1)S(1)} %add_convert_fusion.2.p0), channel_id=1, source_target_pairs={{0,136},{8,128},{128,8},{136,0},{1,137},{9,129},{129,9},{137,1},{2... | collective-permute-start | bytes 245768 | tf_op jit(solution)/shard_map/ppermute | solution.py:508
  136.0 4.3 %collective-permute-start.30 = (bf16[80,512]{1,0:T(8,128)(2,1)S(1)}, bf16[80,512]{1,0:T(8,128)(2,1)S(1)}, u32[]{:S(2)}, u32[]{:S(2)}) collective-permute-start(bf16[80,512]{1,0:T(8,128)(2,1)S(1)} %add_convert_fusion.2.p0), channel_id=1, source_target_pairs={{0,8},{8,0},{128,136},{136,128},{1,9},{9,1},{129,137},{137,129},{2... | collective-permute-start | bytes 245768 | tf_op jit(solution)/shard_map/ppermute | solution.py:508
  140.8 1.7 %collective-permute-start.34 = (bf16[320,512]{1,0:T(8,128)(2,1)S(1)}, bf16[320,512]{1,0:T(8,128)(2,1)S(1)}, u32[]{:S(2)}, u32[]{:S(2)}) collective-permute-start(bf16[320,512]{1,0:T(8,128)(2,1)S(1)} %shard_map.105.mine), channel_id=1, source_target_pairs={{0,4},{4,0},{1,5},{5,1},{2,6},{6,2},{3,7},{7,3},{8,12},{12,8},{9,1... | collective-permute-start | bytes 983048 | tf_op jit(solution)/shard_map/ppermute | solution.py:510
